TPU v7x, 32 devices: a whole 2x2x4 slice. The times are simulated.
32 devices in a mesh: tensor: 4 (over y, x), seq: 4 (over z), dp: 2 (over core).
Axes of the slice: x: 2, y: 2, z: 4, core: 2. Of those that a mesh axis runs over, the one named last changes fastest.
Arguments:
- residual_in: bfloat16 [8, 2048, 1536], P('dp', 'seq'), may hold values from -6 to 6
- lengths: int32 [8], P('dp'), may hold values from 512 to 2048, as said below
- input_gain: float32 [1536], replicated, may hold values from 0.5 to 1.5
- main_in_weight: bfloat16 [1536, 2, 3072], P(None, None, 'tensor'), may hold values from -0.15625 to 0.15625
- weight_shared: bfloat16 [1536, 256], replicated, may hold values from -0.15625 to 0.15625
- step_in_weight: bfloat16 [1536, 48], P(None, 'tensor'), may hold values from -0.0390625 to 0.0390625
- filter_main: float32 [5, 3072], P(None, 'tensor'), may hold values from -3 to 3
- filter_shared: float32 [5, 256], replicated, may hold values from -3 to 3
- head_terms: float32 [3, 48], P(None, 'tensor'), may hold values from -12 to 2
- output_gain: float32 [3072], P('tensor'), may hold values from 0.5 to 1.5
- out_projection_weight: bfloat16 [3072, 1536], P('tensor'), may hold values from -0.109375 to 0.109375
- cotangent: bfloat16 [8, 2048, 1536], P('dp', 'seq'), may hold values from -6 to 6
Outputs:
- block_out: bfloat16 [8, 2048, 1536], P('dp', 'seq')
- input_grad: bfloat16 [8, 2048, 1536], P('dp', 'seq')
- grad_input_gain: float32 [1536], replicated
- grad_weight_main: float32 [1536, 2, 3072], P(('seq', 'dp'), None, 'tensor')
- grad_weight_shared: float32 [1536, 256], P(('seq', 'dp'))
- grad_weight_step: float32 [1536, 48], P(('seq', 'dp'), 'tensor')
- grad_filter_main: float32 [5, 3072], P(None, 'tensor')
- grad_filter_shared: float32 [5, 256], replicated
- grad_head_terms: float32 [3, 48], P(None, 'tensor')
- grad_output_gain: float32 [3072], P('tensor')
- grad_weight_out: float32 [3072, 1536], P('tensor', ('seq', 'dp'))
Inputs may be any that keep to these rules, and one draw needn't show every extreme that they name: `lengths`: in each aligned group of 4 sequences (those of one index of dp) one sequence has length 2048.
All inputs are finite; a program needn't handle non-finite values.
Results may differ from a plain program's by a relative error of at most 0.0088.
Values may be sent and summed in bfloat16 or wider, within the bound.
No kernel may reach another device: no remote copies, remote signals or barrier semaphores. Data moves between devices by JAX's collectives and lax.ppermute only.
A program may use at most 256 MiB of HBM per device.

v0:
```python
import jax
import jax.numpy as jnp
from jax import lax
from jax.sharding import PartitionSpec as P

HEADDIM = 64
CONV = 4
BLOCK_LEN = 256


EPSILON = 1e-05
PRECISE_MODE = lax.Precision.HIGHEST


def shifted(block, axis, distance):
    devices = range(lax.axis_size(axis))
    route = [(i - distance, i) for i in devices if i - distance in devices]
    return lax.ppermute(block, axis, route)


def block_step(carry_state, pieces):
    values, step_size, log_decay, inject, readout = pieces
    running = jnp.cumsum(log_decay, axis=1)
    extent = log_decay.shape[1]
    lower = (jnp.arange(extent)[:, None] >= jnp.arange(extent)[None, :])[None, :, :, None]
    spread = running[:, :, None, :] - running[:, None, :, :]
    decay = jnp.where(lower, jnp.exp(jnp.where(lower, spread, 0.0)), 0.0)
    intersection = jnp.einsum("sqn,skn->sqk", readout, inject, precision=PRECISE_MODE)
    mixing = decay * intersection[:, :, :, None] * step_size[:, None, :, :]
    outputs = jnp.einsum("sqkh,skhp->sqhp", mixing, values, precision=PRECISE_MODE)
    carried = jnp.einsum("sqn,shpn->sqhp", readout, carry_state, precision=PRECISE_MODE)
    outputs = outputs + carried * jnp.exp(running)[:, :, :, None]
    toward_end = jnp.exp(running[:, -1:, :] - running) * step_size
    gained = jnp.einsum("skh,skhp,skn->shpn", toward_end, values, inject, precision=PRECISE_MODE)
    carry_state = carry_state * jnp.exp(running[:, -1, :])[:, :, None, None] + gained
    return (carry_state, outputs)


def span_pass(values, step_size, log_decay, inject, readout, start):
    batch_seqs = step_size.shape[0]
    length = step_size.shape[1]
    block = min(BLOCK_LEN, length)
    count = length // block

    def split(array):
        shaped = array.reshape((batch_seqs, count, block) + array.shape[2:])
        return jnp.moveaxis(shaped, 1, 0)

    final, outputs = lax.scan(
        jax.checkpoint(block_step),
        start,
        (split(values), split(step_size), split(log_decay), split(inject), split(readout)),
    )
    outputs = jnp.moveaxis(outputs, 0, 1).reshape(values.shape)
    return (outputs, final)


def silu_slope(value):
    sigma = jax.nn.sigmoid(value)
    return sigma * (1.0 + value * (1.0 - sigma))


def times_transposed(left, right):
    return lax.dot_general(
        left, right, (((1,), (1,)), ((), ())), preferred_element_type=jnp.float32
    )


def rows_product(left, right):
    return lax.dot_general(
        left, right, (((0,), (0,)), ((), ())), preferred_element_type=jnp.float32
    )


def norm_back(grad_lowered, normed_in, scale_in, grad_top, input_gain):
    grad_normed = grad_lowered * input_gain
    grad_in = grad_top.astype(jnp.float32) + scale_in * (
        grad_normed - normed_in * jnp.mean(grad_normed * normed_in, axis=1, keepdims=True)
    )
    return (grad_in.astype(jnp.bfloat16), jnp.sum(grad_lowered * normed_in, axis=0))


def per_device(
    residual_in,
    lengths,
    input_gain,
    main_in_weight,
    weight_shared,
    step_in_weight,
    filter_main,
    filter_shared,
    head_terms,
    output_gain,
    out_projection_weight,
    cotangent,
):
    batch_seqs, span_rows, model_width = residual_in.shape
    head_count = step_in_weight.shape[1]
    inner_local = main_in_weight.shape[2]
    state_width = weight_shared.shape[1] // 2
    row_count = batch_seqs * span_rows
    inner_total = inner_local * lax.axis_size("tensor")
    reach = CONV - 1
    flat_in = residual_in.reshape(row_count, model_width).astype(jnp.float32)
    scale_in = lax.rsqrt(jnp.mean(flat_in * flat_in, axis=1, keepdims=True) + EPSILON)
    normed_in = flat_in * scale_in
    reduced_output = (normed_in * input_gain).astype(jnp.bfloat16)
    gate_before_act = jnp.dot(
        reduced_output, main_in_weight[:, 0, :], preferred_element_type=jnp.float32
    )
    main_in = jnp.dot(reduced_output, main_in_weight[:, 1, :], preferred_element_type=jnp.float32)
    shared_in = jnp.dot(reduced_output, weight_shared, preferred_element_type=jnp.float32)
    step_before_act = jnp.dot(reduced_output, step_in_weight, preferred_element_type=jnp.float32)
    mixer_input = (
        jnp.concatenate([main_in, shared_in], axis=1)
        .astype(jnp.bfloat16)
        .reshape(batch_seqs, span_rows, -1)
    )
    before = shifted(mixer_input[:, span_rows - reach :, :], "seq", 1)
    extended = jnp.concatenate([before, mixer_input], axis=1).astype(jnp.float32)
    taps = jnp.concatenate([filter_main, filter_shared], axis=1)
    conv_pre = taps[CONV]
    for offset in range(CONV):
        conv_pre = conv_pre + taps[offset] * extended[:, offset : offset + span_rows, :]
    active = jax.nn.silu(conv_pre)
    values = active[:, :, :inner_local].reshape(batch_seqs, span_rows, head_count, HEADDIM)
    inject = active[:, :, inner_local : inner_local + state_width]
    readout = active[:, :, inner_local + state_width :]
    step_arg = step_before_act.reshape(batch_seqs, span_rows, head_count) + head_terms[0]
    step_size = jax.nn.softplus(step_arg)
    rate = -jnp.exp(head_terms[1])
    log_decay = step_size * rate
    empty_state = jnp.zeros((batch_seqs, head_count, HEADDIM, state_width), jnp.float32)
    local_out, local_state = span_pass(values, step_size, log_decay, inject, readout, empty_state)
    through = jnp.exp(jnp.sum(log_decay, axis=1))

    def advance(turn, carried):
        return shifted(carried * through[:, :, None, None] + local_state, "seq", 1)

    entering = lax.fori_loop(0, lax.axis_size("seq") - 1, advance, empty_state)
    span_decay = jnp.exp(jnp.cumsum(log_decay, axis=1))
    carried_in = (
        jnp.einsum("sln,shpn->slhp", readout, entering, precision=PRECISE_MODE)
        * span_decay[:, :, :, None]
    )
    skip = head_terms[2][:, None]
    scanned = local_out + carried_in + skip * values
    gate_act = jax.nn.silu(gate_before_act)
    scanned_flat = scanned.reshape(row_count, inner_local)
    gated = scanned_flat * gate_act
    squares = lax.psum(jnp.sum(gated * gated, axis=1), "tensor")
    scale_out = lax.rsqrt(squares / inner_total + EPSILON)[:, None]
    normalized_output = (gated * scale_out * output_gain).astype(jnp.bfloat16)
    out_terms = jnp.dot(
        normalized_output, out_projection_weight, preferred_element_type=jnp.float32
    )
    mixer = lax.psum(out_terms, "tensor")
    block_out = (flat_in + mixer).astype(jnp.bfloat16).reshape(residual_in.shape)
    places = lax.axis_index("seq") * span_rows + jnp.arange(span_rows, dtype=jnp.int32)
    live = places[None, :] < lengths[:, None]
    grad_top = jnp.where(live[:, :, None], cotangent, jnp.zeros_like(cotangent)).reshape(
        row_count, model_width
    )
    grad_weight_out = rows_product(normalized_output, grad_top)
    grad_normed_out = times_transposed(grad_top, out_projection_weight)
    grad_output_gain = jnp.sum(grad_normed_out * gated * scale_out, axis=0)
    scaled_back = grad_normed_out * output_gain
    projected = lax.psum(jnp.sum(scaled_back * gated, axis=1), "tensor")
    grad_gated = scale_out * scaled_back - gated * scale_out**3 * (projected / inner_total)[:, None]
    grad_scanned = (grad_gated * gate_act).reshape(batch_seqs, span_rows, head_count, HEADDIM)
    grad_gate_low = (grad_gated * scanned_flat * silu_slope(gate_before_act)).astype(jnp.bfloat16)
    arriving = jnp.einsum(
        "slhp,sln->shpn", grad_scanned * span_decay[:, :, :, None], readout, precision=PRECISE_MODE
    )

    def retreat(turn, carried):
        return shifted(carried * through[:, :, None, None] + arriving, "seq", -1)

    leaving = lax.fori_loop(0, lax.axis_size("seq") - 1, retreat, empty_state)
    primal_out, pullback = jax.vjp(
        span_pass, values, step_size, log_decay, inject, readout, entering
    )
    grad_values, grad_step, grad_decay, grad_inject, grad_readout, grad_entering = pullback(
        (grad_scanned, leaving)
    )
    grad_values = grad_values + skip * grad_scanned
    grad_skip = jnp.sum(grad_scanned * values, axis=(0, 1, 3))
    grad_decay_rate = jnp.sum(grad_decay * log_decay, axis=(0, 1))
    grad_step_arg = (grad_step + grad_decay * rate) * jax.nn.sigmoid(step_arg)
    grad_step_bias = jnp.sum(grad_step_arg, axis=(0, 1))
    grad_head_terms = jnp.stack([grad_step_bias, grad_decay_rate, grad_skip])
    grad_step_low = grad_step_arg.reshape(row_count, head_count).astype(jnp.bfloat16)
    grad_shared_act = lax.psum(jnp.concatenate([grad_inject, grad_readout], axis=2), "tensor")
    grad_active = jnp.concatenate(
        [grad_values.reshape(batch_seqs, span_rows, inner_local), grad_shared_act], axis=2
    )
    grad_conv_pre = grad_active * silu_slope(conv_pre)
    filter_rows = [
        jnp.sum(extended[:, offset : offset + span_rows, :] * grad_conv_pre, axis=(0, 1))
        for offset in range(CONV)
    ]
    filter_rows.append(jnp.sum(grad_conv_pre, axis=(0, 1)))
    grad_filter = jnp.stack(filter_rows)
    grad_extended = jnp.zeros((batch_seqs, span_rows + reach, grad_conv_pre.shape[2]), jnp.float32)
    for offset in range(CONV):
        grad_extended = grad_extended + jnp.pad(
            taps[offset] * grad_conv_pre, ((0, 0), (offset, reach - offset), (0, 0))
        )
    from_next = shifted(grad_extended[:, :reach, :].astype(jnp.bfloat16), "seq", -1).astype(
        jnp.float32
    )
    grad_mixed = grad_extended[:, reach:, :] + jnp.pad(
        from_next, ((0, 0), (span_rows - reach, 0), (0, 0))
    )
    grad_mixed_low = grad_mixed.reshape(row_count, -1).astype(jnp.bfloat16)
    grad_main_low = grad_mixed_low[:, :inner_local]
    grad_shared_low = grad_mixed_low[:, inner_local:]
    grad_partial = (
        times_transposed(grad_gate_low, main_in_weight[:, 0, :])
        + times_transposed(grad_main_low, main_in_weight[:, 1, :])
        + times_transposed(grad_step_low, step_in_weight)
    )
    grad_lowered = lax.psum(grad_partial, "tensor") + times_transposed(
        grad_shared_low, weight_shared
    )
    input_low, grad_input_gain = norm_back(grad_lowered, normed_in, scale_in, grad_top, input_gain)
    input_grad = input_low.reshape(residual_in.shape)
    grad_main = jnp.stack(
        [rows_product(reduced_output, grad_gate_low), rows_product(reduced_output, grad_main_low)],
        axis=1,
    )
    grad_shared = rows_product(reduced_output, grad_shared_low)
    grad_step_weight = rows_product(reduced_output, grad_step_low)
    summed_main, summed_shared, summed_step, summed_out = (
        lax.psum_scatter(grad_main, ("seq", "dp"), scatter_dimension=0, tiled=True),
        lax.psum_scatter(grad_shared, ("seq", "dp"), scatter_dimension=0, tiled=True),
        lax.psum_scatter(grad_step_weight, ("seq", "dp"), scatter_dimension=0, tiled=True),
        lax.psum_scatter(grad_weight_out, ("seq", "dp"), scatter_dimension=1, tiled=True),
    )
    small_input, small_output, small_filter_main, small_filter_shared, small_heads = lax.psum(
        (
            grad_input_gain,
            grad_output_gain,
            grad_filter[:, :inner_local],
            grad_filter[:, inner_local:],
            grad_head_terms,
        ),
        ("seq", "dp"),
    )
    return (
        block_out,
        input_grad,
        small_input,
        summed_main,
        summed_shared,
        summed_step,
        small_filter_main,
        small_filter_shared,
        small_heads,
        small_output,
        summed_out,
    )


def solution(mesh):
    placed = (
        P("dp", "seq", None),
        P("dp"),
        P(),
        P(None, None, "tensor"),
        P(),
        P(None, "tensor"),
        P(None, "tensor"),
        P(),
        P(None, "tensor"),
        P("tensor"),
        P("tensor", None),
        P("dp", "seq", None),
    )
    return jax.shard_map(
        per_device,
        mesh=mesh,
        in_specs=placed,
        out_specs=(
            P("dp", "seq", None),
            P("dp", "seq", None),
            P(),
            P(("seq", "dp"), None, "tensor"),
            P(("seq", "dp"), None),
            P(("seq", "dp"), "tensor"),
            P(None, "tensor"),
            P(),
            P(None, "tensor"),
            P("tensor"),
            P("tensor", ("seq", "dp")),
        ),
        check_vma=False,
    )
```

profile of v0, /device:TPU:0, one launch (start us, length us, event | category | flops | bytes accessed | tf_op | source)
XLA Modules:
  0.0 1727.7 jit_solution(8777719476974737591)
XLA Ops:
  86.9 19.0 %fusion.115 = (f32[4,512,1024]{2,1,0:T(8,128)}, f32[4,512,1024]{2,1,0:T(8,128)}) fusion(f32[4,515,1024]{2,1,0:T(8,128)} %maximum_convert_fusion, f32[1024]{0:T(1024)S(1)} %bitcast.568, f32[1024]{0:T(1024)S(1)} %bitcast.570, f32[1024]{0:T(1024)S(1)} %bitcast.572, f32[1024]{0:T(1024)S(1)} %bitcast.574, f32[1024]{0:T(1024)S(1)} %bitcast.576), kind=kLoop, calls=%fused_computation.172 | loop fusion | flops 25165824 | bytes 50352128 | tf_op jit(solution)/shard_map/jit(silu)/mul | solution.py:125
  140.9 73.4 %while.73 = (s32[]{:T(128)}, f32[4,12,64,128]{3,2,1,0:T(8,128)}, f32[2,4,256,12,64]{2,4,3,1,0:T(8,128)}, f32[2,4,256,12]{2,1,3,0:T(4,128)}, f32[2,4,256,12]{2,1,...) while((s32[]{:T(128)}, f32[4,12,64,128]{3,2,1,0:T(8,128)}, ...), condition=%wide.region_4.5_spmd.clone, body=%wide.region_1.4_spmd.clone.sunk | while | flops 5255815168 | bytes 26404676 | solution.py:49
  147.5 17.1 fusion.279
  183.4 17.1 fusion.279
  215.7 119.9 %while.69 = (s32[]{:T(128)}, f32[4,12,64,128]{3,2,1,0:T(8,128)}, f32[4,12]{1,0:T(4,128)S(1)}, f32[4,12,64,128]{3,2,1,0:T(8,128)}, s32[]{:T(128)}) while((s32[]{:T(128)}, f32[4,12,64,128]{3,2,1,0:T(8,128)}, f32[4,12]{1,0:T(4,128)S(1)}, f32[4,12,64,128]{3,2,1,0:T(8,128)}, s32[]{:T(128)}) %tuple.189), condition=%wide.region_7.8_spmd, body=%wide.region_6.7_spmd.sunk | while | flops 786434 | bytes 11010341 | solution.py:140
  223.1 32.5 %collective-permute-done = f32[4,12,64,128]{3,2,1,0:T(8,128)} collective-permute-done((f32[4,12,64,128]{3,2,1,0:T(8,128)}, f32[4,12,64,128]{3,2,1,0:T(8,128)}, u32[]{:S(2)}, u32[]{:S(2)}) %collective-permute-start) | collective-permute-done | bytes 1572896 | tf_op jit(solution)/shard_map/while/body/eval_jaxpr/ppermute | solution.py:18
  264.5 31.6 %collective-permute-done = f32[4,12,64,128]{3,2,1,0:T(8,128)} collective-permute-done((f32[4,12,64,128]{3,2,1,0:T(8,128)}, f32[4,12,64,128]{3,2,1,0:T(8,128)}, u32[]{:S(2)}, u32[]{:S(2)}) %collective-permute-start) | collective-permute-done | bytes 1572896 | tf_op jit(solution)/shard_map/while/body/eval_jaxpr/ppermute | solution.py:18
  305.0 30.7 %collective-permute-done = f32[4,12,64,128]{3,2,1,0:T(8,128)} collective-permute-done((f32[4,12,64,128]{3,2,1,0:T(8,128)}, f32[4,12,64,128]{3,2,1,0:T(8,128)}, u32[]{:S(2)}, u32[]{:S(2)}) %collective-permute-start) | collective-permute-done | bytes 1572896 | tf_op jit(solution)/shard_map/while/body/eval_jaxpr/ppermute | solution.py:18
  366.3 12.9 multiply_reduce_fusion.10
  389.3 11.8 multiply_reduce_fusion.8
  409.2 16.6 fusion.116
  449.9 26.6 %while.71 = (s32[]{:T(128)}, f32[4,12,64,128]{3,2,1,0:T(8,128)}, f32[2,4,12,64,128]{4,3,2,1,0:T(8,128)}, f32[2,4,256,12]{2,1,3,0:T(4,128)}, f32[2,4,256,12]{2,1,...) while((s32[]{:T(128)}, f32[4,12,64,128]{3,2,1,0:T(8,128)}, ...), condition=%wide.region_20.21_spmd, body=%wide.region_17.20_spmd.sunk | while | flops 1211129984 | bytes 10952489 | solution.py:49
  489.1 102.9 %while.70 = (s32[]{:T(128)}, f32[4,12,64,128]{3,2,1,0:T(8,128)}, f32[4,12]{1,0:T(4,128)S(1)}, f32[4,12,64,128]{3,2,1,0:T(8,128)}, s32[]{:T(128)}) while((s32[]{:T(128)}, f32[4,12,64,128]{3,2,1,0:T(8,128)}, f32[4,12]{1,0:T(4,128)S(1)}, f32[4,12,64,128]{3,2,1,0:T(8,128)}, s32[]{:T(128)}) %tuple.218), condition=%wide.region_16.17_spmd, body=%wide.region_15.16_spmd.sunk | while | flops 786434 | bytes 11010341 | solution.py:179
  493.7 30.7 %collective-permute-done.1 = f32[4,12,64,128]{3,2,1,0:T(8,128)} collective-permute-done((f32[4,12,64,128]{3,2,1,0:T(8,128)}, f32[4,12,64,128]{3,2,1,0:T(8,128)}, u32[]{:S(2)}, u32[]{:S(2)}) %collective-permute-start.1) | collective-permute-done | bytes 1572896 | tf_op jit(solution)/shard_map/while/body/eval_jaxpr/ppermute | solution.py:18
  528.9 30.0 %collective-permute-done.1 = f32[4,12,64,128]{3,2,1,0:T(8,128)} collective-permute-done((f32[4,12,64,128]{3,2,1,0:T(8,128)}, f32[4,12,64,128]{3,2,1,0:T(8,128)}, u32[]{:S(2)}, u32[]{:S(2)}) %collective-permute-start.1) | collective-permute-done | bytes 1572896 | tf_op jit(solution)/shard_map/while/body/eval_jaxpr/ppermute | solution.py:18
  563.5 28.5 %collective-permute-done.1 = f32[4,12,64,128]{3,2,1,0:T(8,128)} collective-permute-done((f32[4,12,64,128]{3,2,1,0:T(8,128)}, f32[4,12,64,128]{3,2,1,0:T(8,128)}, u32[]{:S(2)}, u32[]{:S(2)}) %collective-permute-start.1) | collective-permute-done | bytes 1572896 | tf_op jit(solution)/shard_map/while/body/eval_jaxpr/ppermute | solution.py:18
  599.4 278.1 %while.72 = (s32[]{:T(128)}, f32[4,12,64,128]{3,2,1,0:T(8,128)}, f32[2,4,256,12,64]{2,4,3,1,0:T(8,128)}, f32[2,4,256,12]{3,1,2,0:T(4,128)}, f32[2,4,256,12]{2,1,...) while((s32[]{:T(128)}, f32[4,12,64,128]{3,2,1,0:T(8,128)}, ...), condition=%wide.region_33.34_spmd, body=%wide.region_21.33_spmd.sunk | while | flops 12154507264 | bytes 143420160 | solution.py:49
  627.8 23.2 %fusion.261 = (f32[4,256,12]{1,2,0:T(8,128)}, f32[4,256,12]{1,2,0:T(8,128)}, f32[4,256,12]{1,2,0:T(8,128)}, f32[4,256,256]{2,1,0:T(8,128)}) fusion(f32[4,256,12]{1,2,0:T(8,128)S(1)} %copy.587, f32[4,256,256]{2,1,0:T(8,128)} %fusion.259, f32[4,256,12]{1,2,0:T(8,128)S(1)} %copy.592, pred[256,256]{1,0:T(8,128)(4,1)S(1)} %iota_compare_fusion.4, ...), kind=kOutput, calls=%fused_computation.76.clone.1 | convolution fusion | flops 2462806016 | bytes 8699904 | tf_op jit(solution)/shard_map/transpose(jvp())/while/body/eval_jaxpr/checkpoint/sqkh,skhp->sqhp/dot_general | solution.py:30
  714.0 14.7 bitcast_dynamic-update-slice_fusion.11
  763.7 23.0 %fusion.261 = (f32[4,256,12]{1,2,0:T(8,128)}, f32[4,256,12]{1,2,0:T(8,128)}, f32[4,256,12]{1,2,0:T(8,128)}, f32[4,256,256]{2,1,0:T(8,128)}) fusion(f32[4,256,12]{1,2,0:T(8,128)S(1)} %copy.587, f32[4,256,256]{2,1,0:T(8,128)} %fusion.259, f32[4,256,12]{1,2,0:T(8,128)S(1)} %copy.592, pred[256,256]{1,0:T(8,128)(4,1)S(1)} %iota_compare_fusion.4, ...), kind=kOutput, calls=%fused_computation.76.clone.1 | convolution fusion | flops 2462806016 | bytes 8699904 | tf_op jit(solution)/shard_map/transpose(jvp())/while/body/eval_jaxpr/checkpoint/sqkh,skhp->sqhp/dot_general | solution.py:30
  849.7 14.7 bitcast_dynamic-update-slice_fusion.11
  940.1 36.1 %all-reduce.12.cloned.1.call-done = f32[4,512,256]{2,1,0:T(8,128)} async-done(((f32[4,512,256]{2,1,0:T(8,128)}), f32[4,512,256]{2,1,0:T(8,128)}) %all-reduce.12.cloned.1.call-update) | async-done | bytes 2097168 | tf_op jit(solution)/shard_map/psum | solution.py:193
  976.2 20.2 %multiply_reduce_fusion.4 = (f32[1024]{0:T(1024)S(1)}, f32[1024]{0:T(1024)S(1)}, f32[1024]{0:T(1024)S(1)}, f32[1024]{0:T(1024)S(1)}, f32[1024]{0:T(1024)S(1)}, /*index=5*/f32[4,512,1024]{2,1,0:T(8,128)S(1)}) fusion(f32[4,515,1024]{2,1,0:T(8,128)} %maximum_convert_fusion, f32[4,512,1024]{2,1,0:T(8,128)} %get-tuple-element.792, ...), kind=kLoop, calls=%fused_computation.167 | loop fusion | flops 37743616 | bytes 58740736 | tf_op jit(solution)/shard_map/reduce_sum | solution.py:199
  996.5 12.2 broadcast_multiply_fusion.3
  1008.8 12.8 pad_add_fusion
  1059.3 437.3 %all-reduce.14.cloned.1.call-done = (f32[2048,1536]{1,0:T(8,128)}, f32[2048,1536]{1,0:T(8,128)}) async-done(((f32[2048,1536]{1,0:T(8,128)}, f32[2048,1536]{1,0:T(8,128)}), (f32[2048,1536]{1,0:T(8,128)}, f32[2048,1536]{1,0:T(8,128)})) %all-reduce.14.cloned.1.call-update) | async-done | bytes 25165840 | tf_op jit(solution)/shard_map/psum | solution.py:157
  1496.6 12.0 fusion.108
  1546.5 32.4 %all-reduce.7 = (f32[1536]{0:T(1024)}, f32[5,768]{1,0:T(8,128)}, f32[5,256]{1,0:T(8,128)}, f32[3,12]{1,0:T(4,128)}, f32[768]{0:T(1024)}) all-reduce(f32[1536]{0:T(1024)S(1)} %get-tuple-element.687, f32[5,768]{1,0:T(8,128)S(1)} %slice.213, f32[5,256]{1,0:T(8,128)S(1)} %slice.214, ...), channel_id=1, replica_groups=mesh['tensor'=4,'seq'=4,'dp'=2] {'seq','dp'}, use_global_device_ids=true, to_apply=%region_38.39 | all-reduce | flops 7460 | bytes 59680 | tf_op jit(solution)/shard_map/psum | solution.py:240
  1578.9 18.4 %fusion.107 = (bf16[2048,1536]{1,0:T(8,128)(2,1)}, bf16[2048,1536]{1,0:T(8,128)(2,1)}) fusion(bf16[4,512,1536]{2,1,0:T(8,128)(2,1)} %param.22, f32[2048,1536]{1,0:T(8,128)} %get-tuple-element.834, f32[2048]{0:T(1024)S(1)} %broadcast_multiply_fusion.5, f32[1536]{0:T(1024)S(1)} %copy-done.29, f32[2048]{0:T(1024)S(1)} %bitcast.567, ...), kind=kLoop, calls=%fused_computation.153 | loop fusion | flops 34603008 | bytes 50354176 | tf_op jit(solution)/shard_map/convert_element_type | solution.py:80
  1597.3 31.4 %reduce-scatter.7.cloned.1.call-done = f32[192,2,768]{2,0,1:T(8,128)} async-done(((f32[1536,2,768]{2,0,1:T(8,128)}), f32[192,2,768]{2,0,1:T(8,128)}) %reduce-scatter.7.cloned.1.call-update) | async-done | bytes 1179664 | tf_op jit(solution)/shard_map/reduce_scatter | solution.py:235
  1631.9 52.8 %reduce-scatter.11.cloned.1.call-done = f32[768,192]{0,1:T(8,128)} async-done(((f32[768,1536]{0,1:T(8,128)}), f32[768,192]{0,1:T(8,128)}) %reduce-scatter.11.cloned.1.call-update) | async-done | bytes 589840 | tf_op jit(solution)/shard_map/reduce_scatter | solution.py:238
  1684.7 35.2 %reduce-scatter.9.cloned.1.call-done = f32[192,256]{1,0:T(8,128)} async-done(((f32[1536,256]{1,0:T(8,128)}), f32[192,256]{1,0:T(8,128)}) %reduce-scatter.9.cloned.1.call-update) | async-done | bytes 196624 | tf_op jit(solution)/shard_map/reduce_scatter | solution.py:236
  (461 shorter events, 646.2 us)
Async XLA Ops:
  8.0 381.3 %copy-start = (bf16[768,1536]{1,0:T(8,128)(2,1)S(1)}, bf16[768,1536]{1,0:T(8,128)(2,1)}, u32[]{:S(2)}) copy-start(bf16[768,1536]{1,0:T(8,128)(2,1)} %param.32) | copy-start | bytes 7077892
  8.0 968.2 %all-reduce.12.cloned.1.call-start = ((), (), s32[]{:S(2)}) async-start(), calls=%async_computation.4 | async-start | bytes 4194304 | tf_op jit(solution)/shard_map/psum | solution.py:193
  25.4 19.3 %copy-start.4 = (bf16[4,512,1536]{2,1,0:T(8,128)(2,1)}, bf16[4,512,1536]{2,1,0:T(8,128)(2,1)S(1)}, u32[]{:S(2)}) copy-start(bf16[4,512,1536]{2,1,0:T(8,128)(2,1)S(1)} %fusion.112) | copy-start | bytes 18874372
  37.9 43.6 %collective-permute-start.2 = (bf16[4,3,1024]{2,1,0:T(4,128)(2,1)}, bf16[4,3,1024]{2,1,0:T(4,128)(2,1)}, u32[]{:S(2)}, u32[]{:S(2)}) collective-permute-start(bf16[4,3,1024]{2,1,0:T(4,128)(2,1)} %pad_maximum_fusion.2), channel_id=1, source_target_pairs={{0,2},{2,4},{4,6},{1,3},{3,5},{5,7},{8,10},{10,12},{12,14},{9,11},... | collective-permute-start | bytes 73736 | tf_op jit(solution)/shard_map/ppermute | solution.py:18
  69.8 17.0 copy-start.35
  69.8 17.0 copy-start.37
  219.1 36.6 %collective-permute-start = (f32[4,12,64,128]{3,2,1,0:T(8,128)}, f32[4,12,64,128]{3,2,1,0:T(8,128)}, u32[]{:S(2)}, u32[]{:S(2)}) collective-permute-start(f32[4,12,64,128]{3,2,1,0:T(8,128)} %multiply_add_fusion.14), channel_id=1, source_target_pairs={{0,2},{2,4},{4,6},{1,3},{3,5},{5,7},{8,10},{10,12},{12,14},{9,11},... | collective-permute-start | bytes 4718600 | tf_op jit(solution)/shard_map/while/body/eval_jaxpr/ppermute | solution.py:18
  259.0 37.1 %collective-permute-start = (f32[4,12,64,128]{3,2,1,0:T(8,128)}, f32[4,12,64,128]{3,2,1,0:T(8,128)}, u32[]{:S(2)}, u32[]{:S(2)}) collective-permute-start(f32[4,12,64,128]{3,2,1,0:T(8,128)} %multiply_add_fusion.14), channel_id=1, source_target_pairs={{0,2},{2,4},{4,6},{1,3},{3,5},{5,7},{8,10},{10,12},{12,14},{9,11},... | collective-permute-start | bytes 4718600 | tf_op jit(solution)/shard_map/while/body/eval_jaxpr/ppermute | solution.py:18
  299.4 36.2 %collective-permute-start = (f32[4,12,64,128]{3,2,1,0:T(8,128)}, f32[4,12,64,128]{3,2,1,0:T(8,128)}, u32[]{:S(2)}, u32[]{:S(2)}) collective-permute-start(f32[4,12,64,128]{3,2,1,0:T(8,128)} %multiply_add_fusion.14), channel_id=1, source_target_pairs={{0,2},{2,4},{4,6},{1,3},{3,5},{5,7},{8,10},{10,12},{12,14},{9,11},... | collective-permute-start | bytes 4718600 | tf_op jit(solution)/shard_map/while/body/eval_jaxpr/ppermute | solution.py:18
  366.3 23.0 %copy-start.49 = (f32[768]{0:T(1024)S(1)}, f32[768]{0:T(1024)}, u32[]{:S(2)}) copy-start(f32[768]{0:T(1024)} %param.31) | copy-start | bytes 9220
  389.3 19.9 %copy-start.39 = (f32[2048]{0:T(1024)}, f32[2048]{0:T(1024)S(1)}, u32[]{:S(2)}) copy-start(f32[2048]{0:T(1024)S(1)} %get-tuple-element.826) | copy-start | bytes 24580
  492.4 32.0 %collective-permute-start.1 = (f32[4,12,64,128]{3,2,1,0:T(8,128)}, f32[4,12,64,128]{3,2,1,0:T(8,128)}, u32[]{:S(2)}, u32[]{:S(2)}) collective-permute-start(f32[4,12,64,128]{3,2,1,0:T(8,128)} %multiply_add_fusion.15), channel_id=1, source_target_pairs={{2,0},{4,2},{6,4},{3,1},{5,3},{7,5},{10,8},{12,10},{14,12},{11,9},... | collective-permute-start | bytes 4718600 | tf_op jit(solution)/shard_map/while/body/eval_jaxpr/ppermute | solution.py:18
  527.6 31.3 %collective-permute-start.1 = (f32[4,12,64,128]{3,2,1,0:T(8,128)}, f32[4,12,64,128]{3,2,1,0:T(8,128)}, u32[]{:S(2)}, u32[]{:S(2)}) collective-permute-start(f32[4,12,64,128]{3,2,1,0:T(8,128)} %multiply_add_fusion.15), channel_id=1, source_target_pairs={{2,0},{4,2},{6,4},{3,1},{5,3},{7,5},{10,8},{12,10},{14,12},{11,9},... | collective-permute-start | bytes 4718600 | tf_op jit(solution)/shard_map/while/body/eval_jaxpr/ppermute | solution.py:18
  562.2 29.8 %collective-permute-start.1 = (f32[4,12,64,128]{3,2,1,0:T(8,128)}, f32[4,12,64,128]{3,2,1,0:T(8,128)}, u32[]{:S(2)}, u32[]{:S(2)}) collective-permute-start(f32[4,12,64,128]{3,2,1,0:T(8,128)} %multiply_add_fusion.15), channel_id=1, source_target_pairs={{2,0},{4,2},{6,4},{3,1},{5,3},{7,5},{10,8},{12,10},{14,12},{11,9},... | collective-permute-start | bytes 4718600 | tf_op jit(solution)/shard_map/while/body/eval_jaxpr/ppermute | solution.py:18
  626.5 24.5 %copy-start.16 = (f32[4,256,12]{1,2,0:T(8,128)}, f32[4,256,12]{1,2,0:T(8,128)S(1)}, u32[]{:S(2)}) copy-start(f32[4,256,12]{1,2,0:T(8,128)S(1)} %copy.592) | copy-start | bytes 147460 | tf_op jit(solution)/shard_map/transpose(jvp())/while
  627.7 23.3 %copy-start.17 = (f32[4,256,12]{1,2,0:T(8,128)}, f32[4,256,12]{1,2,0:T(8,128)S(1)}, u32[]{:S(2)}) copy-start(f32[4,256,12]{1,2,0:T(8,128)S(1)} %copy.587) | copy-start | bytes 147460 | tf_op jit(solution)/shard_map/transpose(jvp())/while
  627.8 23.2 %copy-start.18 = (pred[256,256]{1,0:T(8,128)(4,1)}, pred[256,256]{1,0:T(8,128)(4,1)S(1)}, u32[]{:S(2)}) copy-start(pred[256,256]{1,0:T(8,128)(4,1)S(1)} %iota_compare_fusion.4) | copy-start | bytes 196612 | tf_op jit(solution)/shard_map/transpose(jvp())/while
  762.4 24.3 %copy-start.16 = (f32[4,256,12]{1,2,0:T(8,128)}, f32[4,256,12]{1,2,0:T(8,128)S(1)}, u32[]{:S(2)}) copy-start(f32[4,256,12]{1,2,0:T(8,128)S(1)} %copy.592) | copy-start | bytes 147460 | tf_op jit(solution)/shard_map/transpose(jvp())/while
  763.7 23.0 %copy-start.17 = (f32[4,256,12]{1,2,0:T(8,128)}, f32[4,256,12]{1,2,0:T(8,128)S(1)}, u32[]{:S(2)}) copy-start(f32[4,256,12]{1,2,0:T(8,128)S(1)} %copy.587) | copy-start | bytes 147460 | tf_op jit(solution)/shard_map/transpose(jvp())/while
  763.7 23.0 %copy-start.18 = (pred[256,256]{1,0:T(8,128)(4,1)}, pred[256,256]{1,0:T(8,128)(4,1)S(1)}, u32[]{:S(2)}) copy-start(pred[256,256]{1,0:T(8,128)(4,1)S(1)} %iota_compare_fusion.4) | copy-start | bytes 196612 | tf_op jit(solution)/shard_map/transpose(jvp())/while
  907.1 589.5 %all-reduce.14.cloned.1.call-start = ((), (), s32[]{:S(2)}) async-start(), calls=%async_computation.9 | async-start | bytes 50331648 | tf_op jit(solution)/shard_map/psum | solution.py:157
  976.2 20.3 %copy-start.32 = (f32[1,1024]{1,0:T(1,128)S(1)}, f32[1,1024]{1,0:T(1,128)}, u32[]{:S(2)}) copy-start(f32[1,1024]{1,0:T(1,128)} %copy-done.31) | copy-start | bytes 12292
  976.2 20.3 %copy-start.34 = (f32[1,1024]{1,0:T(1,128)S(1)}, f32[1,1024]{1,0:T(1,128)}, u32[]{:S(2)}) copy-start(f32[1,1024]{1,0:T(1,128)} %copy-done.33) | copy-start | bytes 12292
  976.2 20.3 %copy-start.36 = (f32[1,1024]{1,0:T(1,128)S(1)}, f32[1,1024]{1,0:T(1,128)}, u32[]{:S(2)}) copy-start(f32[1,1024]{1,0:T(1,128)} %copy-done.35) | copy-start | bytes 12292
  976.2 20.3 %copy-start.38 = (f32[1,1024]{1,0:T(1,128)S(1)}, f32[1,1024]{1,0:T(1,128)}, u32[]{:S(2)}) copy-start(f32[1,1024]{1,0:T(1,128)} %copy-done.37) | copy-start | bytes 12292
  1021.6 5.8 collective-permute-start.3
  1053.0 443.6 %copy-start.23 = (bf16[1536,256]{1,0:T(8,128)(2,1)S(1)}, bf16[1536,256]{1,0:T(8,128)(2,1)}, u32[]{:S(2)}) copy-start(bf16[1536,256]{1,0:T(8,128)(2,1)} %param.26) | copy-start | bytes 2359300
  1053.0 443.6 %copy-start.29 = (f32[1536]{0:T(1024)S(1)}, f32[1536]{0:T(1024)}, u32[]{:S(2)}) copy-start(f32[1536]{0:T(1024)} %param.24) | copy-start | bytes 18436
  1053.0 491.8 %reduce-scatter.13.cloned.1.call-start = ((), (), s32[]{:S(2)}) async-start(), calls=%async_computation.8 | async-start | bytes 884736
  1059.2 569.5 %reduce-scatter.7.cloned.1.call-start = ((), (), s32[]{:S(2)}) async-start(), calls=%async_computation.5 | async-start | bytes 10616832 | tf_op jit(solution)/shard_map/reduce_scatter | solution.py:235
  1527.3 157.3 %reduce-scatter.11.cloned.1.call-start = ((), (), s32[]{:S(2)}) async-start(), calls=%async_computation.7 | async-start | bytes 5308416 | tf_op jit(solution)/shard_map/reduce_scatter | solution.py:238
  1538.5 181.5 %reduce-scatter.9.cloned.1.call-start = ((), (), s32[]{:S(2)}) async-start(), calls=%async_computation.6 | async-start | bytes 1769472 | tf_op jit(solution)/shard_map/reduce_scatter | solution.py:236
  (48 other events, 442.5 us)
Sparse Core Ops, SparseCore 0:
  907.2 68.9 all-reduce.11
  1053.1 443.4 all-reduce.13
Sparse Core Ops, SparseCore 1:
  1059.3 30.5 reduce-scatter.12
  1527.4 101.2 reduce-scatter.6
  1631.4 53.2 reduce-scatter.10
  1687.6 32.3 reduce-scatter.8
where the time goes:
time: 1740 us; the launch traced here: 1730 us
  waiting for transfers between devices  781 us (45%)
  matrix products  388 us (22%)
  local copies, waits for them, and re-layouts  229 us (13%)
  other arithmetic  227 us (13%)
  blocking collectives  50.5 us (3%)
  starting transfers between devices  26.3 us (2%)
    psum x1, waiting for transfers between devices, per_device(): mixer = lax.psum(out_terms, 'tensor')  437 us
    ppermute x8, waiting for transfers between devices, shifted(): return lax.ppermute(block, axis, route)  188 us
    dot_general x6, matrix products, block_step(): jnp.einsum('sqkh,skhp->sqhp', mixing, values, precision=PRECISE_MODE)  110 us
    dot_general x5, matrix products, times_transposed(): lax.dot_general(left, right, (((1,), (1,)), ((), ())), preferred_element_...  57 us
    dot_general x8, matrix products, block_step(): jnp.einsum('skh,skhp,skn->shpn', toward_end, values, inject, precision=PR...  55.1 us
    reduce_scatter x1, waiting for transfers between devices, per_device(): lax.psum_scatter(grad_weight_out, ('seq', 'dp'), scatter_dimension=1, til...  52.8 us
    dot_general x8, matrix products, block_step(): jnp.einsum('sqn,shpn->sqhp', readout, carry_state, precision=PRECISE_MODE)  49.6 us
    another operation x26, other arithmetic  45.2 us
  transfers between devices with their start and end apart: 14, of which 12 were waited for; matrix products, arithmetic and copies ran while one was open for 9% of the time, Pallas kernels for 0%

commit v1 on v0

v1 whole, which is shorter than its diff:
```python
import functools

import jax
import jax.numpy as jnp
from jax import lax
from jax.experimental import pallas as pl
from jax.experimental.pallas import tpu as pltpu
from jax.sharding import PartitionSpec as P

HEADDIM = 64
CONV = 4
BLOCK_LEN = 256
EPSILON = 1e-05
LOG2E = 1.4426950408889634
LANES = 128
SEG = 16
HALO = 16
VMEM = 60 * 1024 * 1024
STREAMS = 2

F32 = jnp.float32
LOW = jnp.bfloat16


def shifted(block, axis, distance):
    devices = range(lax.axis_size(axis))
    route = [(i - distance, i) for i in devices if i - distance in devices]
    return lax.ppermute(block, axis, route)


def mm(a, b):
    return lax.dot_general(a, b, (((1,), (0,)), ((), ())), preferred_element_type=F32)


def mm_nt(a, b):
    return lax.dot_general(a, b, (((1,), (1,)), ((), ())), preferred_element_type=F32)


def mm_tn(a, b):
    return lax.dot_general(a, b, (((0,), (0,)), ((), ())), preferred_element_type=F32)


def halves(a):
    high = a.astype(LOW)
    return high, (a - high.astype(F32)).astype(LOW)


def sigmoid(v):
    return 0.5 * jnp.tanh(0.5 * v) + 0.5


def lane_of(shape):
    return lax.broadcasted_iota(jnp.int32, shape, 1)


def first_lanes(a, count):
    return jnp.where(lane_of(a.shape) < count, a, 0.0)


def pieces_of(a):
    high = a.astype(LOW).astype(F32)
    rest = a - high
    middle = rest.astype(LOW).astype(F32)
    least = rest - middle
    return (high + pltpu.roll(middle, SEG, 1) + pltpu.roll(least, 2 * SEG, 1)).astype(LOW)


def spread_heads(a, one_hot):
    return mm(pieces_of(a), one_hot)


def sum_heads(a, one_hot_t):
    high, least = halves(a)
    return mm(high, one_hot_t) + mm(least, one_hot_t)


def running_sum(a, triangle, heads):
    p = mm(triangle, pieces_of(a))
    p = p + pltpu.roll(p, LANES - SEG, 1) + pltpu.roll(p, LANES - 2 * SEG, 1)
    return first_lanes(p, heads)


def row_sums(a):
    rows, width = a.shape
    return jnp.sum(a.reshape(rows // 8, 8, width), axis=0)


def lower(extent):
    return lax.broadcasted_iota(jnp.int32, (extent, extent), 0) >= lane_of((extent, extent))


def pair_split(tile):
    first = lane_of(tile.shape) < HEADDIM
    zero = jnp.zeros_like(tile)
    return jnp.where(first, tile, zero), jnp.where(first, zero, tile)


def params(vmem=VMEM):
    return pltpu.CompilerParams(dimension_semantics=("arbitrary",), vmem_limit_bytes=vmem)


def whole(shape):
    return pl.BlockSpec(shape, lambda i: (0,) * len(shape), pipeline_mode=pl.Buffered(1))


def per_seq(*shape, offset=0):
    return pl.BlockSpec((1,) + shape, lambda i: (i + offset,) + (0,) * len(shape))


def project_kernel(
    heads, width, state, block,
    x_ref, halo_ref, gain_ref, main_w, side_w, taps_ref, terms_ref, hot_ref,
    low_ref, mixed_ref, edge_ref, pre_ref, gate_ref, heads_ref, step_ref, y_ref, state_ref, end_ref, through_ref,
    low_scr, mix_scr, k_scr,
):
    rows = x_ref.shape[1]
    gain = gain_ref[...]

    def lowered(x):
        x = x.astype(F32)
        scale = lax.rsqrt(jnp.mean(x * x, axis=1, keepdims=True) + EPSILON)
        return (x * scale * gain).astype(LOW)

    low_scr[:HALO] = lowered(halo_ref[0])
    low_scr[HALO:] = lowered(x_ref[0])
    low_ref[0] = low_scr[HALO:]
    gate_ref[0] = mm(low_scr[HALO:], main_w[:, :width])
    main_in = mm(low_scr[...], main_w[:, width:]).astype(LOW)
    side_in = mm(low_scr[...], side_w[...])
    mix_scr[:, :width] = main_in.astype(F32)
    mix_scr[:, width:] = side_in[:, : 2 * state].astype(LOW).astype(F32)
    mixed_ref[0] = mix_scr[HALO:].astype(LOW)
    edge_ref[0] = mix_scr[:HALO].astype(LOW)
    conv = taps_ref[CONV : CONV + 1]
    for k in range(CONV):
        at = HALO - (CONV - 1) + k
        conv = conv + taps_ref[k : k + 1] * mix_scr[at : at + rows]
    pre_ref[0] = conv
    active = conv * sigmoid(conv)
    step_arg = side_in[HALO:, 2 * state :] + terms_ref[0:1]
    step = jnp.maximum(step_arg, 0.0) + jnp.log1p(jnp.exp(-jnp.abs(step_arg)))
    step = first_lanes(step, heads)
    slope = first_lanes(sigmoid(step_arg), heads)
    decay2 = step * (terms_ref[1:2] * LOG2E)
    hot = hot_ref[...]
    triangle = lower(block).astype(F32).astype(LOW)
    sub = block // 2
    tri_sub = lower(sub)
    k_scr[:, :sub, sub:block] = jnp.zeros((2, sub, sub), LOW)
    k_scr[:, :sub, block + sub :] = jnp.zeros((2, sub, sub), LOW)
    held = None
    for b in range(rows // block):
        span = slice(b * block, (b + 1) * block)
        run = running_sum(decay2[span], triangle, heads)
        heads_ref[0, span] = step[span] + pltpu.roll(run, SEG, 1) + pltpu.roll(slope[span], 2 * SEG, 1)
        last = run[block - 1 : block]
        toward = jnp.exp2(last - run)
        values = active[span, :width]
        stepped = spread_heads(step[span], hot) * values
        step_low = stepped.astype(LOW)
        step_ref[0, span] = step_low
        inject_h, inject_l = halves(active[span, width : width + state])
        readout_h, readout_l = halves(active[span, width + state :])
        meet = mm_nt(readout_h, inject_h) + mm_nt(readout_l, inject_h) + mm_nt(readout_h, inject_l)
        meet_tiles = {
            (0, 0): jnp.where(tri_sub, meet[:sub, :sub], 0.0),
            (1, 0): meet[sub:, :sub],
            (1, 1): jnp.where(tri_sub, meet[sub:, sub:], 0.0),
        }
        run_t = jnp.transpose(run)
        for pair in range(heads // 2):
            slot = pair % 2
            for j in range(2):
                h = 2 * pair + j
                for (r, c), tile in meet_tiles.items():
                    gap = run[r * sub : (r + 1) * sub, h : h + 1] - run_t[h : h + 1, c * sub : (c + 1) * sub]
                    at = j * block + c * sub
                    k_scr[slot, r * sub : (r + 1) * sub, at : at + sub] = (
                        tile * jnp.exp2(jnp.minimum(gap, 0.0))
                    ).astype(LOW)
            lanes = slice(pair * LANES, (pair + 1) * LANES)
            one, two = pair_split(step_low[:, lanes])
            y_ref[0, span, lanes] = mm(k_scr[slot], jnp.concatenate([one, two], axis=0))
        weighed = (spread_heads(first_lanes(toward, heads), hot) * stepped).astype(LOW)
        gained = mm_tn(inject_h, weighed)
        through = spread_heads(first_lanes(jnp.broadcast_to(jnp.exp2(last), (8, LANES)), heads), hot)
        if held is not None:
            gained = gained + held * through[0:1]
            total_through = total_through * through
        else:
            total_through = through
        held = gained
        state_ref[0, b] = held
    end_ref[0] = held
    through_ref[0] = total_through


def gate_kernel(
    heads, width, state, block,
    y_in, pre_ref, gate_ref, heads_ref, state_ref, back_ref, gain_ref, skip_ref, hot_ref, *refs,
):
    y_ref, enter_ref, stats_ref = refs[-3:]
    rows = y_in.shape[1]
    hot = hot_ref[...]
    enter = decayed = sum(ref[0] for ref in refs[:-3])
    enter_ref[0] = enter
    gain = gain_ref[...]
    skip = skip_ref[...]
    for b in range(rows // block):
        span = slice(b * block, (b + 1) * block)
        run = first_lanes(pltpu.roll(heads_ref[0, span], LANES - SEG, 1), heads)
        grown = spread_heads(first_lanes(jnp.exp2(run), heads), hot)
        pre = pre_ref[0, span]
        active = pre * sigmoid(pre)
        readout_h, readout_l = halves(active[:, width + state :])
        enter_h, enter_l = halves(enter)
        carried = mm(readout_h, enter_h) + mm(readout_l, enter_h) + mm(readout_h, enter_l)
        y = y_in[0, span] + grown * carried
        y_ref[0, span] = y
        decayed = decayed * grown[block - 1 : block]
        enter = state_ref[0, b] + decayed
        scanned = y + skip * active[:, :width]
        gate = gate_ref[0, span]
        gated = scanned * (gate * sigmoid(gate))
        squares = jnp.sum(gated * gated, axis=1, keepdims=True)
        inner = jnp.sum(gated * (back_ref[0, span] * gain), axis=1, keepdims=True)
        lane = lane_of((block, LANES))
        stats = jnp.where(lane == 0, squares, jnp.where(lane == 1, inner, 0.0))
        stats_ref[0, :, span] = jnp.transpose(stats)[:8]


def out_kernel(
    heads, width, state, block, inner_total, rank_ref,
    y_ref, pre_ref, gate_ref, heads_ref, back_ref, stats_ref, gain_ref, skip_ref, hot_ref,
    normed_ref, grad_y_ref, grad_gate_ref, adjoint_ref, sums_ref, *out_refs,
):
    rows = y_ref.shape[1]

    @pl.when(pl.program_id(0) == 0)
    def _():
        sums_ref[...] = jnp.zeros_like(sums_ref)

    hot = hot_ref[...]
    gain = gain_ref[...]
    skip = skip_ref[...]
    held = None
    for b in reversed(range(rows // block)):
        span = slice(b * block, (b + 1) * block)
        total = jnp.sum(stats_ref[:, 0, :, span], axis=0)
        total = jnp.transpose(jnp.concatenate([total, jnp.zeros((LANES - 8, block), F32)], axis=0))
        scale = lax.rsqrt(total[:, 0:1] / inner_total + EPSILON)
        bend = scale * scale * scale * (total[:, 1:2] / inner_total)
        pre = pre_ref[0, span]
        active = pre * sigmoid(pre)
        values = active[:, :width]
        scanned = y_ref[0, span] + skip * values
        gate = gate_ref[0, span]
        sig = sigmoid(gate)
        gate_act = gate * sig
        gated = scanned * gate_act
        normed = (gated * scale * gain).astype(LOW)
        normed_ref[0, span] = normed
        back = back_ref[0, span]
        grad_gated = scale * (back * gain) - gated * bend
        grad_y = grad_gated * gate_act
        grad_y_ref[0, span] = grad_y
        grad_gate_ref[0, span] = (grad_gated * scanned * (sig * (1.0 + gate * (1.0 - sig)))).astype(LOW)
        sums_ref[:8] += row_sums(back * gated * scale)
        sums_ref[8:] += row_sums(grad_y * values)
        run = first_lanes(pltpu.roll(heads_ref[0, span], LANES - SEG, 1), heads)
        grown = spread_heads(first_lanes(jnp.exp2(run), heads), hot)
        gained = mm_tn(active[:, width + state :].astype(LOW), (grown * grad_y).astype(LOW))
        if held is not None:
            gained = gained + held * grown[block - 1 : block]
        held = gained
        adjoint_ref[0, b] = held
    by_rank(normed_ref[0], rank_ref[0], out_refs)


def back_kernel(
    heads, width, state, block,
    y_ref, pre_ref, mixed_ref, edge_ref, heads_ref, step_ref, grad_y_ref, enter_ref, state_ref, adjoint_ref,
    taps_ref, terms_ref, skip_ref, hot_ref, hot_t_ref, *refs,
):
    leave_refs, refs = refs[:-10], refs[-10:]
    (
    grad_mixed_ref, grad_step_ref, head_ref, tail_ref, filter_ref, terms_out_ref,
    k_scr, u_scr, cross_scr, conv_scr,
    ) = refs
    rows = y_ref.shape[1]
    blocks = rows // block

    @pl.when(pl.program_id(0) == 0)
    def _():
        filter_ref[...] = jnp.zeros_like(filter_ref)
        terms_out_ref[...] = jnp.zeros_like(terms_out_ref)

    hot = hot_ref[...]
    hot_t = hot_t_ref[...]
    skip = skip_ref[...]
    sub = block // 2
    tri = lower(block)
    upper_sub = jnp.logical_not(lower(sub)) | (
        lax.broadcasted_iota(jnp.int32, (sub, sub), 0) == lane_of((sub, sub))
    )
    upper = jnp.logical_not(tri) | (
        lax.broadcasted_iota(jnp.int32, (block, block), 0) == lane_of((block, block))
    )
    suffix = upper.astype(F32).astype(LOW)
    rate = terms_ref[1:2]
    k_scr[:, sub:, :sub] = jnp.zeros((2, sub, sub), LOW)
    k_scr[:, sub:, block : block + sub] = jnp.zeros((2, sub, sub), LOW)
    conv_scr[:HALO] = jnp.zeros((HALO, conv_scr.shape[1]), F32)
    conv_scr[HALO + rows :] = jnp.zeros((HALO, conv_scr.shape[1]), F32)
    leave = sum(ref[0].astype(F32) for ref in leave_refs)
    runs = [first_lanes(pltpu.roll(heads_ref[0, b * block : (b + 1) * block], LANES - SEG, 1), heads) for b in range(blocks)]
    enters = [enter_ref[0]]
    decayed = enter_ref[0]
    for b in range(blocks):
        last = jnp.broadcast_to(jnp.exp2(runs[b][block - 1 : block]), (8, LANES))
        decayed = decayed * spread_heads(first_lanes(last, heads), hot)[0:1]
        enters.append(state_ref[0, b] + decayed)
    for b in reversed(range(blocks)):
        span = slice(b * block, (b + 1) * block)
        packed = heads_ref[0, span]
        step = first_lanes(packed, heads)
        slope_step = first_lanes(pltpu.roll(packed, LANES - 2 * SEG, 1), heads)
        run = runs[b]
        last = run[block - 1 : block]
        pre = pre_ref[0, span]
        sig = sigmoid(pre)
        active = pre * sig
        slope = sig * (1.0 + pre * (1.0 - sig))
        values = active[:, :width]
        inject_h, inject_l = halves(active[:, width : width + state])
        readout_h, readout_l = halves(active[:, width + state :])
        step_low = step_ref[0, span]
        grad_y = grad_y_ref[0, span]
        grad_low = grad_y.astype(LOW)
        leave_low = leave.astype(LOW)
        toward = spread_heads(first_lanes(jnp.exp2(last - run), heads), hot)
        grown = spread_heads(first_lanes(jnp.exp2(run), heads), hot)
        grown_h, grown_l = halves(grown * grad_y)
        u_scr[...] = toward * mm(inject_h, leave_low)
        meet = mm_nt(inject_h, readout_h) + mm_nt(inject_h, readout_l) + mm_nt(inject_l, readout_h)
        meet_tiles = {
            (0, 0): jnp.where(upper_sub, meet[:sub, :sub], 0.0),
            (0, 1): meet[:sub, sub:],
            (1, 1): jnp.where(upper_sub, meet[sub:, sub:], 0.0),
        }
        run_t = jnp.transpose(run)
        cross_scr[...] = jnp.zeros_like(cross_scr)
        for pair in range(heads // 2):
            slot = pair % 2
            lanes = slice(pair * LANES, (pair + 1) * LANES)
            tile_low = step_low[:, lanes]
            split = pair_split(grad_low[:, lanes])
            for j in range(2):
                h = 2 * pair + j
                products = {}
                top = mm_nt(tile_low[:sub], split[j])
                products[(0, 0)] = top[:, :sub]
                products[(0, 1)] = top[:, sub:]
                products[(1, 1)] = mm_nt(tile_low[sub:], split[j][sub:])
                for (r, c), tile in meet_tiles.items():
                    gap = run_t[h : h + 1, c * sub : (c + 1) * sub] - run[r * sub : (r + 1) * sub, h : h + 1]
                    fall = jnp.exp2(jnp.minimum(gap, 0.0))
                    at = j * block + c * sub
                    k_scr[slot, r * sub : (r + 1) * sub, at : at + sub] = (tile * fall).astype(LOW)
                    cross_scr[r * sub : (r + 1) * sub, c * sub : (c + 1) * sub] += fall * products[(r, c)]
            u_scr[:, lanes] += mm(k_scr[slot], jnp.concatenate(split, axis=0))
        cross = jnp.where(upper, cross_scr[...], 0.0).astype(LOW)
        enter_h, enter_l = halves(enters[b])
        grad_readout = (
            mm_tn(cross, inject_h) + mm_nt(grown_h, enter_h) + mm_nt(grown_l, enter_h) + mm_nt(grown_h, enter_l)
        )
        weighed = (toward * step_low.astype(F32)).astype(LOW)
        grad_inject = mm(cross, readout_h) + mm_nt(weighed, leave_low)
        u = u_scr[...]
        grad_step = sum_heads(values * u, hot_t)
        taken = step_low.astype(F32) * u
        given = grad_low.astype(F32) * y_ref[0, span]
        flow = running_sum(sum_heads(given - taken, hot_t), suffix, heads)
        ends = jnp.sum(leave * enters[b + 1], axis=0, keepdims=True)
        flow = flow + first_lanes(sum_heads(jnp.broadcast_to(ends, (8, width)), hot_t)[0:1], heads)
        grad_arg = (grad_step + rate * flow) * slope_step
        grad_step_ref[0, span] = grad_arg.astype(LOW)
        terms_out_ref[:8] += row_sums(grad_arg)
        terms_out_ref[8:] += row_sums(flow * step * rate)
        grad_values = spread_heads(step, hot) * u + skip * grad_y
        conv_scr[HALO + b * block : HALO + (b + 1) * block, :width] = grad_values * slope[:, :width]
        conv_scr[HALO + b * block : HALO + (b + 1) * block, width : width + state] = (
            grad_inject * slope[:, width : width + state]
        )
        conv_scr[HALO + b * block : HALO + (b + 1) * block, width + state :] = (
            grad_readout * slope[:, width + state :]
        )
        if b:
            leave = adjoint_ref[0, b] + grown[block - 1 : block] * leave
    head_ref[0] = conv_scr[HALO : HALO + 8]
    mixed = mixed_ref[0].astype(F32)
    edge = edge_ref[0].astype(F32)
    total = None
    for k in range(CONV):
        ahead = CONV - 1 - k
        moved = conv_scr[HALO + ahead : HALO + ahead + rows]
        term = taps_ref[k : k + 1] * moved
        total = term if total is None else total + term
        filter_ref[8 * k : 8 * k + 8] += row_sums(mixed * moved) + row_sums(edge * conv_scr[ahead : ahead + HALO])
    filter_ref[8 * CONV :] += row_sums(conv_scr[HALO : HALO + rows])
    high, least = halves(total)
    grad_mixed_ref[0, :, : width + 2 * state] = high
    grad_mixed_ref[0, :, width + 2 * state :] = least[:, width:]
    tail_ref[0] = total[rows - HALO :]


def top_kernel(rows, first, length_ref, place_ref, cot_ref, out_w, top_ref, back_ref):
    valid = length_ref[first + pl.program_id(0)] - place_ref[0]
    cot = cot_ref[0]
    row = lax.broadcasted_iota(jnp.int32, cot.shape, 0)
    top = jnp.where(row < valid, cot.astype(F32), 0.0).astype(LOW)
    top_ref[0] = top
    back_ref[0] = mm_nt(top, out_w[...])


def by_rank(rows, rank, out_refs):
    share = out_refs[0].shape[0]
    count = rows.shape[0] // share
    for k in range(count):
        place = (pl.program_id(0) * count + k) ^ rank
        for d in range(len(out_refs)):

            @pl.when(place == d)
            def _(k=k, d=d):
                out_refs[d][...] = rows[k * share : (k + 1) * share]


def lowered_kernel(width, state, gate_ref, mixed_ref, step_ref, main_w, side_w, out_ref):
    main = jnp.concatenate([gate_ref[0], mixed_ref[0, :, :width]], axis=1)
    side = jnp.concatenate([mixed_ref[0, :, width : width + 2 * state], step_ref[0]], axis=1)
    out_ref[0] = (mm_nt(main, main_w[...]) + mm_nt(side, side_w[...])).astype(LOW)


def product_kernel(ranks, rank_ref, *refs):
    x_refs, weight_ref = refs[:STREAMS], refs[STREAMS]
    parts = refs[STREAMS + 1 : -2]
    out_ref, acc_ref = refs[-2:]
    share = parts[0].shape[0]
    at = pl.program_id(0)
    for d in range(ranks):

        @pl.when(at == d)
        def _(d=d):
            rows = jnp.concatenate([parts[s * ranks + d][...] for s in range(STREAMS)], axis=0)
            part = mm(rows, weight_ref[0])
            if d == 0:
                part = part + jnp.concatenate([x[0].astype(F32) for x in x_refs], axis=0)
            else:
                part = part + acc_ref[...]
            acc_ref[...] = part

    @pl.when(at == ranks - 1)
    def _():
        for s in range(STREAMS):
            out_ref[s] = acc_ref[s * share : (s + 1) * share].astype(LOW)


def merged(ref):
    return ref[...].reshape(ref.shape[0] * ref.shape[1], ref.shape[2])


def lane_sums(a):
    return sum(a[:, k : k + LANES] for k in range(0, a.shape[1], LANES))


def gate_grad_kernel(*refs):
    low, grads = refs[:STREAMS], refs[STREAMS : 2 * STREAMS]
    main_w, out_ref, gain_ref = refs[2 * STREAMS :]
    gate = sum(mm_tn(merged(a), merged(b)) for a, b in zip(low, grads))
    out_ref[...] = gate.astype(LOW)
    gain_ref[...] = lane_sums(main_w[...].astype(F32) * gate)


def out_grad_kernel(*refs):
    top, normed, out_ref = refs[:STREAMS], refs[STREAMS : 2 * STREAMS], refs[-1]
    out_ref[...] = sum(mm_tn(merged(a), merged(b)) for a, b in zip(top, normed)).astype(LOW)


def late_kernel(width, state, *refs):
    low, mixed, step = (refs[k * STREAMS : (k + 1) * STREAMS] for k in range(3))
    main_w, side_w, gain_in, own_ref, shared_ref, gain_ref = refs[3 * STREAMS :]
    total = sum(mm_tn(merged(a), merged(b)) for a, b in zip(low, mixed))
    steps = sum(mm_tn(merged(a), merged(b)) for a, b in zip(low, step))
    main = total[:, :width]
    shared = total[:, width : width + 2 * state] + total[:, width + 2 * state :]
    own_ref[:, :width] = main.astype(LOW)
    own_ref[:, width:] = steps.astype(LOW)
    shared_ref[...] = shared
    side = side_w[...].astype(F32)
    gain_ref[...] = (
        gain_in[...]
        + lane_sums(main_w[...].astype(F32) * main)
        + lane_sums(side[:, : 2 * state] * shared)
        + side[:, 2 * state :] * steps
    )


def by_rank(rows, rank, out_refs):
    share = out_refs[0].shape[0]
    count = rows.shape[0] // share
    for k in range(count):
        place = (pl.program_id(0) * count + k) ^ rank
        for d in range(len(out_refs)):

            @pl.when(place == d)
            def _(k=k, d=d):
                out_refs[d][...] = rows[k * share : (k + 1) * share]


def lowered_kernel(width, state, rank_ref, gate_ref, mixed_ref, step_ref, main_w, side_w, *out_refs):
    main = jnp.concatenate([gate_ref[0], mixed_ref[0, :, :width]], axis=1)
    side = jnp.concatenate([mixed_ref[0, :, width : width + 2 * state], step_ref[0]], axis=1)
    total = (mm_nt(main, main_w[...]) + mm_nt(side, side_w[...])).astype(LOW)
    by_rank(total, rank_ref[0], out_refs)


def norm_kernel(ranks, rank_ref, x_ref, top_ref, gain_ref, *refs):
    out_ref = refs[ranks]
    x = x_ref[0].astype(F32)
    scale = lax.rsqrt(jnp.mean(x * x, axis=1, keepdims=True) + EPSILON)
    normed = x * scale
    grad = sum(ref[...].astype(F32) for ref in refs[:ranks])
    scaled = grad * gain_ref[...]
    out = top_ref[0].astype(F32) + scale * (scaled - normed * jnp.mean(scaled * normed, axis=1, keepdims=True))
    out_ref[...] = out.astype(LOW)


def per_device(
    residual_in,
    lengths,
    input_gain,
    main_in_weight,
    weight_shared,
    step_in_weight,
    filter_main,
    filter_shared,
    head_terms,
    output_gain,
    out_projection_weight,
    cotangent,
):
    all_seqs, rows, model = residual_in.shape
    seqs = all_seqs // STREAMS
    heads = step_in_weight.shape[1]
    width = main_in_weight.shape[2]
    state = weight_shared.shape[1] // 2
    mixed_width = width + 2 * state
    kept_width = mixed_width + 2 * state
    ranks = lax.axis_size("tensor")
    spans = lax.axis_size("seq")
    inner_total = width * ranks
    reach = CONV - 1
    block = min(BLOCK_LEN, rows)
    blocks = rows // block
    share = seqs * rows // ranks
    sds = jax.ShapeDtypeStruct

    main_w = main_in_weight.reshape(model, 2 * width)
    side_w = jnp.concatenate(
        [weight_shared, jnp.pad(step_in_weight, ((0, 0), (0, LANES - heads)))], axis=1
    )
    side_width = side_w.shape[1]
    taps = jnp.pad(jnp.concatenate([filter_main, filter_shared], axis=1), ((0, 8 - CONV - 1), (0, 0)))
    rate = -jnp.exp(head_terms[1])
    terms = jnp.pad(jnp.stack([head_terms[0], rate]), ((0, 6), (0, LANES - heads)))
    skip = jnp.repeat(head_terms[2], HEADDIM)[None]
    channel_head = jnp.arange(width, dtype=jnp.int32)[None, :] // HEADDIM
    lane = jnp.arange(LANES, dtype=jnp.int32)[:, None]
    hot = ((lane % SEG == channel_head) & (lane < 3 * SEG)).astype(LOW)
    hot_t = (lane == channel_head).astype(LOW).T
    in_gain = input_gain[None]
    out_gain = output_gain[None]
    dims = (heads, width, state, block)
    place = (lax.axis_index("seq") * rows).astype(jnp.int32)[None]
    rank = lax.axis_index("tensor").astype(jnp.int32)[None]
    halo = shifted(residual_in[:, rows - HALO :, :], "seq", 1)
    full_w = lax.all_gather(out_projection_weight, "tensor", axis=0)
    smem = pl.BlockSpec(memory_space=pltpu.SMEM)

    def cost(flops):
        return pl.CostEstimate(flops=int(flops), bytes_accessed=30 << 20, transcendentals=0)

    def after(value, *others):
        return lax.optimization_barrier((value,) + others)[0]

    def project(s, halo):
        return pl.pallas_call(
            functools.partial(project_kernel, *dims),
            grid=(seqs,),
            in_specs=[
                per_seq(rows, model, offset=s * seqs), per_seq(HALO, model, offset=s * seqs), whole((1, model)),
                whole((model, 2 * width)), whole((model, side_width)), whole((8, mixed_width)), whole((8, LANES)),
                whole((LANES, width)),
            ],
            out_specs=[
                per_seq(rows, model), per_seq(rows, mixed_width), per_seq(HALO, mixed_width),
                per_seq(rows, mixed_width), per_seq(rows, width), per_seq(rows, LANES), per_seq(rows, width),
                per_seq(rows, width), per_seq(blocks, state, width), per_seq(state, width), per_seq(8, width),
            ],
            out_shape=[
                sds((seqs, rows, model), LOW), sds((seqs, rows, mixed_width), LOW),
                sds((seqs, HALO, mixed_width), LOW), sds((seqs, rows, mixed_width), F32),
                sds((seqs, rows, width), F32), sds((seqs, rows, LANES), F32), sds((seqs, rows, width), LOW),
                sds((seqs, rows, width), F32), sds((seqs, blocks, state, width), F32),
                sds((seqs, state, width), F32), sds((seqs, 8, width), F32),
            ],
            scratch_shapes=[
                pltpu.VMEM((HALO + rows, model), LOW), pltpu.VMEM((HALO + rows, mixed_width), F32),
                pltpu.VMEM((2, block, 2 * block), LOW),
            ],
            compiler_params=params(),
            cost_estimate=cost(8e9 * seqs),
            name="project",
        )(residual_in, halo, in_gain, main_w, side_w, taps, terms, hot)

    def chained(local, through, direction, kind, marks):
        arrivals = []
        for hop in range(spans - 1):
            sender = hop if direction > 0 else spans - 1 - hop
            sent = local if hop == 0 else local + through[:, :1] * arrivals[-1].astype(F32)
            arrived = lax.ppermute(sent.astype(kind), "seq", [(sender, sender + direction)])
            arrivals.append(after(arrived, marks[min(hop, len(marks) - 1)]))
        return arrivals

    def top_of(s, place):
        return pl.pallas_call(
            functools.partial(top_kernel, rows, s * seqs),
            grid=(seqs,),
            in_specs=[smem, smem, per_seq(rows, model, offset=s * seqs), whole((width, model))],
            out_specs=[per_seq(rows, model), per_seq(rows, width)],
            out_shape=[sds((seqs, rows, model), LOW), sds((seqs, rows, width), F32)],
            compiler_params=params(),
            cost_estimate=cost(2.5e9 * seqs),
            name="top",
        )(lengths, place, cotangent, out_projection_weight)

    def gated_of(y_local, pre, gate, packed, arrivals, states, back):
        return pl.pallas_call(
            functools.partial(gate_kernel, *dims),
            grid=(seqs,),
            in_specs=[
                per_seq(rows, width), per_seq(rows, mixed_width), per_seq(rows, width), per_seq(rows, LANES),
                per_seq(blocks, state, width), per_seq(rows, width), whole((1, width)),
                whole((1, width)), whole((LANES, width)),
            ]
            + [per_seq(state, width)] * len(arrivals),
            out_specs=[per_seq(rows, width), per_seq(state, width), per_seq(8, rows)],
            out_shape=[sds((seqs, rows, width), F32), sds((seqs, state, width), F32), sds((seqs, 8, rows), F32)],
            compiler_params=params(),
            cost_estimate=cost(4e9 * seqs),
            name="gated",
        )(y_local, pre, gate, packed, states, back, out_gain, skip, hot, *arrivals)

    def outward(y, pre, gate, packed, back, all_stats):
        seq = lambda *shape: pl.BlockSpec((1,) + shape, lambda i, r: (i,) + (0,) * len(shape))
        fixed = lambda *shape: pl.BlockSpec(shape, lambda i, r: (0,) * len(shape))
        return pl.pallas_call(
            functools.partial(out_kernel, *dims, inner_total),
            grid_spec=pltpu.PrefetchScalarGridSpec(
                num_scalar_prefetch=1,
                grid=(seqs,),
                in_specs=[
                    seq(rows, width), seq(rows, mixed_width), seq(rows, width), seq(rows, LANES), seq(rows, width),
                    pl.BlockSpec((ranks, 1, 8, rows), lambda i, r: (0, i, 0, 0)), fixed(1, width), fixed(1, width),
                    fixed(LANES, width),
                ],
                out_specs=[
                    seq(rows, width), seq(rows, width), seq(rows, width), seq(blocks, state, width), fixed(16, width),
                ]
                + [fixed(share, width)] * ranks,
            ),
            out_shape=[
                sds((seqs, rows, width), LOW), sds((seqs, rows, width), F32), sds((seqs, rows, width), LOW),
                sds((seqs, blocks, state, width), F32), sds((16, width), F32),
            ]
            + [sds((share, width), LOW)] * ranks,
            compiler_params=params(),
            cost_estimate=cost(5e9 * seqs),
            name="outward",
        )(rank, y, pre, gate, packed, back, all_stats, out_gain, skip, hot)

    def backward(y, pre, mixed, edge, packed, stepped, grad_y, entering, states, leaving, adjoint):
        return pl.pallas_call(
            functools.partial(back_kernel, *dims),
            grid=(seqs,),
            in_specs=[
                per_seq(rows, width), per_seq(rows, mixed_width), per_seq(rows, mixed_width),
                per_seq(HALO, mixed_width), per_seq(rows, LANES), per_seq(rows, width), per_seq(rows, width),
                per_seq(state, width), per_seq(blocks, state, width),
                per_seq(blocks, state, width), whole((8, mixed_width)), whole((8, LANES)), whole((1, width)),
                whole((LANES, width)), whole((width, LANES)),
            ]
            + [per_seq(state, width)] * len(leaving),
            out_specs=[
                per_seq(rows, kept_width), per_seq(rows, LANES), per_seq(8, mixed_width), per_seq(HALO, mixed_width),
                pl.BlockSpec((8 * (CONV + 1), mixed_width), lambda i: (0, 0)),
                pl.BlockSpec((16, LANES), lambda i: (0, 0)),
            ],
            out_shape=[
                sds((seqs, rows, kept_width), LOW), sds((seqs, rows, LANES), LOW), sds((seqs, 8, mixed_width), F32),
                sds((seqs, HALO, mixed_width), F32), sds((8 * (CONV + 1), mixed_width), F32), sds((16, LANES), F32),
            ],
            scratch_shapes=[
                pltpu.VMEM((2, block, 2 * block), LOW), pltpu.VMEM((block, width), F32),
                pltpu.VMEM((block, block), F32), pltpu.VMEM((2 * HALO + rows, mixed_width), F32),
            ],
            compiler_params=params(),
            cost_estimate=cost(11e9 * seqs),
            name="backward",
        )(
            y, pre, mixed, edge, packed, stepped, grad_y, entering, states, adjoint,
            taps, terms, skip, hot, hot_t, *leaving,
        )

    def lowered_of(grad_gate, grad_mixed, grad_step):
        seq = lambda *shape: pl.BlockSpec((1,) + shape, lambda i, r: (i,) + (0,) * len(shape))
        fixed = lambda *shape: pl.BlockSpec(shape, lambda i, r: (0,) * len(shape), pipeline_mode=pl.Buffered(1))
        return pl.pallas_call(
            functools.partial(lowered_kernel, width, state),
            grid_spec=pltpu.PrefetchScalarGridSpec(
                num_scalar_prefetch=1,
                grid=(seqs,),
                in_specs=[
                    seq(rows, width), seq(rows, kept_width), seq(rows, LANES), fixed(model, 2 * width),
                    fixed(model, side_width),
                ],
                out_specs=[pl.BlockSpec((share, model), lambda i, r: (0, 0))] * ranks,
            ),
            out_shape=[sds((share, model), LOW)] * ranks,
            compiler_params=params(),
            cost_estimate=cost(4.5e9 * seqs),
            name="lowered",
        )(rank, grad_gate, grad_mixed, grad_step, main_w, side_w)

    def input_norm(s, parts, top):
        return pl.pallas_call(
            functools.partial(norm_kernel, ranks),
            grid_spec=pltpu.PrefetchScalarGridSpec(
                num_scalar_prefetch=1,
                grid=(1,),
                in_specs=[
                    pl.BlockSpec((1, share, model), lambda i, r: (s * ranks + r[0], 0, 0)),
                    pl.BlockSpec((1, share, model), lambda i, r: (r[0], 0, 0)),
                    pl.BlockSpec((1, model), lambda i, r: (0, 0)),
                ]
                + [pl.BlockSpec((share, model), lambda i, r: (0, 0))] * ranks,
                out_specs=pl.BlockSpec((share, model), lambda i, r: (0, 0)),
            ),
            out_shape=sds((share, model), LOW),
            compiler_params=params(),
            name="input_norm",
        )(rank, residual_in.reshape(-1, share, model), top.reshape(-1, share, model), in_gain, *parts)

    def product(parts):
        row_of = lambda s: pl.BlockSpec((1, share, model), lambda i, r: (s * ranks + r[0], 0, 0))
        x = residual_in.reshape(-1, share, model)
        return pl.pallas_call(
            functools.partial(product_kernel, ranks),
            grid_spec=pltpu.PrefetchScalarGridSpec(
                num_scalar_prefetch=1,
                grid=(ranks,),
                in_specs=[row_of(s) for s in range(STREAMS)]
                + [pl.BlockSpec((1, width, model), lambda i, r: (r[0] ^ i, 0, 0))]
                + [pl.BlockSpec((share, width), lambda i, r: (0, 0))] * (STREAMS * ranks),
                out_specs=pl.BlockSpec((STREAMS, share, model), lambda i, r: (0, 0, 0)),
                scratch_shapes=[pltpu.VMEM((STREAMS * share, model), F32)],
            ),
            out_shape=sds((STREAMS, share, model), LOW),
            compiler_params=params(),
            cost_estimate=cost(2.4e9 * all_seqs),
            name="product",
        )(rank, *[x] * STREAMS, full_w, *parts)

    tile = 256
    tiles = model // tile
    column = pl.BlockSpec((seqs, rows, tile), lambda i: (0, 0, i))
    row = lambda n: pl.BlockSpec((tile, n), lambda i: (i, 0))

    def gate_grad(low, grads):
        return pl.pallas_call(
            gate_grad_kernel,
            grid=(tiles,),
            in_specs=[column] * STREAMS + [whole((seqs, rows, width))] * STREAMS + [row(width)],
            out_specs=[row(width), row(LANES)],
            out_shape=[sds((model, width), LOW), sds((model, LANES), F32)],
            compiler_params=params(),
            cost_estimate=cost(2.5e9 * all_seqs),
            name="gate_grad",
        )(*low, *grads, main_w)

    def out_grad(top, normed):
        return pl.pallas_call(
            out_grad_kernel,
            grid=(tiles,),
            in_specs=[column] * STREAMS + [whole((seqs, rows, width))] * STREAMS,
            out_specs=row(width),
            out_shape=sds((model, width), LOW),
            compiler_params=params(),
            cost_estimate=cost(2.5e9 * all_seqs),
            name="out_grad",
        )(*top, *normed)

    def late_of(low, mixed, step, gain):
        return pl.pallas_call(
            functools.partial(late_kernel, width, state),
            grid=(tiles,),
            in_specs=[column] * STREAMS
            + [whole((seqs, rows, kept_width))] * STREAMS
            + [whole((seqs, rows, LANES))] * STREAMS
            + [pl.BlockSpec((tile, width), lambda i: (i, 1)), row(side_width), row(LANES)],
            out_specs=[row(width + LANES), row(2 * state), row(LANES)],
            out_shape=[sds((model, width + LANES), LOW), sds((model, 2 * state), F32), sds((model, LANES), F32)],
            compiler_params=params(),
            cost_estimate=cost(5e9 * all_seqs),
            name="late",
        )(*low, *mixed, *step, main_w, side_w, gain)

    def exchanged(own):
        return [own] + [
            lax.ppermute(own, "tensor", [(i, i ^ d) for i in range(ranks)]) for d in range(1, ranks)
        ]

    def swapped(blocks_of):
        return [
            lax.ppermute(b, "tensor", [(i, i ^ d) for i in range(ranks)]) if d else b for d, b in enumerate(blocks_of)
        ]

    def scattered(whole_rows):
        blocks_of = whole_rows.reshape(ranks, share, -1)
        return swapped([lax.dynamic_index_in_dim(blocks_of, rank[0] ^ d, axis=0, keepdims=False) for d in range(ranks)])

    def assembled(ready, pieces):
        held = ready.reshape(-1, share, model)
        count = held.shape[0]

        def kernel(rank_ref, held_ref, *refs):
            out_ref, sems = refs[ranks:]
            copies = [pltpu.make_async_copy(held_ref, out_ref.at[pl.ds(0, count)], sems.at[ranks])]
            for d in range(ranks):
                copies.append(pltpu.make_async_copy(refs[d], out_ref.at[count + (rank_ref[0] ^ d)], sems.at[d]))
            for copy in copies:
                copy.start()
            for copy in copies:
                copy.wait()

        return pl.pallas_call(
            kernel,
            in_specs=[smem] + [pl.BlockSpec(memory_space=pltpu.VMEM)] * (1 + ranks),
            out_specs=pl.BlockSpec(memory_space=pl.ANY),
            out_shape=sds((count + ranks, share, model), LOW),
            scratch_shapes=[pltpu.SemaphoreType.DMA((ranks + 1,))],
            compiler_params=pltpu.CompilerParams(vmem_limit_bytes=VMEM),
            name="assemble",
        )(rank, held, *pieces).reshape(residual_in.shape)

    flat = lambda a: a.reshape(seqs * rows, a.shape[-1])
    both = range(STREAMS)

    def gate_on(values, *marks):
        return list(lax.optimization_barrier(tuple(values) + marks)[: len(values)])

    def backward_of(s, leaving, mark, fill):
        made, step_low, head, tail, filter_sum, term_sum = backward(
            after(y[s], mark), pre[s], mixed[s], edge[s], packed[s], stepped[s], grad_y[s], entering[s], states[s],
            leaving, adjoint[s],
        )
        raw = step_low
        following = after(shifted(head[:, :reach], "seq", -1), fill(raw))
        fix = jnp.zeros((seqs, reach, mixed_width), F32)
        for k in range(reach):
            fix = fix + jnp.pad(taps[k] * following[:, : reach - k], ((0, 0), (k, 0), (0, 0)))
        tail = tail + jnp.pad(fix, ((0, 0), (HALO - reach, 0), (0, 0)))
        tail_high = tail.astype(LOW)
        tail_least = (tail - lax.optimization_barrier(tail_high).astype(F32)).astype(LOW)[:, :, width:]
        made = lax.dynamic_update_slice(
            made, jnp.concatenate([tail_high, tail_least], axis=2), (0, rows - HALO, 0)
        )
        return made, step_low, filter_sum, term_sum, raw

    reduced = lambda a: lax.psum_scatter(a, ("seq", "dp"), scatter_dimension=0, tiled=True)

    first = [project(0, halo)]
    first.append(project(1, after(halo, first[0][-1])))
    low, mixed, edge, pre, gate, packed, stepped, y_local, states, local, through = zip(*first)
    tops = [top_of(0, after(place, local[1]))]
    tops.append(top_of(1, after(place, tops[0][0])))
    top, back = zip(*tops)

    def gated_of_stream(s, arrivals):
        y, entering, stats = gated_of(y_local[s], pre[s], gate[s], packed[s], arrivals, states[s], back[s])
        return y, entering, stats, lax.all_gather(stats, "tensor", axis=0)

    y, entering, stats, all_stats = [None] * 2, [None] * 2, [None] * 2, [None] * 2
    second = []
    arrivals = chained(local[0], through[0], 1, F32, [local[1], top[0], top[1]])
    y[0], entering[0], stats[0], all_stats[0] = gated_of_stream(0, arrivals)
    second.append(outward(y[0], pre[0], gate[0], packed[0], back[0], all_stats[0]))
    arrivals = chained(local[1], through[1], 1, F32, [top[1], stats[0], second[0][0]])
    y[1], entering[1], stats[1], all_stats[1] = gated_of_stream(1, arrivals)
    parts = gate_on(swapped(second[0][5:]), all_stats[1])
    second.append(outward(after(y[1], *parts), pre[1], gate[1], packed[1], back[1], all_stats[1]))
    normed, grad_y, grad_gate, adjoint, out_sums = list(zip(*second))[:5]
    gate_w, gain_sums = gate_grad(gate_on(low, normed[1]), grad_gate)
    gate_w_sum = reduced(gate_w)
    made_out = product(parts + gate_on(swapped(second[1][5:]), gate_w))
    block_out = lax.all_gather(made_out, "tensor", axis=1, tiled=True)
    leaving = chained(adjoint[0][:, 0], through[0], -1, LOW, [stats[1], normed[1], gate_w])
    early = []

    def out_first(raw):
        early.append(out_grad(gate_on(top, raw), normed))
        return early[0]

    third = [backward_of(0, leaving, made_out, out_first)]
    out_w = reduced(early[0])
    leaving = chained(adjoint[1][:, 0], through[1], -1, LOW, [gate_w, made_out, third[0][4]])
    partial = [lowered_of(grad_gate[0], *third[0][:2])]
    first_own = []

    def norm_first(raw):
        first_own.append(input_norm(0, gate_on(swapped(partial[0]), raw), top[0]))
        return first_own[0]

    third.append(backward_of(1, gate_on(leaving, gate_w_sum), partial[0][0], norm_first))
    first_in = lax.all_gather(first_own[0], "tensor", axis=0, tiled=True)
    grad_mixed, grad_step, filter_sums, term_sums = list(zip(*third))[:4]
    grad_own, grad_side, gain_sums = late_of(low, grad_mixed, grad_step, gain_sums)
    partial.append(lowered_of(after(grad_gate[1], grad_own, block_out, out_w), *third[1][:2]))
    grad_own_w = reduced(grad_own).astype(F32)
    shared_w = reduced(grad_side)
    grad_gate_w = gate_w_sum.astype(F32)
    grad_out_w = out_w.astype(F32).T
    grad_main_w = jnp.stack([grad_gate_w, grad_own_w[:, :width]], axis=1)
    grad_shared_w = jnp.sum(lax.all_gather(shared_w, "tensor", axis=0), axis=0)
    grad_step_w = grad_own_w[:, width : width + heads]
    filters = jnp.sum(sum(filter_sums).reshape(CONV + 1, 8, mixed_width), axis=1)
    term_rows = jnp.sum(sum(term_sums).reshape(2, 8, LANES), axis=1)
    out_rows = jnp.sum(sum(out_sums).reshape(2, 8, width), axis=1)
    grad_skip = jnp.pad(jnp.sum(out_rows[1].reshape(heads, HEADDIM), axis=1), (0, LANES - heads))
    everywhere = (jnp.sum(gain_sums, axis=1) / input_gain, filters[:, width:])
    per_rank = (filters[:, :width], jnp.concatenate([term_rows, grad_skip[None]], axis=0), out_rows[0])
    packed_sums = jnp.concatenate([a.reshape(-1) for a in everywhere + per_rank])
    packed_sums = jnp.sum(lax.all_gather(packed_sums.reshape(-1, LANES), ("seq", "dp"), axis=0), axis=0)
    split = (everywhere[0].size + everywhere[1].size) // LANES
    shared_sums = jnp.sum(lax.all_gather(packed_sums[:split], "tensor", axis=0), axis=0).reshape(-1)
    rank_sums = packed_sums[split:].reshape(-1)
    small_in = shared_sums[:model]
    small_shared = shared_sums[model:].reshape(CONV + 1, 2 * state)
    small_main = rank_sums[: (CONV + 1) * width].reshape(CONV + 1, width)
    small_terms = rank_sums[(CONV + 1) * width : -width].reshape(3, LANES)[:, :heads]
    small_out = rank_sums[-width:]
    own = input_norm(1, gate_on(swapped(partial[1]), shared_sums), top[1])
    pieces = exchanged(own)
    return (
        block_out.reshape(residual_in.shape),
        assembled(first_in, gate_on(pieces, grad_out_w)),
        small_in,
        grad_main_w,
        grad_shared_w,
        grad_step_w,
        small_main,
        small_shared,
        small_terms,
        small_out,
        grad_out_w,
    )


def solution(mesh):
    placed = (
        P("dp", "seq", None),
        P("dp"),
        P(),
        P(None, None, "tensor"),
        P(),
        P(None, "tensor"),
        P(None, "tensor"),
        P(),
        P(None, "tensor"),
        P("tensor"),
        P("tensor", None),
        P("dp", "seq", None),
    )
    return jax.shard_map(
        per_device,
        mesh=mesh,
        in_specs=placed,
        out_specs=(
            P("dp", "seq", None),
            P("dp", "seq", None),
            P(),
            P(("seq", "dp"), None, "tensor"),
            P(("seq", "dp"), None),
            P(("seq", "dp"), "tensor"),
            P(None, "tensor"),
            P(),
            P(None, "tensor"),
            P("tensor"),
            P("tensor", ("seq", "dp")),
        ),
        check_vma=False,
    )
```

time: 1740 us -> 517 us (0.30)
  waiting for transfers between devices: 781 us -> 80.8 us
  matrix products: 388 us -> 0 us
  Pallas kernels: 0 us -> 236 us
  other arithmetic: 227 us -> 11.9 us
  local copies, waits for them, and re-layouts: 229 us -> 31.8 us
  blocking collectives: 50.5 us -> 86.9 us
  starting transfers between devices: 26.3 us -> 44.1 us
    psum x2 -> x0, waiting for transfers between devices: 473 us -> none  [the longest x1 437 us: per_device(): mixer = lax.psum(out_terms, 'tensor')]
    dot_general x47 -> x0, matrix products: 388 us -> none  [the longest x6 110 us: block_step(): jnp.einsum('sqkh,skhp->sqhp', mixing, values, precision=PRECISE_MODE)]
    pallas_call x0 -> x19, Pallas kernels: none -> 236 us  [the longest x2 49.8 us: backward(): pl.pallas_call(functools.partial(back_kernel, *dims), grid=(seqs,), in_sp...]
    ppermute x8 -> x3, waiting for transfers between devices: 188 us -> 41 us  [shifted(): return lax.ppermute(block, axis, route)]
    reduce_scatter x3 -> x4, waiting for transfers between devices: 119 us -> 0.03 us  [per_device(): lax.psum_scatter(a, ('seq', 'dp'), scatter_dimension=0, tiled=True)]
    all_gather x0 -> x5, blocking collectives: none -> 86.9 us  [the longest x1 29.4 us: per_device(): grad_shared_w = jnp.sum(lax.all_gather(shared_w, 'tensor', axis=0), axis=0)]
    another operation x28 -> x3, other arithmetic: 51.7 us -> 0.72 us  [the longest x1 0.6 us: per_device(): jnp.stack([head_terms[0], rate])]
    reduce_sum x10 -> x8, other arithmetic: 51.8 us -> 1.25 us  [the longest x1 0.73 us: per_device(): grad_shared_w = jnp.sum(lax.all_gather(shared_w, 'tensor', axis=0), axis=0)]
  transfers between devices with their start and end apart: 14 -> 37, of which waited for: 12 -> 7; matrix products, arithmetic and copies ran while one was open for 9% -> 6% of each run, Pallas kernels for 0% -> 45%
where the time goes in v1:
time: 517 us; the launch traced here: 509 us
  Pallas kernels  236 us (46%)
  blocking collectives  86.9 us (17%)
  waiting for transfers between devices  80.8 us (16%)
  starting transfers between devices  44.1 us (9%)
  local copies, waits for them, and re-layouts  31.8 us (6%)
  between operations  17 us (3%)
  other arithmetic  11.9 us (2%)
    pallas_call x2, Pallas kernels, backward(): pl.pallas_call(functools.partial(back_kernel, *dims), grid=(seqs,), in_sp...  49.8 us
    pallas_call x2, Pallas kernels, project(): pl.pallas_call(functools.partial(project_kernel, *dims), grid=(seqs,), in...  43.9 us
    ppermute x3, waiting for transfers between devices, shifted(): return lax.ppermute(block, axis, route)  41 us
    all_gather x1, blocking collectives, per_device(): grad_shared_w = jnp.sum(lax.all_gather(shared_w, 'tensor', axis=0), axis=0)  29.4 us
    pallas_call x2, Pallas kernels, lowered_of(): pl.pallas_call(functools.partial(lowered_kernel, width, state), grid_spec...  25.7 us
    ppermute x12, waiting for transfers between devices, swapped(): lax.ppermute(b, 'tensor', [(i, i ^ d) for i in range(ranks)])  24.9 us
    all_gather x1, blocking collectives, per_device(): lax.all_gather(packed_sums[:split], 'tensor', axis=0)  24.2 us
    pallas_call x2, Pallas kernels, outward(): pl.pallas_call(functools.partial(out_kernel, *dims, inner_total), grid_sp...  23.8 us
  transfers between devices with their start and end apart: 37, of which 7 were waited for; matrix products, arithmetic and copies ran while one was open for 6% of the time, Pallas kernels for 45%

profile of v1, /device:TPU:0, one launch (start us, length us, event | category | flops | bytes accessed | tf_op | source)
XLA Modules:
  0.0 508.8 jit_solution(960692872363804402)
XLA Ops:
  9.7 4.9 collective-permute-start
  14.8 5.5 %copy.40 = bf16[192,8,2,768]{3,1,2,0:T(8,128)(2,1)} copy(bf16[192,8,2,768]{3,2,1,0:T(2,128)(2,1)} %bitcast.73) | data formatting | bytes 9437184
  25.0 21.8 %project.2 = (bf16[2,512,1536]{2,1,0:T(8,128)(2,1)}, bf16[2,512,1024]{2,1,0:T(8,128)(2,1)}, bf16[2,16,1024]{2,1,0:T(8,128)(2,1)}, f32[2,512,1024]{2,1,0:T(8,128)...) custom-call(bf16[4,512,1536]{2,1,0:T(8,128)(2,1)} %x_ref.3, ...), custom_call_target="tpu_custom_call" | custom-call | flops 16000000000 | bytes 31457280 | tf_op jit(solution)/shard_map/project/pallas_call | solution.py:597
  51.6 22.0 %project.3 = (bf16[2,512,1536]{2,1,0:T(8,128)(2,1)}, bf16[2,512,1024]{2,1,0:T(8,128)(2,1)}, bf16[2,16,1024]{2,1,0:T(8,128)(2,1)}, f32[2,512,1024]{2,1,0:T(8,128)...) custom-call(bf16[4,512,1536]{2,1,0:T(8,128)(2,1)} %x_ref.3, ...), custom_call_target="tpu_custom_call" | custom-call | flops 16000000000 | bytes 31457280 | tf_op jit(solution)/shard_map/project/pallas_call | solution.py:597
  79.7 6.2 %top.2 = (bf16[2,512,1536]{2,1,0:T(8,128)(2,1)}, f32[2,512,768]{2,1,0:T(8,128)}) custom-call(s32[4]{0:T(128)} %length_ref.3, s32[1]{0:T(128)} %bitcast.3.place_ref, bf16[4,512,1536]{2,1,0:T(8,128)(2,1)} %cot_ref.3, bf16[768,1536]{1,0:T(8,128)(2,1)} %out_w.3), custom_call_target="tpu_custom_call" | custom-call | flops 5000000000 | bytes 31457280 | tf_op jit(solution)/shard_map/top/pallas_call | solution.py:636
  89.4 6.2 %top.3 = (bf16[2,512,1536]{2,1,0:T(8,128)(2,1)}, f32[2,512,768]{2,1,0:T(8,128)}) custom-call(s32[4]{0:T(128)} %length_ref.3, s32[1]{0:T(128)} %bitcast.3.place_ref, bf16[4,512,1536]{2,1,0:T(8,128)(2,1)} %cot_ref.3, bf16[768,1536]{1,0:T(8,128)(2,1)} %out_w.3), custom_call_target="tpu_custom_call" | custom-call | flops 5000000000 | bytes 31457280 | tf_op jit(solution)/shard_map/top/pallas_call | solution.py:636
  99.2 9.5 %gated.2 = (f32[2,512,768]{2,1,0:T(8,128)}, f32[2,128,768]{2,1,0:T(8,128)}, f32[2,8,512]{2,1,0:T(8,128)}) custom-call(f32[2,512,768]{2,1,0:T(8,128)} %get-tuple-element.134.y_in, f32[2,512,1024]{2,1,0:T(8,128)} %get-tuple-element.135.pre_ref, f32[2,512,768]{2,1,0:T(8,128)} %get-tuple-element.136.gate_ref, f32[2,512,128]{2,1,0:T(8,128)} %get-tuple-element.137.heads_ref, ...), custom_call_target="tpu_custom_call" | custom-call | flops 8000000000 | bytes 31457280 | tf_op jit(solution)/shard_map/gated/pallas_call | solution.py:648
  110.0 9.1 %all-gather.1 = f32[8,8,512]{2,1,0:T(8,128)} all-gather(f32[2,8,512]{2,1,0:T(8,128)S(1)} %copy-done.29), channel_id=3, replica_groups=mesh['tensor'=4,'seq'=4,'dp'=2] {'tensor'}, dimensions={0}, use_global_device_ids=true | all-gather | bytes 163840 | tf_op jit(solution)/shard_map/all_gather | solution.py:901
  119.1 11.7 %outward.2 = (bf16[2,512,768]{2,1,0:T(8,128)(2,1)}, f32[2,512,768]{2,1,0:T(8,128)}, bf16[2,512,768]{2,1,0:T(8,128)(2,1)}, f32[2,2,128,768]{3,2,1,0:T(8,128)}, f3...) custom-call(s32[1]{0:T(128)} %bitcast.rank_ref, ...), custom_call_target="tpu_custom_call" | custom-call | flops 10000000000 | bytes 31457280 | tf_op jit(solution)/shard_map/outward/pallas_call | solution.py:667
  137.2 9.5 %gated.3 = (f32[2,512,768]{2,1,0:T(8,128)}, f32[2,128,768]{2,1,0:T(8,128)}, f32[2,8,512]{2,1,0:T(8,128)}) custom-call(f32[2,512,768]{2,1,0:T(8,128)} %get-tuple-element.157.y_in, f32[2,512,1024]{2,1,0:T(8,128)} %get-tuple-element.158.pre_ref, f32[2,512,768]{2,1,0:T(8,128)} %get-tuple-element.159.gate_ref, f32[2,512,128]{2,1,0:T(8,128)} %get-tuple-element.160.heads_ref, ...), custom_call_target="tpu_custom_call" | custom-call | flops 8000000000 | bytes 31457280 | tf_op jit(solution)/shard_map/gated/pallas_call | solution.py:648
  146.7 9.2 %all-gather.2 = f32[8,8,512]{2,1,0:T(8,128)} all-gather(f32[2,8,512]{2,1,0:T(8,128)} %get-tuple-element.168), channel_id=4, replica_groups=mesh['tensor'=4,'seq'=4,'dp'=2] {'tensor'}, dimensions={0}, use_global_device_ids=true | all-gather | bytes 163840 | tf_op jit(solution)/shard_map/all_gather | solution.py:901
  156.0 12.1 %outward.3 = (bf16[2,512,768]{2,1,0:T(8,128)(2,1)}, f32[2,512,768]{2,1,0:T(8,128)}, bf16[2,512,768]{2,1,0:T(8,128)(2,1)}, f32[2,2,128,768]{3,2,1,0:T(8,128)}, f3...) custom-call(s32[1]{0:T(128)} %bitcast.rank_ref, ...), custom_call_target="tpu_custom_call" | custom-call | flops 10000000000 | bytes 31457280 | tf_op jit(solution)/shard_map/outward/pallas_call | solution.py:667
  168.9 10.7 %gate_grad.1 = (bf16[1536,768]{1,0:T(8,128)(2,1)}, f32[1536,128]{1,0:T(8,128)}) custom-call(bf16[2,512,1536]{2,1,0:T(8,128)(2,1)} %get-tuple-element.182.refs_0_, bf16[2,512,1536]{2,1,0:T(8,128)(2,1)} %get-tuple-element.183.refs_1_, bf16[2,512,768]{2,1,0:T(8,128)(2,1)} %get-tuple-element.184.refs_2_.gate_ref, ...), custom_call_target="tpu_custom_call" | custom-call | flops 10000000000 | bytes 31457280 | tf_op jit(solution)/shard_map/gate_grad/pallas_call | solution.py:790
  185.5 5.2 %collective-permute-done.10.refs_8_ = bf16[256,768]{1,0:T(8,128)(2,1)S(1)} collective-permute-done((bf16[256,768]{1,0:T(8,128)(2,1)}, bf16[256,768]{1,0:T(8,128)(2,1)S(1)}, u32[]{:S(2)}, u32[]{:S(2)}) %collective-permute-start.10) | collective-permute-done | bytes 393248 | tf_op jit(solution)/shard_map/ppermute | solution.py:835
  190.7 4.7 collective-permute-done.11.refs_9_
  196.3 11.5 %collective-permute-done.15.refs_2_ = bf16[2,128,768]{2,1,0:T(8,128)(2,1)S(1)} collective-permute-done((bf16[2,128,768]{2,1,0:T(8,128)(2,1)S(1)}, bf16[2,128,768]{2,1,0:T(8,128)(2,1)S(1)}, u32[]{:S(2)}, u32[]{:S(2)}) %collective-permute-start.15) | collective-permute-done | bytes 393248 | tf_op jit(solution)/shard_map/ppermute | solution.py:631
  207.8 10.4 %product.1 = bf16[2,256,1536]{2,1,0:T(8,128)(2,1)} custom-call(s32[1]{0:T(128)} %bitcast.rank_ref, bf16[8,256,1536]{2,1,0:T(8,128)(2,1)} %bitcast.67, bf16[8,256,1536]{2,1,0:T(8,128)(2,1)} %bitcast.68, bf16[4,768,1536]{2,1,0:T(8,128)(2,1)} %bitcast.101, bf16[256,768]{1,0:T(8,128)(2,1)} %get-tuple-element.169.refs_3_, bf16[256,768]{1,0:T(8,128)(2,1)} %copy-done.40, ...), custom_call_target="tpu_custom_call" | custom-call | flops 9600000000 | bytes 31457280 | tf_op jit(solution)/shard_map/product/pallas_call | solution.py:767
  218.2 25.1 %backward.2 = (bf16[2,512,1280]{2,1,0:T(8,128)(2,1)}, bf16[2,512,128]{2,1,0:T(8,128)(2,1)}, f32[2,8,1024]{2,1,0:T(8,128)}, f32[2,16,1024]{2,1,0:T(8,128)}, f32[40,1024]{1,0:T(8,128)}, /*index=5*/f32[16,128]{1,0:T(8,128)}) custom-call(f32[2,512,768]{2,1,0:T(8,128)} %get-tuple-element.191.y_ref, f32[2,512,1024]{2,1,0:T(8,128)} %get-tuple-element.135.pre_ref, ...), custom_call_target="tpu_custom_call" | custom-call | flops 22000001024 | bytes 31457280 | tf_op jit(solution)/shard_map/backward/pallas_call | solution.py:693
  243.2 9.9 %out_grad.1 = bf16[1536,768]{1,0:T(8,128)(2,1)} custom-call(bf16[2,512,1536]{2,1,0:T(8,128)(2,1)} %get-tuple-element.205.refs_0_, bf16[2,512,1536]{2,1,0:T(8,128)(2,1)} %get-tuple-element.206.refs_1_, bf16[2,512,768]{2,1,0:T(8,128)(2,1)} %get-tuple-element.166.refs_2_, bf16[2,512,768]{2,1,0:T(8,128)(2,1)} %get-tuple-element.181.refs_3_), custom_call_target="tpu_custom_call" | custom-call | flops 10000000000 | bytes 31457280 | tf_op jit(solution)/shard_map/out_grad/pallas_call | solution.py:802
  259.0 41.0 %collective-permute-done.16 = f32[2,3,1024]{2,1,0:T(4,128)S(1)} collective-permute-done((f32[2,3,1024]{2,1,0:T(4,128)S(1)}, f32[2,3,1024]{2,1,0:T(4,128)S(1)}, u32[]{:S(2)}, u32[]{:S(2)}) %collective-permute-start.16) | collective-permute-done | bytes 24608 | tf_op jit(solution)/shard_map/ppermute | solution.py:28
  300.8 12.9 %lowered.2 = (bf16[256,1536]{1,0:T(8,128)(2,1)}, bf16[256,1536]{1,0:T(8,128)(2,1)}, bf16[256,1536]{1,0:T(8,128)(2,1)}, bf16[256,1536]{1,0:T(8,128)(2,1)}) custom-call(s32[1]{0:T(128)} %bitcast.rank_ref, bf16[2,512,768]{2,1,0:T(8,128)(2,1)} %get-tuple-element.184.refs_2_.gate_ref, bf16[2,512,1280]{2,1,0:T(8,128)(2,1)} %maximum_dynamic-update-slice_fusion.mixed_ref.refs_2_, ...), custom_call_target="tpu_custom_call" | custom-call | flops 8999999488 | bytes 31457280 | tf_op jit(solution)/shard_map/lowered/pallas_call | solution.py:728
  317.2 24.8 %backward.3 = (bf16[2,512,1280]{2,1,0:T(8,128)(2,1)}, bf16[2,512,128]{2,1,0:T(8,128)(2,1)}, f32[2,8,1024]{2,1,0:T(8,128)}, f32[2,16,1024]{2,1,0:T(8,128)}, f32[40,1024]{1,0:T(8,128)}, /*index=5*/f32[16,128]{1,0:T(8,128)}) custom-call(f32[2,512,768]{2,1,0:T(8,128)} %get-tuple-element.212.y_ref, f32[2,512,1024]{2,1,0:T(8,128)} %get-tuple-element.158.pre_ref, ...), custom_call_target="tpu_custom_call" | custom-call | flops 22000001024 | bytes 31457280 | tf_op jit(solution)/shard_map/backward/pallas_call | solution.py:693
  348.2 10.9 %collective-permute-done.19.refs_3_ = bf16[256,1536]{1,0:T(8,128)(2,1)S(1)} collective-permute-done((bf16[256,1536]{1,0:T(8,128)(2,1)}, bf16[256,1536]{1,0:T(8,128)(2,1)S(1)}, u32[]{:S(2)}, u32[]{:S(2)}) %collective-permute-start.19) | collective-permute-done | bytes 786464 | tf_op jit(solution)/shard_map/ppermute | solution.py:835
  360.0 4.6 input_norm.2
  365.4 15.9 %late.1 = (bf16[1536,896]{1,0:T(8,128)(2,1)}, f32[1536,256]{1,0:T(8,128)}, f32[1536,128]{1,0:T(8,128)}) custom-call(bf16[2,512,1536]{2,1,0:T(8,128)(2,1)} %get-tuple-element.182.refs_0_, bf16[2,512,1536]{2,1,0:T(8,128)(2,1)} %get-tuple-element.183.refs_1_, bf16[2,512,1280]{2,1,0:T(8,128)(2,1)} %maximum_dynamic-update-slice_fusion.mixed_ref.refs_2_, ...), custom_call_target="tpu_custom_call" | custom-call | flops 20000000000 | bytes 31457280 | tf_op jit(solution)/shard_map/late/pallas_call | solution.py:814
  383.9 12.8 %lowered.3 = (bf16[256,1536]{1,0:T(8,128)(2,1)}, bf16[256,1536]{1,0:T(8,128)(2,1)}, bf16[256,1536]{1,0:T(8,128)(2,1)}, bf16[256,1536]{1,0:T(8,128)(2,1)}) custom-call(s32[1]{0:T(128)} %bitcast.rank_ref, bf16[2,512,768]{2,1,0:T(8,128)(2,1)} %get-tuple-element.236.refs_3_.gate_ref, bf16[2,512,1280]{2,1,0:T(8,128)(2,1)} %maximum_dynamic-update-slice_fusion.1.refs_3_.mixed_ref, ...), custom_call_target="tpu_custom_call" | custom-call | flops 8999999488 | bytes 31457280 | tf_op jit(solution)/shard_map/lowered/pallas_call | solution.py:728
  401.3 15.0 %all_gather.47 = f32[8,61,128]{2,1,0:T(8,128)S(1)} all-gather(f32[1,61,128]{2,1,0:T(8,128)S(1)} %bitcast.100), channel_id=1, replica_groups=mesh['tensor'=4,'seq'=4,'dp'=2] {'seq','dp'}, dimensions={0}, use_global_device_ids=true | all-gather | bytes 281088 | tf_op jit(solution)/shard_map/all_gather | solution.py:953
  416.9 24.2 %all-gather.5 = f32[4,22,128]{2,1,0:T(8,128)S(1)} all-gather(f32[1,22,128]{2,1,0:T(8,128)S(1)} %slice_bitcast_fusion.3), channel_id=5, replica_groups=mesh['tensor'=4,'seq'=4,'dp'=2] {'tensor'}, dimensions={0}, use_global_device_ids=true | all-gather | bytes 56320 | tf_op jit(solution)/shard_map/all_gather | solution.py:955
  444.7 4.7 input_norm.3.refs_0_
  452.8 29.4 %all-gather.4 = f32[768,256]{1,0:T(8,128)S(1)} all-gather(f32[192,256]{1,0:T(8,128)} %reduce-scatter.11.cloned.1.call-done), channel_id=6, replica_groups=mesh['tensor'=4,'seq'=4,'dp'=2] {'tensor'}, dimensions={0}, use_global_device_ids=true | all-gather | bytes 983040 | tf_op jit(solution)/shard_map/all_gather | solution.py:944
  489.6 5.5 %assemble.1 = bf16[8,256,1536]{2,1,0:T(8,128)(2,1)} custom-call(s32[1]{0:T(128)} %bitcast.rank_ref, bf16[4,256,1536]{2,1,0:T(8,128)(2,1)} %bitcast.83, bf16[256,1536]{1,0:T(8,128)(2,1)} %input_norm.3.refs_0_, bf16[256,1536]{1,0:T(8,128)(2,1)} %copy-done.4, bf16[256,1536]{1,0:T(8,128)(2,1)} %copy-done.5, bf16[256,1536]{1,0:T(8,128)(2,1)} %collective-permute-done.29.refs_3_), custom_call_target="tpu_custom_call" | custom-call | tf_op jit(solution)/shard_map/assemble/pallas_call | solution.py:856
  495.1 5.9 %copy.66 = bf16[4,512,1536]{2,1,0:T(8,128)(2,1)} copy(bf16[4,512,1536]{2,1,0:T(8,128)(2,1)} %bitcast.71) | data formatting | bytes 12582912
  (256 shorter events, 78.9 us)
Async XLA Ops:
  8.0 199.8 %all-gather.14.cloned.1.call-start = ((), (), s32[]{:S(2)}) async-start(), calls=%async_computation.10 | async-start | bytes 11796480 | tf_op jit(solution)/shard_map/all_gather | solution.py:587
  8.7 308.4 %reduce-scatter.5.cloned.1.call-start = ((), (), s32[]{:S(2)}) async-start(), calls=%async_computation.5 | async-start | bytes 2654208 | tf_op jit(solution)/shard_map/reduce_scatter | solution.py:890
  9.7 14.6 %collective-permute-start = (bf16[4,16,1536]{2,1,0:T(8,128)(2,1)S(1)}, bf16[4,16,1536]{2,1,0:T(8,128)(2,1)S(1)}, u32[]{:S(2)}, u32[]{:S(2)}) collective-permute-start(bf16[4,16,1536]{2,1,0:T(8,128)(2,1)S(1)} %slice.120), channel_id=1, source_target_pairs={{0,2},{2,4},{4,6},{1,3},{3,5},{5,7},{8,10},{10,12},{12,14},{9,11},... | collective-permute-start | bytes 589832 | tf_op jit(solution)/shard_map/ppermute | solution.py:28
  47.7 25.9 %collective-permute-start.1 = (f32[2,128,768]{2,1,0:T(8,128)}, f32[2,128,768]{2,1,0:T(8,128)S(1)}, u32[]{:S(2)}, u32[]{:S(2)}) collective-permute-start(f32[2,128,768]{2,1,0:T(8,128)} %get-tuple-element.144), channel_id=1, source_target_pairs={{0,2},{1,3},{8,10},{9,11},{16,18},{17,19},{24,26},{25,27}} | collective-permute-start | bytes 2359304 | tf_op jit(solution)/shard_map/ppermute | solution.py:631
  74.6 12.1 %collective-permute-start.2 = (f32[2,128,768]{2,1,0:T(8,128)}, f32[2,128,768]{2,1,0:T(8,128)}, u32[]{:S(2)}, u32[]{:S(2)}) collective-permute-start(f32[2,128,768]{2,1,0:T(8,128)} %multiply_add_fusion.3), channel_id=1, source_target_pairs={{2,4},{3,5},{10,12},{11,13},{18,20},{19,21},{26,28},{27,29}} | collective-permute-start | bytes 2359304 | tf_op jit(solution)/shard_map/ppermute | solution.py:631
  76.2 19.9 %collective-permute-start.7 = (f32[2,128,768]{2,1,0:T(8,128)S(1)}, f32[2,128,768]{2,1,0:T(8,128)S(1)}, u32[]{:S(2)}, u32[]{:S(2)}) collective-permute-start(f32[2,128,768]{2,1,0:T(8,128)S(1)} %copy-done), channel_id=1, source_target_pairs={{0,2},{1,3},{8,10},{9,11},{16,18},{17,19},{24,26},{25,27}} | collective-permute-start | bytes 2359304 | tf_op jit(solution)/shard_map/ppermute | solution.py:631
  108.8 27.4 %collective-permute-start.9 = (f32[2,128,768]{2,1,0:T(8,128)S(1)}, f32[2,128,768]{2,1,0:T(8,128)S(1)}, u32[]{:S(2)}, u32[]{:S(2)}) collective-permute-start(f32[2,128,768]{2,1,0:T(8,128)S(1)} %multiply_add_fusion), channel_id=1, source_target_pairs={{4,6},{5,7},{12,14},{13,15},{20,22},{21,23},{28,30},{29,31}} | collective-permute-start | bytes 2359304 | tf_op jit(solution)/shard_map/ppermute | solution.py:631
  130.8 25.0 %collective-permute-start.4 = (bf16[256,768]{1,0:T(8,128)(2,1)}, bf16[256,768]{1,0:T(8,128)(2,1)S(1)}, u32[]{:S(2)}, u32[]{:S(2)}) collective-permute-start(bf16[256,768]{1,0:T(8,128)(2,1)} %get-tuple-element.154), channel_id=1, source_target_pairs={{0,8},{8,0},{16,24},{24,16},{1,9},{9,1},{17,25},{25,17},{2,10},{10... | collective-permute-start | bytes 1179656 | tf_op jit(solution)/shard_map/ppermute | solution.py:835
  132.5 23.4 %collective-permute-start.5 = (bf16[256,768]{1,0:T(8,128)(2,1)}, bf16[256,768]{1,0:T(8,128)(2,1)S(1)}, u32[]{:S(2)}, u32[]{:S(2)}) collective-permute-start(bf16[256,768]{1,0:T(8,128)(2,1)} %get-tuple-element.155), channel_id=1, source_target_pairs={{0,16},{8,24},{16,0},{24,8},{1,17},{9,25},{17,1},{25,9},{2,18},{10... | collective-permute-start | bytes 1179656 | tf_op jit(solution)/shard_map/ppermute | solution.py:835
  132.9 23.0 %collective-permute-start.6 = (bf16[256,768]{1,0:T(8,128)(2,1)}, bf16[256,768]{1,0:T(8,128)(2,1)S(1)}, u32[]{:S(2)}, u32[]{:S(2)}) collective-permute-start(bf16[256,768]{1,0:T(8,128)(2,1)} %get-tuple-element.156), channel_id=1, source_target_pairs={{0,24},{8,16},{16,8},{24,0},{1,25},{9,17},{17,9},{25,1},{2,26},{10... | collective-permute-start | bytes 1179656 | tf_op jit(solution)/shard_map/ppermute | solution.py:835
  135.6 32.5 %collective-permute-start.13 = (bf16[2,128,768]{2,1,0:T(8,128)(2,1)S(1)}, bf16[2,128,768]{2,1,0:T(8,128)(2,1)S(1)}, u32[]{:S(2)}, u32[]{:S(2)}) collective-permute-start(bf16[2,128,768]{2,1,0:T(8,128)(2,1)S(1)} %fusion.2), channel_id=1, source_target_pairs={{6,4},{7,5},{14,12},{15,13},{22,20},{23,21},{30,28},{31,29}} | collective-permute-start | bytes 1179656 | tf_op jit(solution)/shard_map/ppermute | solution.py:631
  168.2 15.0 %collective-permute-start.14 = (bf16[2,128,768]{2,1,0:T(8,128)(2,1)S(1)}, bf16[2,128,768]{2,1,0:T(8,128)(2,1)S(1)}, u32[]{:S(2)}, u32[]{:S(2)}) collective-permute-start(bf16[2,128,768]{2,1,0:T(8,128)(2,1)S(1)} %add_convert_fusion.3), channel_id=1, source_target_pairs={{4,2},{5,3},{12,10},{13,11},{20,18},{21,19},{28,26},{29,27}} | collective-permute-start | bytes 1179656 | tf_op jit(solution)/shard_map/ppermute | solution.py:631
  179.7 204.2 %reduce-scatter.7.cloned.1.call-start = ((), (), s32[]{:S(2)}) async-start(), calls=%async_computation.7 | async-start | bytes 2654208 | tf_op jit(solution)/shard_map/reduce_scatter | solution.py:890
  181.1 14.3 %collective-permute-start.11 = (bf16[256,768]{1,0:T(8,128)(2,1)}, bf16[256,768]{1,0:T(8,128)(2,1)S(1)}, u32[]{:S(2)}, u32[]{:S(2)}) collective-permute-start(bf16[256,768]{1,0:T(8,128)(2,1)} %get-tuple-element.177), channel_id=1, source_target_pairs={{0,16},{8,24},{16,0},{24,8},{1,17},{9,25},{17,1},{25,9},{2,18},{10... | collective-permute-start | bytes 1179656 | tf_op jit(solution)/shard_map/ppermute | solution.py:835
  181.8 13.6 %collective-permute-start.12 = (bf16[256,768]{1,0:T(8,128)(2,1)S(1)}, bf16[256,768]{1,0:T(8,128)(2,1)S(1)}, u32[]{:S(2)}, u32[]{:S(2)}) collective-permute-start(bf16[256,768]{1,0:T(8,128)(2,1)S(1)} %copy-done.43), channel_id=1, source_target_pairs={{0,24},{8,16},{16,8},{24,0},{1,25},{9,17},{17,9},{25,1},{2,26},{10... | collective-permute-start | bytes 1179656 | tf_op jit(solution)/shard_map/ppermute | solution.py:835
  183.4 24.4 %collective-permute-start.15 = (bf16[2,128,768]{2,1,0:T(8,128)(2,1)S(1)}, bf16[2,128,768]{2,1,0:T(8,128)(2,1)S(1)}, u32[]{:S(2)}, u32[]{:S(2)}) collective-permute-start(bf16[2,128,768]{2,1,0:T(8,128)(2,1)S(1)} %add_convert_fusion.2), channel_id=1, source_target_pairs={{2,0},{3,1},{10,8},{11,9},{18,16},{19,17},{26,24},{27,25}} | collective-permute-start | bytes 1179656 | tf_op jit(solution)/shard_map/ppermute | solution.py:631
  253.2 130.7 %all-gather.10.cloned.1.call-start = ((), (), s32[]{:S(2)}) async-start(), calls=%async_computation.4 | async-start | bytes 7864320 | tf_op jit(solution)/shard_map/all_gather | solution.py:916
  253.9 198.9 %reduce-scatter.11.cloned.1.call-start = ((), (), s32[]{:S(2)}) async-start(), calls=%async_computation.9 | async-start | bytes 1769472 | tf_op jit(solution)/shard_map/reduce_scatter | solution.py:890
  256.3 43.7 %collective-permute-start.16 = (f32[2,3,1024]{2,1,0:T(4,128)S(1)}, f32[2,3,1024]{2,1,0:T(4,128)S(1)}, u32[]{:S(2)}, u32[]{:S(2)}) collective-permute-start(f32[2,3,1024]{2,1,0:T(4,128)S(1)} %slice.128), channel_id=1, source_target_pairs={{2,0},{4,2},{6,4},{3,1},{5,3},{7,5},{10,8},{12,10},{14,12},{11,9},... | collective-permute-start | bytes 73736 | tf_op jit(solution)/shard_map/ppermute | solution.py:28
  257.7 59.4 %collective-permute-start.22 = (bf16[2,128,768]{2,1,0:T(8,128)(2,1)S(1)}, bf16[2,128,768]{2,1,0:T(8,128)(2,1)}, u32[]{:S(2)}, u32[]{:S(2)}) collective-permute-start(bf16[2,128,768]{2,1,0:T(8,128)(2,1)S(1)} %add_convert_fusion), channel_id=1, source_target_pairs={{2,0},{3,1},{10,8},{11,9},{18,16},{19,17},{26,24},{27,25}} | collective-permute-start | bytes 1179656 | tf_op jit(solution)/shard_map/ppermute | solution.py:631
  313.7 34.5 %collective-permute-start.17 = (bf16[256,1536]{1,0:T(8,128)(2,1)}, bf16[256,1536]{1,0:T(8,128)(2,1)S(1)}, u32[]{:S(2)}, u32[]{:S(2)}) collective-permute-start(bf16[256,1536]{1,0:T(8,128)(2,1)} %get-tuple-element.209), channel_id=1, source_target_pairs={{0,8},{8,0},{16,24},{24,16},{1,9},{9,1},{17,25},{25,17},{2,10},{10... | collective-permute-start | bytes 2359304 | tf_op jit(solution)/shard_map/ppermute | solution.py:835
  313.7 34.5 %collective-permute-start.18 = (bf16[256,1536]{1,0:T(8,128)(2,1)}, bf16[256,1536]{1,0:T(8,128)(2,1)S(1)}, u32[]{:S(2)}, u32[]{:S(2)}) collective-permute-start(bf16[256,1536]{1,0:T(8,128)(2,1)} %get-tuple-element.210), channel_id=1, source_target_pairs={{0,16},{8,24},{16,0},{24,8},{1,17},{9,25},{17,1},{25,9},{2,18},{10... | collective-permute-start | bytes 2359304 | tf_op jit(solution)/shard_map/ppermute | solution.py:835
  313.8 45.3 %collective-permute-start.19 = (bf16[256,1536]{1,0:T(8,128)(2,1)}, bf16[256,1536]{1,0:T(8,128)(2,1)S(1)}, u32[]{:S(2)}, u32[]{:S(2)}) collective-permute-start(bf16[256,1536]{1,0:T(8,128)(2,1)} %get-tuple-element.211), channel_id=1, source_target_pairs={{0,24},{8,16},{16,8},{24,0},{1,25},{9,17},{17,9},{25,1},{2,26},{10... | collective-permute-start | bytes 2359304 | tf_op jit(solution)/shard_map/ppermute | solution.py:835
  342.8 21.9 %collective-permute-start.23 = (f32[2,3,1024]{2,1,0:T(4,128)S(1)}, f32[2,3,1024]{2,1,0:T(4,128)S(1)}, u32[]{:S(2)}, u32[]{:S(2)}) collective-permute-start(f32[2,3,1024]{2,1,0:T(4,128)S(1)} %slice.135), channel_id=1, source_target_pairs={{2,0},{4,2},{6,4},{3,1},{5,3},{7,5},{10,8},{12,10},{14,12},{11,9},... | collective-permute-start | bytes 73736 | tf_op jit(solution)/shard_map/ppermute | solution.py:28
  381.4 102.5 %reduce-scatter.9.cloned.1.call-start = ((), (), s32[]{:S(2)}) async-start(), calls=%async_computation.8 | async-start | bytes 3096576 | tf_op jit(solution)/shard_map/reduce_scatter | solution.py:890
  382.2 106.3 %all-gather.12.cloned.1.call-start = ((), (), s32[]{:S(2)}) async-start(), calls=%async_computation.6 | async-start | bytes 3932160 | tf_op jit(solution)/shard_map/all_gather | solution.py:935
  396.7 46.8 %collective-permute-start.24 = (bf16[256,1536]{1,0:T(8,128)(2,1)}, bf16[256,1536]{1,0:T(8,128)(2,1)S(1)}, u32[]{:S(2)}, u32[]{:S(2)}) collective-permute-start(bf16[256,1536]{1,0:T(8,128)(2,1)} %get-tuple-element.238), channel_id=1, source_target_pairs={{0,8},{8,0},{16,24},{24,16},{1,9},{9,1},{17,25},{25,17},{2,10},{10... | collective-permute-start | bytes 2359304 | tf_op jit(solution)/shard_map/ppermute | solution.py:835
  398.4 45.1 %collective-permute-start.25 = (bf16[256,1536]{1,0:T(8,128)(2,1)}, bf16[256,1536]{1,0:T(8,128)(2,1)S(1)}, u32[]{:S(2)}, u32[]{:S(2)}) collective-permute-start(bf16[256,1536]{1,0:T(8,128)(2,1)} %get-tuple-element.239), channel_id=1, source_target_pairs={{0,16},{8,24},{16,0},{24,8},{1,17},{9,25},{17,1},{25,9},{2,18},{10... | collective-permute-start | bytes 2359304 | tf_op jit(solution)/shard_map/ppermute | solution.py:835
  400.1 43.4 %collective-permute-start.26 = (bf16[256,1536]{1,0:T(8,128)(2,1)}, bf16[256,1536]{1,0:T(8,128)(2,1)}, u32[]{:S(2)}, u32[]{:S(2)}) collective-permute-start(bf16[256,1536]{1,0:T(8,128)(2,1)} %get-tuple-element.240), channel_id=1, source_target_pairs={{0,24},{8,16},{16,8},{24,0},{1,25},{9,17},{17,9},{25,1},{2,26},{10... | collective-permute-start | bytes 2359304 | tf_op jit(solution)/shard_map/ppermute | solution.py:835
  449.3 39.1 %collective-permute-start.27 = (bf16[256,1536]{1,0:T(8,128)(2,1)}, bf16[256,1536]{1,0:T(8,128)(2,1)S(1)}, u32[]{:S(2)}, u32[]{:S(2)}) collective-permute-start(bf16[256,1536]{1,0:T(8,128)(2,1)} %input_norm.3.refs_0_), channel_id=1, source_target_pairs={{0,8},{8,0},{16,24},{24,16},{1,9},{9,1},{17,25},{25,17},{2,10},{10... | collective-permute-start | bytes 2359304 | tf_op jit(solution)/shard_map/ppermute | solution.py:830
  449.3 39.1 %collective-permute-start.28 = (bf16[256,1536]{1,0:T(8,128)(2,1)}, bf16[256,1536]{1,0:T(8,128)(2,1)S(1)}, u32[]{:S(2)}, u32[]{:S(2)}) collective-permute-start(bf16[256,1536]{1,0:T(8,128)(2,1)} %input_norm.3.refs_0_), channel_id=1, source_target_pairs={{0,16},{8,24},{16,0},{24,8},{1,17},{9,25},{17,1},{25,9},{2,18},{10... | collective-permute-start | bytes 2359304 | tf_op jit(solution)/shard_map/ppermute | solution.py:830
  451.4 37.0 %collective-permute-start.29 = (bf16[256,1536]{1,0:T(8,128)(2,1)}, bf16[256,1536]{1,0:T(8,128)(2,1)}, u32[]{:S(2)}, u32[]{:S(2)}) collective-permute-start(bf16[256,1536]{1,0:T(8,128)(2,1)} %input_norm.3.refs_0_), channel_id=1, source_target_pairs={{0,24},{8,16},{16,8},{24,0},{1,25},{9,17},{17,9},{25,1},{2,26},{10... | collective-permute-start | bytes 2359304 | tf_op jit(solution)/shard_map/ppermute | solution.py:830
  (54 other events, 452.5 us)
Sparse Core Ops, SparseCore 0:
  10.7 99.0 all-gather.13
  255.9 105.1 all-gather.9
  384.9 56.7 all-gather.11
Sparse Core Ops, SparseCore 1:
  179.7 54.8 reduce-scatter.4
  253.3 44.3 reduce-scatter.6
  381.5 34.7 reduce-scatter.10
  419.1 36.2 reduce-scatter.8

commit v2 on v1

--- a/solution.py
+++ b/solution.py
@@ -465,6 +465,14 @@
             out_ref[s] = acc_ref[s * share : (s + 1) * share].astype(LOW)
 
 
+def hand_kernel(local_ref, through_ref, arrived_ref, out_ref):
+    out_ref[0] = local_ref[0] + through_ref[0, :1] * arrived_ref[0]
+
+
+def place_kernel(block_ref, out_ref):
+    out_ref[...] = block_ref[...]
+
+
 def merged(ref):
     return ref[...].reshape(ref.shape[0] * ref.shape[1], ref.shape[2])
 
@@ -482,8 +490,8 @@
 
 
 def out_grad_kernel(*refs):
-    top, normed, out_ref = refs[:STREAMS], refs[STREAMS : 2 * STREAMS], refs[-1]
-    out_ref[...] = sum(mm_tn(merged(a), merged(b)) for a, b in zip(top, normed)).astype(LOW)
+    normed, top, out_ref = refs[:STREAMS], refs[STREAMS : 2 * STREAMS], refs[-1]
+    out_ref[...] = sum(mm_tn(merged(a), merged(b)) for a, b in zip(normed, top)).astype(LOW)
 
 
 def late_kernel(width, state, *refs):
@@ -533,6 +541,13 @@
     scaled = grad * gain_ref[...]
     out = top_ref[0].astype(F32) + scale * (scaled - normed * jnp.mean(scaled * normed, axis=1, keepdims=True))
     out_ref[...] = out.astype(LOW)
+
+
+def ignoring(kernel, first, count):
+    def body(*refs):
+        kernel(*refs[:first], *refs[first + count :])
+
+    return body
 
 
 def per_device(
@@ -586,22 +601,21 @@
     halo = shifted(residual_in[:, rows - HALO :, :], "seq", 1)
     full_w = lax.all_gather(out_projection_weight, "tensor", axis=0)
     smem = pl.BlockSpec(memory_space=pltpu.SMEM)
+    anywhere = pl.BlockSpec(memory_space=pl.ANY)
 
     def cost(flops):
         return pl.CostEstimate(flops=int(flops), bytes_accessed=30 << 20, transcendentals=0)
 
-    def after(value, *others):
-        return lax.optimization_barrier((value,) + others)[0]
-
-    def project(s, halo):
-        return pl.pallas_call(
-            functools.partial(project_kernel, *dims),
+    def project(s, halo, marks=()):
+        return pl.pallas_call(
+            ignoring(functools.partial(project_kernel, *dims), 8, len(marks)),
             grid=(seqs,),
             in_specs=[
                 per_seq(rows, model, offset=s * seqs), per_seq(HALO, model, offset=s * seqs), whole((1, model)),
                 whole((model, 2 * width)), whole((model, side_width)), whole((8, mixed_width)), whole((8, LANES)),
                 whole((LANES, width)),
-            ],
+            ]
+            + [anywhere] * len(marks),
             out_specs=[
                 per_seq(rows, model), per_seq(rows, mixed_width), per_seq(HALO, mixed_width),
                 per_seq(rows, mixed_width), per_seq(rows, width), per_seq(rows, LANES), per_seq(rows, width),
@@ -621,51 +635,68 @@
             compiler_params=params(),
             cost_estimate=cost(8e9 * seqs),
             name="project",
-        )(residual_in, halo, in_gain, main_w, side_w, taps, terms, hot)
-
-    def chained(local, through, direction, kind, marks):
+        )(residual_in, halo, in_gain, main_w, side_w, taps, terms, hot, *marks)
+
+    def handed(local, through, arrived, marks):
+        return pl.pallas_call(
+            ignoring(hand_kernel, 3, len(marks)),
+            grid=(seqs,),
+            in_specs=[per_seq(state, width), per_seq(8, width), per_seq(state, width)] + [anywhere] * len(marks),
+            out_specs=per_seq(state, width),
+            out_shape=sds((seqs, state, width), F32),
+            compiler_params=params(),
+            name="handed",
+        )(local, through, arrived, *marks)
+
+    def chained(local, through, direction, kind, marks=None):
         arrivals = []
         for hop in range(spans - 1):
             sender = hop if direction > 0 else spans - 1 - hop
-            sent = local if hop == 0 else local + through[:, :1] * arrivals[-1].astype(F32)
-            arrived = lax.ppermute(sent.astype(kind), "seq", [(sender, sender + direction)])
-            arrivals.append(after(arrived, marks[min(hop, len(marks) - 1)]))
+            if hop == 0:
+                sent = local
+            elif marks:
+                sent = handed(local, through, arrivals[-1], marks[min(hop, len(marks)) - 1])
+            else:
+                sent = local + through[:, :1] * arrivals[-1].astype(F32)
+            arrivals.append(lax.ppermute(sent.astype(kind), "seq", [(sender, sender + direction)]))
         return arrivals
 
-    def top_of(s, place):
-        return pl.pallas_call(
-            functools.partial(top_kernel, rows, s * seqs),
+    def top_of(s, place, marks=()):
+        return pl.pallas_call(
+            ignoring(functools.partial(top_kernel, rows, s * seqs), 4, len(marks)),
             grid=(seqs,),
-            in_specs=[smem, smem, per_seq(rows, model, offset=s * seqs), whole((width, model))],
+            in_specs=[smem, smem, per_seq(rows, model, offset=s * seqs), whole((width, model))]
+            + [anywhere] * len(marks),
             out_specs=[per_seq(rows, model), per_seq(rows, width)],
             out_shape=[sds((seqs, rows, model), LOW), sds((seqs, rows, width), F32)],
             compiler_params=params(),
             cost_estimate=cost(2.5e9 * seqs),
             name="top",
-        )(lengths, place, cotangent, out_projection_weight)
-
-    def gated_of(y_local, pre, gate, packed, arrivals, states, back):
-        return pl.pallas_call(
-            functools.partial(gate_kernel, *dims),
+        )(lengths, place, cotangent, out_projection_weight, *marks)
+
+    def gated_of(y_local, pre, gate, packed, arrivals, states, back, marks=()):
+        return pl.pallas_call(
+            ignoring(functools.partial(gate_kernel, *dims), 9 + len(arrivals), len(marks)),
             grid=(seqs,),
             in_specs=[
                 per_seq(rows, width), per_seq(rows, mixed_width), per_seq(rows, width), per_seq(rows, LANES),
                 per_seq(blocks, state, width), per_seq(rows, width), whole((1, width)),
                 whole((1, width)), whole((LANES, width)),
             ]
-            + [per_seq(state, width)] * len(arrivals),
+            + [per_seq(state, width)] * len(arrivals)
+            + [anywhere] * len(marks),
             out_specs=[per_seq(rows, width), per_seq(state, width), per_seq(8, rows)],
             out_shape=[sds((seqs, rows, width), F32), sds((seqs, state, width), F32), sds((seqs, 8, rows), F32)],
             compiler_params=params(),
             cost_estimate=cost(4e9 * seqs),
             name="gated",
-        )(y_local, pre, gate, packed, states, back, out_gain, skip, hot, *arrivals)
-
-    def outward(y, pre, gate, packed, back, all_stats):
+        )(y_local, pre, gate, packed, states, back, out_gain, skip, hot, *arrivals, *marks)
+
+    def outward(y, pre, gate, packed, back, all_stats, marks=()):
         seq = lambda *shape: pl.BlockSpec((1,) + shape, lambda i, r: (i,) + (0,) * len(shape))
         fixed = lambda *shape: pl.BlockSpec(shape, lambda i, r: (0,) * len(shape))
         return pl.pallas_call(
-            functools.partial(out_kernel, *dims, inner_total),
+            ignoring(functools.partial(out_kernel, *dims, inner_total), 10, len(marks)),
             grid_spec=pltpu.PrefetchScalarGridSpec(
                 num_scalar_prefetch=1,
                 grid=(seqs,),
@@ -673,7 +704,8 @@
                     seq(rows, width), seq(rows, mixed_width), seq(rows, width), seq(rows, LANES), seq(rows, width),
                     pl.BlockSpec((ranks, 1, 8, rows), lambda i, r: (0, i, 0, 0)), fixed(1, width), fixed(1, width),
                     fixed(LANES, width),
-                ],
+                ]
+                + [anywhere] * len(marks),
                 out_specs=[
                     seq(rows, width), seq(rows, width), seq(rows, width), seq(blocks, state, width), fixed(16, width),
                 ]
@@ -687,11 +719,11 @@
             compiler_params=params(),
             cost_estimate=cost(5e9 * seqs),
             name="outward",
-        )(rank, y, pre, gate, packed, back, all_stats, out_gain, skip, hot)
-
-    def backward(y, pre, mixed, edge, packed, stepped, grad_y, entering, states, leaving, adjoint):
-        return pl.pallas_call(
-            functools.partial(back_kernel, *dims),
+        )(rank, y, pre, gate, packed, back, all_stats, out_gain, skip, hot, *marks)
+
+    def backward(marks, y, pre, mixed, edge, packed, stepped, grad_y, entering, states, leaving, adjoint):
+        return pl.pallas_call(
+            ignoring(functools.partial(back_kernel, *dims), 15 + len(leaving), len(marks)),
             grid=(seqs,),
             in_specs=[
                 per_seq(rows, width), per_seq(rows, mixed_width), per_seq(rows, mixed_width),
@@ -700,7 +732,8 @@
                 per_seq(blocks, state, width), whole((8, mixed_width)), whole((8, LANES)), whole((1, width)),
                 whole((LANES, width)), whole((width, LANES)),
             ]
-            + [per_seq(state, width)] * len(leaving),
+            + [per_seq(state, width)] * len(leaving)
+            + [anywhere] * len(marks),
             out_specs=[
                 per_seq(rows, kept_width), per_seq(rows, LANES), per_seq(8, mixed_width), per_seq(HALO, mixed_width),
                 pl.BlockSpec((8 * (CONV + 1), mixed_width), lambda i: (0, 0)),
@@ -719,32 +752,33 @@
             name="backward",
         )(
             y, pre, mixed, edge, packed, stepped, grad_y, entering, states, adjoint,
-            taps, terms, skip, hot, hot_t, *leaving,
+            taps, terms, skip, hot, hot_t, *leaving, *marks,
         )
 
-    def lowered_of(grad_gate, grad_mixed, grad_step):
+    def lowered_of(grad_gate, grad_mixed, grad_step, marks=()):
         seq = lambda *shape: pl.BlockSpec((1,) + shape, lambda i, r: (i,) + (0,) * len(shape))
         fixed = lambda *shape: pl.BlockSpec(shape, lambda i, r: (0,) * len(shape), pipeline_mode=pl.Buffered(1))
         return pl.pallas_call(
-            functools.partial(lowered_kernel, width, state),
+            ignoring(functools.partial(lowered_kernel, width, state), 6, len(marks)),
             grid_spec=pltpu.PrefetchScalarGridSpec(
                 num_scalar_prefetch=1,
                 grid=(seqs,),
                 in_specs=[
                     seq(rows, width), seq(rows, kept_width), seq(rows, LANES), fixed(model, 2 * width),
                     fixed(model, side_width),
-                ],
+                ]
+                + [anywhere] * len(marks),
                 out_specs=[pl.BlockSpec((share, model), lambda i, r: (0, 0))] * ranks,
             ),
             out_shape=[sds((share, model), LOW)] * ranks,
             compiler_params=params(),
             cost_estimate=cost(4.5e9 * seqs),
             name="lowered",
-        )(rank, grad_gate, grad_mixed, grad_step, main_w, side_w)
-
-    def input_norm(s, parts, top):
-        return pl.pallas_call(
-            functools.partial(norm_kernel, ranks),
+        )(rank, grad_gate, grad_mixed, grad_step, main_w, side_w, *marks)
+
+    def input_norm(s, parts, top, marks=()):
+        return pl.pallas_call(
+            ignoring(functools.partial(norm_kernel, ranks), 4 + len(parts), len(marks)),
             grid_spec=pltpu.PrefetchScalarGridSpec(
                 num_scalar_prefetch=1,
                 grid=(1,),
@@ -753,25 +787,27 @@
                     pl.BlockSpec((1, share, model), lambda i, r: (r[0], 0, 0)),
                     pl.BlockSpec((1, model), lambda i, r: (0, 0)),
                 ]
-                + [pl.BlockSpec((share, model), lambda i, r: (0, 0))] * ranks,
+                + [pl.BlockSpec((share, model), lambda i, r: (0, 0))] * ranks
+                + [anywhere] * len(marks),
                 out_specs=pl.BlockSpec((share, model), lambda i, r: (0, 0)),
             ),
             out_shape=sds((share, model), LOW),
             compiler_params=params(),
             name="input_norm",
-        )(rank, residual_in.reshape(-1, share, model), top.reshape(-1, share, model), in_gain, *parts)
-
-    def product(parts):
+        )(rank, residual_in.reshape(-1, share, model), top.reshape(-1, share, model), in_gain, *parts, *marks)
+
+    def product(parts, marks=()):
         row_of = lambda s: pl.BlockSpec((1, share, model), lambda i, r: (s * ranks + r[0], 0, 0))
         x = residual_in.reshape(-1, share, model)
         return pl.pallas_call(
-            functools.partial(product_kernel, ranks),
+            ignoring(functools.partial(product_kernel, ranks), 2 + STREAMS + len(parts), len(marks)),
             grid_spec=pltpu.PrefetchScalarGridSpec(
                 num_scalar_prefetch=1,
                 grid=(ranks,),
                 in_specs=[row_of(s) for s in range(STREAMS)]
                 + [pl.BlockSpec((1, width, model), lambda i, r: (r[0] ^ i, 0, 0))]
-                + [pl.BlockSpec((share, width), lambda i, r: (0, 0))] * (STREAMS * ranks),
+                + [pl.BlockSpec((share, width), lambda i, r: (0, 0))] * (STREAMS * ranks)
+                + [anywhere] * len(marks),
                 out_specs=pl.BlockSpec((STREAMS, share, model), lambda i, r: (0, 0, 0)),
                 scratch_shapes=[pltpu.VMEM((STREAMS * share, model), F32)],
             ),
@@ -779,51 +815,53 @@
             compiler_params=params(),
             cost_estimate=cost(2.4e9 * all_seqs),
             name="product",
-        )(rank, *[x] * STREAMS, full_w, *parts)
+        )(rank, *[x] * STREAMS, full_w, *parts, *marks)
 
     tile = 256
     tiles = model // tile
     column = pl.BlockSpec((seqs, rows, tile), lambda i: (0, 0, i))
     row = lambda n: pl.BlockSpec((tile, n), lambda i: (i, 0))
 
-    def gate_grad(low, grads):
-        return pl.pallas_call(
-            gate_grad_kernel,
+    def gate_grad(low, grads, marks=()):
+        return pl.pallas_call(
+            ignoring(gate_grad_kernel, 2 * STREAMS + 1, len(marks)),
             grid=(tiles,),
-            in_specs=[column] * STREAMS + [whole((seqs, rows, width))] * STREAMS + [row(width)],
+            in_specs=[column] * STREAMS + [whole((seqs, rows, width))] * STREAMS + [row(width)]
+            + [anywhere] * len(marks),
             out_specs=[row(width), row(LANES)],
             out_shape=[sds((model, width), LOW), sds((model, LANES), F32)],
             compiler_params=params(),
             cost_estimate=cost(2.5e9 * all_seqs),
             name="gate_grad",
-        )(*low, *grads, main_w)
-
-    def out_grad(top, normed):
-        return pl.pallas_call(
-            out_grad_kernel,
-            grid=(tiles,),
-            in_specs=[column] * STREAMS + [whole((seqs, rows, width))] * STREAMS,
-            out_specs=row(width),
-            out_shape=sds((model, width), LOW),
+        )(*low, *grads, main_w, *marks)
+
+    def out_grad(normed, top, marks=()):
+        return pl.pallas_call(
+            ignoring(out_grad_kernel, 2 * STREAMS, len(marks)),
+            grid=(width // tile,),
+            in_specs=[column] * STREAMS + [whole((seqs, rows, model))] * STREAMS + [anywhere] * len(marks),
+            out_specs=row(model),
+            out_shape=sds((width, model), LOW),
             compiler_params=params(),
             cost_estimate=cost(2.5e9 * all_seqs),
             name="out_grad",
-        )(*top, *normed)
-
-    def late_of(low, mixed, step, gain):
-        return pl.pallas_call(
-            functools.partial(late_kernel, width, state),
+        )(*normed, *top, *marks)
+
+    def late_of(low, mixed, step, gain, marks=()):
+        return pl.pallas_call(
+            ignoring(functools.partial(late_kernel, width, state), 3 * STREAMS + 3, len(marks)),
             grid=(tiles,),
             in_specs=[column] * STREAMS
             + [whole((seqs, rows, kept_width))] * STREAMS
             + [whole((seqs, rows, LANES))] * STREAMS
-            + [pl.BlockSpec((tile, width), lambda i: (i, 1)), row(side_width), row(LANES)],
+            + [pl.BlockSpec((tile, width), lambda i: (i, 1)), row(side_width), row(LANES)]
+            + [anywhere] * len(marks),
             out_specs=[row(width + LANES), row(2 * state), row(LANES)],
             out_shape=[sds((model, width + LANES), LOW), sds((model, 2 * state), F32), sds((model, LANES), F32)],
             compiler_params=params(),
             cost_estimate=cost(5e9 * all_seqs),
             name="late",
-        )(*low, *mixed, *step, main_w, side_w, gain)
+        )(*low, *mixed, *step, main_w, side_w, gain, *marks)
 
     def exchanged(own):
         return [own] + [
@@ -839,43 +877,53 @@
         blocks_of = whole_rows.reshape(ranks, share, -1)
         return swapped([lax.dynamic_index_in_dim(blocks_of, rank[0] ^ d, axis=0, keepdims=False) for d in range(ranks)])
 
-    def assembled(ready, pieces):
-        held = ready.reshape(-1, share, model)
-        count = held.shape[0]
+    def placed(blocks, total, marks):
+        count = blocks.shape[0]
+        return pl.pallas_call(
+            ignoring(place_kernel, 1, len(marks)),
+            grid=(count // 2,),
+            in_specs=[pl.BlockSpec((2, share, model), lambda i: (i, 0, 0))] + [anywhere] * len(marks),
+            out_specs=pl.BlockSpec((2, share, model), lambda i: (i, 0, 0)),
+            out_shape=sds((total, share, model), LOW),
+            compiler_params=params(),
+            name="placed",
+        )(blocks, *marks)
+
+    def assembled(held, pieces, marks):
+        total = held.shape[0]
 
         def kernel(rank_ref, held_ref, *refs):
             out_ref, sems = refs[ranks:]
-            copies = [pltpu.make_async_copy(held_ref, out_ref.at[pl.ds(0, count)], sems.at[ranks])]
-            for d in range(ranks):
-                copies.append(pltpu.make_async_copy(refs[d], out_ref.at[count + (rank_ref[0] ^ d)], sems.at[d]))
+            copies = [
+                pltpu.make_async_copy(refs[d], out_ref.at[total - ranks + (rank_ref[0] ^ d)], sems.at[d])
+                for d in range(ranks)
+            ]
             for copy in copies:
                 copy.start()
             for copy in copies:
                 copy.wait()
 
         return pl.pallas_call(
-            kernel,
-            in_specs=[smem] + [pl.BlockSpec(memory_space=pltpu.VMEM)] * (1 + ranks),
-            out_specs=pl.BlockSpec(memory_space=pl.ANY),
-            out_shape=sds((count + ranks, share, model), LOW),
-            scratch_shapes=[pltpu.SemaphoreType.DMA((ranks + 1,))],
+            ignoring(kernel, 2 + ranks, len(marks)),
+            in_specs=[smem, anywhere] + [pl.BlockSpec(memory_space=pltpu.VMEM)] * ranks + [anywhere] * len(marks),
+            out_specs=anywhere,
+            out_shape=sds((total, share, model), LOW),
+            input_output_aliases={1: 0},
+            scratch_shapes=[pltpu.SemaphoreType.DMA((ranks,))],
             compiler_params=pltpu.CompilerParams(vmem_limit_bytes=VMEM),
             name="assemble",
-        )(rank, held, *pieces).reshape(residual_in.shape)
+        )(rank, held, *pieces, *marks)
 
     flat = lambda a: a.reshape(seqs * rows, a.shape[-1])
     both = range(STREAMS)
 
-    def gate_on(values, *marks):
-        return list(lax.optimization_barrier(tuple(values) + marks)[: len(values)])
-
-    def backward_of(s, leaving, mark, fill):
+    def backward_of(s, leaving, marks, fill):
         made, step_low, head, tail, filter_sum, term_sum = backward(
-            after(y[s], mark), pre[s], mixed[s], edge[s], packed[s], stepped[s], grad_y[s], entering[s], states[s],
+            marks, y[s], pre[s], mixed[s], edge[s], packed[s], stepped[s], grad_y[s], entering[s], states[s],
             leaving, adjoint[s],
         )
-        raw = step_low
-        following = after(shifted(head[:, :reach], "seq", -1), fill(raw))
+        following = shifted(head[:, :reach], "seq", -1)
+        fill(step_low)
         fix = jnp.zeros((seqs, reach, mixed_width), F32)
         for k in range(reach):
             fix = fix + jnp.pad(taps[k] * following[:, : reach - k], ((0, 0), (k, 0), (0, 0)))
@@ -885,63 +933,61 @@
         made = lax.dynamic_update_slice(
             made, jnp.concatenate([tail_high, tail_least], axis=2), (0, rows - HALO, 0)
         )
-        return made, step_low, filter_sum, term_sum, raw
-
-    reduced = lambda a: lax.psum_scatter(a, ("seq", "dp"), scatter_dimension=0, tiled=True)
+        return made, step_low, filter_sum, term_sum
+
+    reduced = lambda a, axis=0: lax.psum_scatter(a, ("seq", "dp"), scatter_dimension=axis, tiled=True)
 
     first = [project(0, halo)]
-    first.append(project(1, after(halo, first[0][-1])))
+    first.append(project(1, halo, [first[0][-1]]))
     low, mixed, edge, pre, gate, packed, stepped, y_local, states, local, through = zip(*first)
-    tops = [top_of(0, after(place, local[1]))]
-    tops.append(top_of(1, after(place, tops[0][0])))
+    tops = [top_of(0, place, [through[1]])]
+    tops.append(top_of(1, place, [tops[0][0]]))
     top, back = zip(*tops)
 
-    def gated_of_stream(s, arrivals):
-        y, entering, stats = gated_of(y_local[s], pre[s], gate[s], packed[s], arrivals, states[s], back[s])
+    def gated_of_stream(s, arrivals, marks):
+        y, entering, stats = gated_of(y_local[s], pre[s], gate[s], packed[s], arrivals, states[s], back[s], marks)
         return y, entering, stats, lax.all_gather(stats, "tensor", axis=0)
 
     y, entering, stats, all_stats = [None] * 2, [None] * 2, [None] * 2, [None] * 2
     second = []
-    arrivals = chained(local[0], through[0], 1, F32, [local[1], top[0], top[1]])
-    y[0], entering[0], stats[0], all_stats[0] = gated_of_stream(0, arrivals)
+    arrivals = chained(local[0], through[0], 1, F32)
+    y[0], entering[0], stats[0], all_stats[0] = gated_of_stream(0, arrivals, [top[1]])
     second.append(outward(y[0], pre[0], gate[0], packed[0], back[0], all_stats[0]))
-    arrivals = chained(local[1], through[1], 1, F32, [top[1], stats[0], second[0][0]])
-    y[1], entering[1], stats[1], all_stats[1] = gated_of_stream(1, arrivals)
-    parts = gate_on(swapped(second[0][5:]), all_stats[1])
-    second.append(outward(after(y[1], *parts), pre[1], gate[1], packed[1], back[1], all_stats[1]))
+    arrivals = chained(local[1], through[1], 1, F32)
+    y[1], entering[1], stats[1], all_stats[1] = gated_of_stream(1, arrivals, [second[0][0]])
+    parts = swapped(second[0][5:])
+    leaving = [chained(second[0][3][:, 0], through[0], -1, LOW)]
+    second.append(outward(y[1], pre[1], gate[1], packed[1], back[1], all_stats[1], [leaving[0][0]]))
     normed, grad_y, grad_gate, adjoint, out_sums = list(zip(*second))[:5]
-    gate_w, gain_sums = gate_grad(gate_on(low, normed[1]), grad_gate)
+    leaving.append(chained(adjoint[1][:, 0], through[1], -1, LOW))
+    gate_w, gain_sums = gate_grad(low, grad_gate, [normed[1], leaving[0][1]])
     gate_w_sum = reduced(gate_w)
-    made_out = product(parts + gate_on(swapped(second[1][5:]), gate_w))
+    made_out = product(parts + swapped(second[1][5:]), [gate_w, leaving[1][0]])
     block_out = lax.all_gather(made_out, "tensor", axis=1, tiled=True)
-    leaving = chained(adjoint[0][:, 0], through[0], -1, LOW, [stats[1], normed[1], gate_w])
-    early = []
-
-    def out_first(raw):
-        early.append(out_grad(gate_on(top, raw), normed))
-        return early[0]
-
-    third = [backward_of(0, leaving, made_out, out_first)]
-    out_w = reduced(early[0])
-    leaving = chained(adjoint[1][:, 0], through[1], -1, LOW, [gate_w, made_out, third[0][4]])
-    partial = [lowered_of(grad_gate[0], *third[0][:2])]
-    first_own = []
-
-    def norm_first(raw):
-        first_own.append(input_norm(0, gate_on(swapped(partial[0]), raw), top[0]))
-        return first_own[0]
-
-    third.append(backward_of(1, gate_on(leaving, gate_w_sum), partial[0][0], norm_first))
-    first_in = lax.all_gather(first_own[0], "tensor", axis=0, tiled=True)
-    grad_mixed, grad_step, filter_sums, term_sums = list(zip(*third))[:4]
-    grad_own, grad_side, gain_sums = late_of(low, grad_mixed, grad_step, gain_sums)
-    partial.append(lowered_of(after(grad_gate[1], grad_own, block_out, out_w), *third[1][:2]))
-    grad_own_w = reduced(grad_own).astype(F32)
+    out_w = []
+    third = [
+        backward_of(0, leaving[0], [made_out, leaving[1][1]], lambda raw: out_w.append(out_grad(normed, top, [raw])))
+    ]
+    out_w_sum = reduced(out_w[0], 1)
+    partial = [lowered_of(grad_gate[0], *third[0][:2], [out_w[0]])]
+    sums = [swapped(partial[0])]
+    own = []
+    third.append(
+        backward_of(
+            1, leaving[1], [partial[0][0], block_out], lambda raw: own.append(input_norm(0, sums[0], top[0], [raw]))
+        )
+    )
+    first_in = lax.all_gather(own[0], "tensor", axis=0, tiled=True)
+    grad_mixed, grad_step, filter_sums, term_sums = zip(*third)
+    grad_own, grad_side, gain_sums = late_of(low, grad_mixed, grad_step, gain_sums, [own[0]])
+    partial.append(lowered_of(grad_gate[1], *third[1][:2], [grad_own, gate_w_sum]))
+    sums.append(swapped(partial[1]))
+    own_sum = reduced(grad_own)
+    grad_own_w = own_sum.astype(F32)
     shared_w = reduced(grad_side)
     grad_gate_w = gate_w_sum.astype(F32)
-    grad_out_w = out_w.astype(F32).T
+    grad_out_w = out_w_sum.astype(F32)
     grad_main_w = jnp.stack([grad_gate_w, grad_own_w[:, :width]], axis=1)
-    grad_shared_w = jnp.sum(lax.all_gather(shared_w, "tensor", axis=0), axis=0)
     grad_step_w = grad_own_w[:, width : width + heads]
     filters = jnp.sum(sum(filter_sums).reshape(CONV + 1, 8, mixed_width), axis=1)
     term_rows = jnp.sum(sum(term_sums).reshape(2, 8, LANES), axis=1)
@@ -959,11 +1005,23 @@
     small_main = rank_sums[: (CONV + 1) * width].reshape(CONV + 1, width)
     small_terms = rank_sums[(CONV + 1) * width : -width].reshape(3, LANES)[:, :heads]
     small_out = rank_sums[-width:]
-    own = input_norm(1, gate_on(swapped(partial[1]), shared_sums), top[1])
-    pieces = exchanged(own)
+    last_own = input_norm(1, sums[1], top[1], [shared_sums, first_in])
+    pieces = exchanged(last_own)
+    stacked = STREAMS * ranks
+    block_out = placed(block_out.reshape(stacked, share, model), stacked, [last_own])
+    input_grad = placed(first_in.reshape(-1, share, model), stacked, [last_own, block_out])
+    shared_w = pl.pallas_call(
+        ignoring(place_kernel, 1, 2),
+        in_specs=[pl.BlockSpec(memory_space=pltpu.VMEM), anywhere, anywhere],
+        out_specs=pl.BlockSpec(memory_space=pltpu.VMEM),
+        out_shape=sds(shared_w.shape, F32),
+        name="settled",
+    )(shared_w, input_grad, own_sum)
+    grad_shared_w = jnp.sum(lax.all_gather(shared_w, "tensor", axis=0), axis=0)
+    input_grad = assembled(input_grad, pieces, [block_out])
     return (
         block_out.reshape(residual_in.shape),
-        assembled(first_in, gate_on(pieces, grad_out_w)),
+        input_grad.reshape(residual_in.shape),
         small_in,
         grad_main_w,
         grad_shared_w,

time: 517 us -> 480 us (0.928)
  waiting for transfers between devices: 80.8 us -> 38.7 us
  Pallas kernels: 236 us -> 246 us
  blocking collectives: 86.9 us -> 78.4 us
    ppermute x3, waiting for transfers between devices: 41 us -> 8.34 us  [shifted(): return lax.ppermute(block, axis, route)]
    ppermute x12, waiting for transfers between devices: 24.9 us -> 8.97 us  [swapped(): lax.ppermute(b, 'tensor', [(i, i ^ d) for i in range(ranks)])]
    pallas_call x19 -> x22, Pallas kernels: 236 us -> 246 us  [the longest x2 50.6 us: backward(): pl.pallas_call(ignoring(functools.partial(back_kernel, *dims), 15 + len(l...]
    ppermute x12, waiting for transfers between devices: 12 us -> 20 us  [chained(): lax.ppermute(sent.astype(kind), 'seq', [(sender, sender + direction)])]
    all_gather x1, blocking collectives: 29.4 us -> 23.1 us  [per_device(): grad_shared_w = jnp.sum(lax.all_gather(shared_w, 'tensor', axis=0), axis=0)]
    unnamed x109 -> x113, local copies, waits for them, and re-layouts: 20.7 us -> 22.8 us
  transfers between devices with their start and end apart: 37 -> 37, of which waited for: 7 -> 6; matrix products, arithmetic and copies ran while one was open for 6% -> 9% of each run, Pallas kernels for 45% -> 49%
where the time goes in v2:
time: 480 us; the launch traced here: 472 us
  Pallas kernels  246 us (51%)
  blocking collectives  78.4 us (16%)
  starting transfers between devices  42.1 us (9%)
  waiting for transfers between devices  38.7 us (8%)
  local copies, waits for them, and re-layouts  35.1 us (7%)
  between operations  16.7 us (3%)
  other arithmetic  15.1 us (3%)
    pallas_call x2, Pallas kernels, backward(): pl.pallas_call(ignoring(functools.partial(back_kernel, *dims), 15 + len(l...  50.6 us
    pallas_call x2, Pallas kernels, project(): pl.pallas_call(ignoring(functools.partial(project_kernel, *dims), 8, len(...  43.8 us
    pallas_call x2, Pallas kernels, lowered_of(): pl.pallas_call(ignoring(functools.partial(lowered_kernel, width, state),...  25.2 us
    pallas_call x2, Pallas kernels, outward(): pl.pallas_call(ignoring(functools.partial(out_kernel, *dims, inner_total)...  23.5 us
    all_gather x1, blocking collectives, per_device(): grad_shared_w = jnp.sum(lax.all_gather(shared_w, 'tensor', axis=0), axis=0)  23.1 us
    unnamed x113, local copies, waits for them, and re-layouts  22.8 us
    all_gather x1, blocking collectives, per_device(): lax.all_gather(packed_sums[:split], 'tensor', axis=0)  20.4 us
    ppermute x12, waiting for transfers between devices, chained(): lax.ppermute(sent.astype(kind), 'seq', [(sender, sender + direction)])  20 us
  transfers between devices with their start and end apart: 37, of which 6 were waited for; matrix products, arithmetic and copies ran while one was open for 9% of the time, Pallas kernels for 49%

profile of v2, /device:TPU:0, one launch (start us, length us, event | category | flops | bytes accessed | tf_op | source)
XLA Modules:
  0.0 471.7 jit_solution(9592524524949077454)
XLA Ops:
  9.7 4.9 %collective-permute-start = (bf16[4,16,1536]{2,1,0:T(8,128)(2,1)S(1)}, bf16[4,16,1536]{2,1,0:T(8,128)(2,1)S(1)}, u32[]{:S(2)}, u32[]{:S(2)}) collective-permute-start(bf16[4,16,1536]{2,1,0:T(8,128)(2,1)S(1)} %slice.120), channel_id=1, source_target_pairs={{0,2},{2,4},{4,6},{1,3},{3,5},{5,7},{8,10},{10,12},{12,14},{9,11},... | collective-permute-start | bytes 589832 | tf_op jit(solution)/shard_map/ppermute | solution.py:28
  14.8 5.5 %copy.46 = bf16[192,8,2,768]{3,1,2,0:T(8,128)(2,1)} copy(bf16[192,8,2,768]{3,2,1,0:T(2,128)(2,1)} %bitcast.78) | data formatting | bytes 9437184
  25.1 21.8 %project.2 = (bf16[2,512,1536]{2,1,0:T(8,128)(2,1)}, bf16[2,512,1024]{2,1,0:T(8,128)(2,1)}, bf16[2,16,1024]{2,1,0:T(8,128)(2,1)}, f32[2,512,1024]{2,1,0:T(8,128)...) custom-call(bf16[4,512,1536]{2,1,0:T(8,128)(2,1)} %refs_0_.5, ...), custom_call_target="tpu_custom_call" | custom-call | flops 16000000000 | bytes 31457280 | tf_op jit(solution)/shard_map/project/pallas_call | solution.py:610
  47.7 3.9 collective-permute-start.1
  51.7 22.0 %project.3 = (bf16[2,512,1536]{2,1,0:T(8,128)(2,1)}, bf16[2,512,1024]{2,1,0:T(8,128)(2,1)}, bf16[2,16,1024]{2,1,0:T(8,128)(2,1)}, f32[2,512,1024]{2,1,0:T(8,128)...) custom-call(bf16[4,512,1536]{2,1,0:T(8,128)(2,1)} %refs_0_.5, ...), custom_call_target="tpu_custom_call" | custom-call | flops 16000000000 | bytes 31457280 | tf_op jit(solution)/shard_map/project/pallas_call | solution.py:610
  79.9 12.3 %collective-permute-done.7.refs_9_ = f32[2,128,768]{2,1,0:T(8,128)S(1)} collective-permute-done((f32[2,128,768]{2,1,0:T(8,128)}, f32[2,128,768]{2,1,0:T(8,128)S(1)}, u32[]{:S(2)}, u32[]{:S(2)}) %collective-permute-start.7) | collective-permute-done | bytes 786464 | tf_op jit(solution)/shard_map/ppermute | solution.py:661
  97.6 6.2 %top.2 = (bf16[2,512,1536]{2,1,0:T(8,128)(2,1)}, f32[2,512,768]{2,1,0:T(8,128)}) custom-call(s32[4]{0:T(128)} %refs_0_.7, s32[1]{0:T(128)} %bitcast.5.refs_1_, bf16[4,512,1536]{2,1,0:T(8,128)(2,1)} %refs_2_.3, bf16[768,1536]{1,0:T(8,128)(2,1)} %refs_3_.3, f32[2,8,768]{2,1,0:T(8,128)} %get-tuple-element.92.refs_4_), custom_call_target="tpu_custom_call" | custom-call | flops 5000000000 | bytes 31457280 | tf_op jit(solution)/shard_map/top/pallas_call | solution.py:665
  103.8 6.2 %top.3 = (bf16[2,512,1536]{2,1,0:T(8,128)(2,1)}, f32[2,512,768]{2,1,0:T(8,128)}) custom-call(s32[4]{0:T(128)} %refs_0_.7, s32[1]{0:T(128)} %bitcast.5.refs_1_, bf16[4,512,1536]{2,1,0:T(8,128)(2,1)} %refs_2_.3, bf16[768,1536]{1,0:T(8,128)(2,1)} %refs_3_.3, bf16[2,512,1536]{2,1,0:T(8,128)(2,1)} %get-tuple-element.95.refs_4_.refs_2_), custom_call_target="tpu_custom_call" | custom-call | flops 5000000000 | bytes 31457280 | tf_op jit(solution)/shard_map/top/pallas_call | solution.py:665
  112.0 9.5 %gated.2 = (f32[2,512,768]{2,1,0:T(8,128)}, f32[2,128,768]{2,1,0:T(8,128)}, f32[2,8,512]{2,1,0:T(8,128)}) custom-call(f32[2,512,768]{2,1,0:T(8,128)} %get-tuple-element.86.refs_0_, f32[2,512,1024]{2,1,0:T(8,128)} %get-tuple-element.87.refs_1_.refs_2_, f32[2,512,768]{2,1,0:T(8,128)} %get-tuple-element.88.refs_2_.refs_3_, ...), custom_call_target="tpu_custom_call" | custom-call | flops 8000000000 | bytes 31457280 | tf_op jit(solution)/shard_map/gated/pallas_call | solution.py:678
  121.5 10.5 %all-gather.1 = f32[8,8,512]{2,1,0:T(8,128)} all-gather(f32[2,8,512]{2,1,0:T(8,128)} %get-tuple-element.98), channel_id=3, replica_groups=mesh['tensor'=4,'seq'=4,'dp'=2] {'tensor'}, dimensions={0}, use_global_device_ids=true | all-gather | bytes 163840 | tf_op jit(solution)/shard_map/all_gather | solution.py:949
  132.0 11.7 %outward.2 = (bf16[2,512,768]{2,1,0:T(8,128)(2,1)}, f32[2,512,768]{2,1,0:T(8,128)}, bf16[2,512,768]{2,1,0:T(8,128)(2,1)}, f32[2,2,128,768]{3,2,1,0:T(8,128)}, f3...) custom-call(s32[1]{0:T(128)} %bitcast.2.refs_0_, ...), custom_call_target="tpu_custom_call" | custom-call | flops 10000000000 | bytes 31457280 | tf_op jit(solution)/shard_map/outward/pallas_call | solution.py:698
  150.0 9.6 %gated.3 = (f32[2,512,768]{2,1,0:T(8,128)}, f32[2,128,768]{2,1,0:T(8,128)}, f32[2,8,512]{2,1,0:T(8,128)}) custom-call(f32[2,512,768]{2,1,0:T(8,128)} %get-tuple-element.103.refs_0_, f32[2,512,1024]{2,1,0:T(8,128)} %get-tuple-element.104.refs_1_.refs_2_, f32[2,512,768]{2,1,0:T(8,128)} %get-tuple-element.105.refs_2_.refs_3_, ...), custom_call_target="tpu_custom_call" | custom-call | flops 8000000000 | bytes 31457280 | tf_op jit(solution)/shard_map/gated/pallas_call | solution.py:678
  159.6 8.9 %all-gather.2 = f32[8,8,512]{2,1,0:T(8,128)} all-gather(f32[2,8,512]{2,1,0:T(8,128)} %get-tuple-element.112), channel_id=4, replica_groups=mesh['tensor'=4,'seq'=4,'dp'=2] {'tensor'}, dimensions={0}, use_global_device_ids=true | all-gather | bytes 163840 | tf_op jit(solution)/shard_map/all_gather | solution.py:949
  169.4 11.8 %outward.3 = (bf16[2,512,768]{2,1,0:T(8,128)(2,1)}, f32[2,512,768]{2,1,0:T(8,128)}, bf16[2,512,768]{2,1,0:T(8,128)(2,1)}, f32[2,2,128,768]{3,2,1,0:T(8,128)}, f3...) custom-call(s32[1]{0:T(128)} %bitcast.2.refs_0_, ...), custom_call_target="tpu_custom_call" | custom-call | flops 10000000000 | bytes 31457280 | tf_op jit(solution)/shard_map/outward/pallas_call | solution.py:698
  186.7 10.7 %gate_grad.1 = (bf16[1536,768]{1,0:T(8,128)(2,1)}, f32[1536,128]{1,0:T(8,128)}) custom-call(bf16[2,512,1536]{2,1,0:T(8,128)(2,1)} %get-tuple-element.118.refs_0_, bf16[2,512,1536]{2,1,0:T(8,128)(2,1)} %get-tuple-element.119.refs_1_, bf16[2,512,768]{2,1,0:T(8,128)(2,1)} %get-tuple-element.120.refs_2_.refs_1_, ...), custom_call_target="tpu_custom_call" | custom-call | flops 10000000000 | bytes 31457280 | tf_op jit(solution)/shard_map/gate_grad/pallas_call | solution.py:826
  201.5 10.2 %product.1.refs_18_ = bf16[2,256,1536]{2,1,0:T(8,128)(2,1)} custom-call(s32[1]{0:T(128)} %bitcast.2.refs_0_, bf16[8,256,1536]{2,1,0:T(8,128)(2,1)} %bitcast.71, bf16[8,256,1536]{2,1,0:T(8,128)(2,1)} %bitcast.72, bf16[4,768,1536]{2,1,0:T(8,128)(2,1)} %bitcast.107, bf16[256,768]{1,0:T(8,128)(2,1)} %get-tuple-element.99.refs_4_, bf16[256,768]{1,0:T(8,128)(2,1)} %copy-done.45, ...), custom_call_target="tpu_custom_call" | custom-call | flops 9600000000 | bytes 31457280 | tf_op jit(solution)/shard_map/product/pallas_call | solution.py:802
  216.6 7.7 %collective-permute-done.18.refs_17_ = bf16[2,128,768]{2,1,0:T(8,128)(2,1)S(1)} collective-permute-done((bf16[2,128,768]{2,1,0:T(8,128)(2,1)S(1)}, bf16[2,128,768]{2,1,0:T(8,128)(2,1)S(1)}, u32[]{:S(2)}, u32[]{:S(2)}) %collective-permute-start.18) | collective-permute-done | bytes 393248 | tf_op jit(solution)/shard_map/ppermute | solution.py:661
  225.2 25.7 %backward.2 = (bf16[2,512,1280]{2,1,0:T(8,128)(2,1)}, bf16[2,512,128]{2,1,0:T(8,128)(2,1)}, f32[2,8,1024]{2,1,0:T(8,128)}, f32[2,16,1024]{2,1,0:T(8,128)}, f32[40,1024]{1,0:T(8,128)}, /*index=5*/f32[16,128]{1,0:T(8,128)}) custom-call(f32[2,512,768]{2,1,0:T(8,128)} %get-tuple-element.97.refs_1_.refs_0_, f32[2,512,1024]{2,1,0:T(8,128)} %get-tuple-element.87.refs_1_.refs_2_, ...), custom_call_target="tpu_custom_call" | custom-call | flops 22000001024 | bytes 31457280 | tf_op jit(solution)/shard_map/backward/pallas_call | solution.py:725
  250.9 10.5 %out_grad.1.refs_6_ = bf16[768,1536]{1,0:T(8,128)(2,1)} custom-call(bf16[2,512,768]{2,1,0:T(8,128)(2,1)} %get-tuple-element.110.refs_12_.refs_0_, bf16[2,512,768]{2,1,0:T(8,128)(2,1)} %get-tuple-element.122.refs_5_.refs_1_, bf16[2,512,1536]{2,1,0:T(8,128)(2,1)} %get-tuple-element.95.refs_4_.refs_2_, ...), custom_call_target="tpu_custom_call" | custom-call | flops 10000000000 | bytes 31457280 | tf_op jit(solution)/shard_map/out_grad/pallas_call | solution.py:839
  261.5 4.3 copy.42
  274.5 12.6 %lowered.2 = (bf16[256,1536]{1,0:T(8,128)(2,1)}, bf16[256,1536]{1,0:T(8,128)(2,1)}, bf16[256,1536]{1,0:T(8,128)(2,1)}, bf16[256,1536]{1,0:T(8,128)(2,1)}) custom-call(s32[1]{0:T(128)} %bitcast.2.refs_0_, bf16[2,512,768]{2,1,0:T(8,128)(2,1)} %get-tuple-element.120.refs_2_.refs_1_, bf16[2,512,1280]{2,1,0:T(8,128)(2,1)} %maximum_dynamic-update-slice_fusion.refs_2_, ...), custom_call_target="tpu_custom_call" | custom-call | flops 8999999488 | bytes 31457280 | tf_op jit(solution)/shard_map/lowered/pallas_call | solution.py:761
  291.3 24.8 %backward.3 = (bf16[2,512,1280]{2,1,0:T(8,128)(2,1)}, bf16[2,512,128]{2,1,0:T(8,128)(2,1)}, f32[2,8,1024]{2,1,0:T(8,128)}, f32[2,16,1024]{2,1,0:T(8,128)}, f32[40,1024]{1,0:T(8,128)}, /*index=5*/f32[16,128]{1,0:T(8,128)}) custom-call(f32[2,512,768]{2,1,0:T(8,128)} %get-tuple-element.111.refs_1_.refs_0_, f32[2,512,1024]{2,1,0:T(8,128)} %get-tuple-element.104.refs_1_.refs_2_, ...), custom_call_target="tpu_custom_call" | custom-call | flops 22000001024 | bytes 31457280 | tf_op jit(solution)/shard_map/backward/pallas_call | solution.py:725
  316.2 5.6 %collective-permute-done.23.refs_7_ = bf16[256,1536]{1,0:T(8,128)(2,1)S(1)} collective-permute-done((bf16[256,1536]{1,0:T(8,128)(2,1)}, bf16[256,1536]{1,0:T(8,128)(2,1)S(1)}, u32[]{:S(2)}, u32[]{:S(2)}) %collective-permute-start.23) | collective-permute-done | bytes 786464 | tf_op jit(solution)/shard_map/ppermute | solution.py:873
  322.7 4.6 input_norm.2.refs_9_
  328.8 4.5 collective-permute-done.20
  334.0 16.1 %late.1 = (bf16[1536,896]{1,0:T(8,128)(2,1)}, f32[1536,256]{1,0:T(8,128)}, f32[1536,128]{1,0:T(8,128)}) custom-call(bf16[2,512,1536]{2,1,0:T(8,128)(2,1)} %get-tuple-element.118.refs_0_, bf16[2,512,1536]{2,1,0:T(8,128)(2,1)} %get-tuple-element.119.refs_1_, bf16[2,512,1280]{2,1,0:T(8,128)(2,1)} %maximum_dynamic-update-slice_fusion.refs_2_, ...), custom_call_target="tpu_custom_call" | custom-call | flops 20000000000 | bytes 31457280 | tf_op jit(solution)/shard_map/late/pallas_call | solution.py:851
  355.3 12.6 %lowered.3 = (bf16[256,1536]{1,0:T(8,128)(2,1)}, bf16[256,1536]{1,0:T(8,128)(2,1)}, bf16[256,1536]{1,0:T(8,128)(2,1)}, bf16[256,1536]{1,0:T(8,128)(2,1)}) custom-call(s32[1]{0:T(128)} %bitcast.2.refs_0_, bf16[2,512,768]{2,1,0:T(8,128)(2,1)} %get-tuple-element.121.refs_3_.refs_1_, bf16[2,512,1280]{2,1,0:T(8,128)(2,1)} %maximum_dynamic-update-slice_fusion.1.refs_3_.refs_2_, ...), custom_call_target="tpu_custom_call" | custom-call | flops 8999999488 | bytes 31457280 | tf_op jit(solution)/shard_map/lowered/pallas_call | solution.py:761
  371.5 15.5 %all_gather.46 = f32[8,61,128]{2,1,0:T(8,128)S(1)} all-gather(f32[1,61,128]{2,1,0:T(8,128)S(1)} %bitcast.106), channel_id=1, replica_groups=mesh['tensor'=4,'seq'=4,'dp'=2] {'seq','dp'}, dimensions={0}, use_global_device_ids=true | all-gather | bytes 281088 | tf_op jit(solution)/shard_map/all_gather | solution.py:999
  387.0 20.4 %all-gather.5 = f32[4,22,128]{2,1,0:T(8,128)S(1)} all-gather(f32[1,22,128]{2,1,0:T(8,128)S(1)} %slice_bitcast_fusion.3), channel_id=5, replica_groups=mesh['tensor'=4,'seq'=4,'dp'=2] {'tensor'}, dimensions={0}, use_global_device_ids=true | all-gather | bytes 56320 | tf_op jit(solution)/shard_map/all_gather | solution.py:1001
  409.1 4.6 input_norm.3.refs_1_.refs_2_
  420.3 5.9 %placed.2.refs_2_.refs_6_ = bf16[8,256,1536]{2,1,0:T(8,128)(2,1)} custom-call(bf16[8,256,1536]{2,1,0:T(8,128)(2,1)} %bitcast.77, bf16[256,1536]{1,0:T(8,128)(2,1)} %input_norm.3.refs_1_.refs_2_), custom_call_target="tpu_custom_call" | custom-call | tf_op jit(solution)/shard_map/placed/pallas_call | solution.py:882
  434.1 23.1 %all-gather.4 = f32[768,256]{1,0:T(8,128)S(1)} all-gather(f32[192,256]{1,0:T(8,128)} %settled.1), channel_id=6, replica_groups=mesh['tensor'=4,'seq'=4,'dp'=2] {'tensor'}, dimensions={0}, use_global_device_ids=true | all-gather | bytes 983040 | tf_op jit(solution)/shard_map/all_gather | solution.py:1020
  (262 shorter events, 90.5 us)
Async XLA Ops:
  8.0 192.7 %all-gather.14.cloned.1.call-start = ((), (), s32[]{:S(2)}) async-start(), calls=%async_computation.9 | async-start | bytes 11796480 | tf_op jit(solution)/shard_map/all_gather | solution.py:602
  8.7 281.8 %all-gather.10.cloned.1.call-start = ((), (), s32[]{:S(2)}) async-start(), calls=%async_computation.4 | async-start | bytes 7864320 | tf_op jit(solution)/shard_map/all_gather | solution.py:966
  9.7 14.7 %collective-permute-start = (bf16[4,16,1536]{2,1,0:T(8,128)(2,1)S(1)}, bf16[4,16,1536]{2,1,0:T(8,128)(2,1)S(1)}, u32[]{:S(2)}, u32[]{:S(2)}) collective-permute-start(bf16[4,16,1536]{2,1,0:T(8,128)(2,1)S(1)} %slice.120), channel_id=1, source_target_pairs={{0,2},{2,4},{4,6},{1,3},{3,5},{5,7},{8,10},{10,12},{12,14},{9,11},... | collective-permute-start | bytes 589832 | tf_op jit(solution)/shard_map/ppermute | solution.py:28
  47.7 27.4 %collective-permute-start.1 = (f32[2,128,768]{2,1,0:T(8,128)}, f32[2,128,768]{2,1,0:T(8,128)S(1)}, u32[]{:S(2)}, u32[]{:S(2)}) collective-permute-start(f32[2,128,768]{2,1,0:T(8,128)} %get-tuple-element.94), channel_id=1, source_target_pairs={{0,2},{1,3},{8,10},{9,11},{16,18},{17,19},{24,26},{25,27}} | collective-permute-start | bytes 2359304 | tf_op jit(solution)/shard_map/ppermute | solution.py:661
  73.7 18.5 %collective-permute-start.7 = (f32[2,128,768]{2,1,0:T(8,128)}, f32[2,128,768]{2,1,0:T(8,128)S(1)}, u32[]{:S(2)}, u32[]{:S(2)}) collective-permute-start(f32[2,128,768]{2,1,0:T(8,128)} %get-tuple-element.109), channel_id=1, source_target_pairs={{0,2},{1,3},{8,10},{9,11},{16,18},{17,19},{24,26},{25,27}} | collective-permute-start | bytes 2359304 | tf_op jit(solution)/shard_map/ppermute | solution.py:661
  76.3 18.5 %collective-permute-start.2 = (f32[2,128,768]{2,1,0:T(8,128)}, f32[2,128,768]{2,1,0:T(8,128)}, u32[]{:S(2)}, u32[]{:S(2)}) collective-permute-start(f32[2,128,768]{2,1,0:T(8,128)} %multiply_add_fusion.3), channel_id=1, source_target_pairs={{2,4},{3,5},{10,12},{11,13},{18,20},{19,21},{26,28},{27,29}} | collective-permute-start | bytes 2359304 | tf_op jit(solution)/shard_map/ppermute | solution.py:661
  93.3 16.8 %collective-permute-start.8 = (f32[2,128,768]{2,1,0:T(8,128)}, f32[2,128,768]{2,1,0:T(8,128)}, u32[]{:S(2)}, u32[]{:S(2)}) collective-permute-start(f32[2,128,768]{2,1,0:T(8,128)} %multiply_add_fusion.1), channel_id=1, source_target_pairs={{2,4},{3,5},{10,12},{11,13},{18,20},{19,21},{26,28},{27,29}} | collective-permute-start | bytes 2359304 | tf_op jit(solution)/shard_map/ppermute | solution.py:661
  96.1 15.9 %collective-permute-start.3 = (f32[2,128,768]{2,1,0:T(8,128)S(1)}, f32[2,128,768]{2,1,0:T(8,128)}, u32[]{:S(2)}, u32[]{:S(2)}) collective-permute-start(f32[2,128,768]{2,1,0:T(8,128)S(1)} %multiply_add_fusion.2), channel_id=1, source_target_pairs={{4,6},{5,7},{12,14},{13,15},{20,22},{21,23},{28,30},{29,31}} | collective-permute-start | bytes 2359304 | tf_op jit(solution)/shard_map/ppermute | solution.py:661
  111.3 37.8 %collective-permute-start.9 = (f32[2,128,768]{2,1,0:T(8,128)S(1)}, f32[2,128,768]{2,1,0:T(8,128)S(1)}, u32[]{:S(2)}, u32[]{:S(2)}) collective-permute-start(f32[2,128,768]{2,1,0:T(8,128)S(1)} %multiply_add_fusion), channel_id=1, source_target_pairs={{4,6},{5,7},{12,14},{13,15},{20,22},{21,23},{28,30},{29,31}} | collective-permute-start | bytes 2359304 | tf_op jit(solution)/shard_map/ppermute | solution.py:661
  144.9 23.7 %collective-permute-start.10 = (bf16[2,128,768]{2,1,0:T(8,128)(2,1)S(1)}, bf16[2,128,768]{2,1,0:T(8,128)(2,1)S(1)}, u32[]{:S(2)}, u32[]{:S(2)}) collective-permute-start(bf16[2,128,768]{2,1,0:T(8,128)(2,1)S(1)} %fusion.2), channel_id=1, source_target_pairs={{6,4},{7,5},{14,12},{15,13},{22,20},{23,21},{30,28},{31,29}} | collective-permute-start | bytes 1179656 | tf_op jit(solution)/shard_map/ppermute | solution.py:661
  145.5 37.5 %collective-permute-start.4 = (bf16[256,768]{1,0:T(8,128)(2,1)}, bf16[256,768]{1,0:T(8,128)(2,1)S(1)}, u32[]{:S(2)}, u32[]{:S(2)}) collective-permute-start(bf16[256,768]{1,0:T(8,128)(2,1)} %get-tuple-element.100), channel_id=1, source_target_pairs={{0,8},{8,0},{16,24},{24,16},{1,9},{9,1},{17,25},{25,17},{2,10},{10... | collective-permute-start | bytes 1179656 | tf_op jit(solution)/shard_map/ppermute | solution.py:873
  146.1 37.7 %collective-permute-start.5 = (bf16[256,768]{1,0:T(8,128)(2,1)}, bf16[256,768]{1,0:T(8,128)(2,1)}, u32[]{:S(2)}, u32[]{:S(2)}) collective-permute-start(bf16[256,768]{1,0:T(8,128)(2,1)} %get-tuple-element.101), channel_id=1, source_target_pairs={{0,16},{8,24},{16,0},{24,8},{1,17},{9,25},{17,1},{25,9},{2,18},{10... | collective-permute-start | bytes 1179656 | tf_op jit(solution)/shard_map/ppermute | solution.py:873
  147.6 49.7 %collective-permute-start.6 = (bf16[256,768]{1,0:T(8,128)(2,1)}, bf16[256,768]{1,0:T(8,128)(2,1)}, u32[]{:S(2)}, u32[]{:S(2)}) collective-permute-start(bf16[256,768]{1,0:T(8,128)(2,1)} %get-tuple-element.102), channel_id=1, source_target_pairs={{0,24},{8,16},{16,8},{24,0},{1,25},{9,17},{17,9},{25,1},{2,26},{10... | collective-permute-start | bytes 1179656 | tf_op jit(solution)/shard_map/ppermute | solution.py:873
  168.7 16.5 %collective-permute-start.14 = (bf16[2,128,768]{2,1,0:T(8,128)(2,1)S(1)}, bf16[2,128,768]{2,1,0:T(8,128)(2,1)S(1)}, u32[]{:S(2)}, u32[]{:S(2)}) collective-permute-start(bf16[2,128,768]{2,1,0:T(8,128)(2,1)S(1)} %add_convert_fusion.3), channel_id=1, source_target_pairs={{4,2},{5,3},{12,10},{13,11},{20,18},{21,19},{28,26},{29,27}} | collective-permute-start | bytes 1179656 | tf_op jit(solution)/shard_map/ppermute | solution.py:661
  182.4 15.0 %collective-permute-start.15 = (bf16[2,128,768]{2,1,0:T(8,128)(2,1)S(1)}, bf16[2,128,768]{2,1,0:T(8,128)(2,1)S(1)}, u32[]{:S(2)}, u32[]{:S(2)}) collective-permute-start(bf16[2,128,768]{2,1,0:T(8,128)(2,1)S(1)} %fusion.3), channel_id=1, source_target_pairs={{6,4},{7,5},{14,12},{15,13},{22,20},{23,21},{30,28},{31,29}} | collective-permute-start | bytes 1179656 | tf_op jit(solution)/shard_map/ppermute | solution.py:661
  183.9 16.9 %collective-permute-start.12 = (bf16[256,768]{1,0:T(8,128)(2,1)}, bf16[256,768]{1,0:T(8,128)(2,1)}, u32[]{:S(2)}, u32[]{:S(2)}) collective-permute-start(bf16[256,768]{1,0:T(8,128)(2,1)} %get-tuple-element.116), channel_id=1, source_target_pairs={{0,16},{8,24},{16,0},{24,8},{1,17},{9,25},{17,1},{25,9},{2,18},{10... | collective-permute-start | bytes 1179656 | tf_op jit(solution)/shard_map/ppermute | solution.py:873
  185.2 15.5 %collective-permute-start.13 = (bf16[256,768]{1,0:T(8,128)(2,1)}, bf16[256,768]{1,0:T(8,128)(2,1)S(1)}, u32[]{:S(2)}, u32[]{:S(2)}) collective-permute-start(bf16[256,768]{1,0:T(8,128)(2,1)} %get-tuple-element.117), channel_id=1, source_target_pairs={{0,24},{8,16},{16,8},{24,0},{1,25},{9,17},{17,9},{25,1},{2,26},{10... | collective-permute-start | bytes 1179656 | tf_op jit(solution)/shard_map/ppermute | solution.py:873
  211.7 139.7 %reduce-scatter.7.cloned.1.call-start = ((), (), s32[]{:S(2)}) async-start(), calls=%async_computation.5 | async-start | bytes 2654208 | tf_op jit(solution)/shard_map/reduce_scatter | solution.py:938
  212.3 140.4 %reduce-scatter.13.cloned.1.call-start = ((), (), s32[]{:S(2)}) async-start(), calls=%async_computation.10 | async-start | bytes 2654208
  265.8 142.3 %all-gather.12.cloned.1.call-start = ((), (), s32[]{:S(2)}) async-start(), calls=%async_computation.6 | async-start | bytes 3932160 | tf_op jit(solution)/shard_map/all_gather | solution.py:980
  268.2 22.4 %collective-permute-start.17 = (bf16[2,128,768]{2,1,0:T(8,128)(2,1)S(1)}, bf16[2,128,768]{2,1,0:T(8,128)(2,1)S(1)}, u32[]{:S(2)}, u32[]{:S(2)}) collective-permute-start(bf16[2,128,768]{2,1,0:T(8,128)(2,1)S(1)} %add_convert_fusion.1), channel_id=1, source_target_pairs={{2,0},{3,1},{10,8},{11,9},{18,16},{19,17},{26,24},{27,25}} | collective-permute-start | bytes 1179656 | tf_op jit(solution)/shard_map/ppermute | solution.py:661
  287.1 29.1 %collective-permute-start.21 = (bf16[256,1536]{1,0:T(8,128)(2,1)}, bf16[256,1536]{1,0:T(8,128)(2,1)S(1)}, u32[]{:S(2)}, u32[]{:S(2)}) collective-permute-start(bf16[256,1536]{1,0:T(8,128)(2,1)} %get-tuple-element.145), channel_id=1, source_target_pairs={{0,8},{8,0},{16,24},{24,16},{1,9},{9,1},{17,25},{25,17},{2,10},{10... | collective-permute-start | bytes 2359304 | tf_op jit(solution)/shard_map/ppermute | solution.py:873
  288.6 27.7 %collective-permute-start.22 = (bf16[256,1536]{1,0:T(8,128)(2,1)}, bf16[256,1536]{1,0:T(8,128)(2,1)S(1)}, u32[]{:S(2)}, u32[]{:S(2)}) collective-permute-start(bf16[256,1536]{1,0:T(8,128)(2,1)} %get-tuple-element.146), channel_id=1, source_target_pairs={{0,16},{8,24},{16,0},{24,8},{1,17},{9,25},{17,1},{25,9},{2,18},{10... | collective-permute-start | bytes 2359304 | tf_op jit(solution)/shard_map/ppermute | solution.py:873
  289.3 32.5 %collective-permute-start.23 = (bf16[256,1536]{1,0:T(8,128)(2,1)}, bf16[256,1536]{1,0:T(8,128)(2,1)S(1)}, u32[]{:S(2)}, u32[]{:S(2)}) collective-permute-start(bf16[256,1536]{1,0:T(8,128)(2,1)} %get-tuple-element.147), channel_id=1, source_target_pairs={{0,24},{8,16},{16,8},{24,0},{1,25},{9,17},{17,9},{25,1},{2,26},{10... | collective-permute-start | bytes 2359304 | tf_op jit(solution)/shard_map/ppermute | solution.py:873
  327.4 102.0 %reduce-scatter.9.cloned.1.call-start = ((), (), s32[]{:S(2)}) async-start(), calls=%async_computation.7 | async-start | bytes 3096576 | tf_op jit(solution)/shard_map/reduce_scatter | solution.py:938
  350.2 82.2 %reduce-scatter.11.cloned.1.call-start = ((), (), s32[]{:S(2)}) async-start(), calls=%async_computation.8 | async-start | bytes 1769472 | tf_op jit(solution)/shard_map/reduce_scatter | solution.py:938
  367.9 40.1 %collective-permute-start.24 = (bf16[256,1536]{1,0:T(8,128)(2,1)}, bf16[256,1536]{1,0:T(8,128)(2,1)S(1)}, u32[]{:S(2)}, u32[]{:S(2)}) collective-permute-start(bf16[256,1536]{1,0:T(8,128)(2,1)} %get-tuple-element.150), channel_id=1, source_target_pairs={{0,8},{8,0},{16,24},{24,16},{1,9},{9,1},{17,25},{25,17},{2,10},{10... | collective-permute-start | bytes 2359304 | tf_op jit(solution)/shard_map/ppermute | solution.py:873
  368.8 39.2 %collective-permute-start.25 = (bf16[256,1536]{1,0:T(8,128)(2,1)}, bf16[256,1536]{1,0:T(8,128)(2,1)S(1)}, u32[]{:S(2)}, u32[]{:S(2)}) collective-permute-start(bf16[256,1536]{1,0:T(8,128)(2,1)} %get-tuple-element.151), channel_id=1, source_target_pairs={{0,16},{8,24},{16,0},{24,8},{1,17},{9,25},{17,1},{25,9},{2,18},{10... | collective-permute-start | bytes 2359304 | tf_op jit(solution)/shard_map/ppermute | solution.py:873
  369.9 38.1 %collective-permute-start.26 = (bf16[256,1536]{1,0:T(8,128)(2,1)}, bf16[256,1536]{1,0:T(8,128)(2,1)}, u32[]{:S(2)}, u32[]{:S(2)}) collective-permute-start(bf16[256,1536]{1,0:T(8,128)(2,1)} %get-tuple-element.152), channel_id=1, source_target_pairs={{0,24},{8,16},{16,8},{24,0},{1,25},{9,17},{17,9},{25,1},{2,26},{10... | collective-permute-start | bytes 2359304 | tf_op jit(solution)/shard_map/ppermute | solution.py:873
  413.8 45.6 %collective-permute-start.27 = (bf16[256,1536]{1,0:T(8,128)(2,1)}, bf16[256,1536]{1,0:T(8,128)(2,1)S(1)}, u32[]{:S(2)}, u32[]{:S(2)}) collective-permute-start(bf16[256,1536]{1,0:T(8,128)(2,1)} %input_norm.3.refs_1_.refs_2_), channel_id=1, source_target_pairs={{0,8},{8,0},{16,24},{24,16},{1,9},{9,1},{17,25},{25,17},{2,10},{10... | collective-permute-start | bytes 2359304 | tf_op jit(solution)/shard_map/ppermute | solution.py:868
  415.3 44.1 %collective-permute-start.28 = (bf16[256,1536]{1,0:T(8,128)(2,1)}, bf16[256,1536]{1,0:T(8,128)(2,1)S(1)}, u32[]{:S(2)}, u32[]{:S(2)}) collective-permute-start(bf16[256,1536]{1,0:T(8,128)(2,1)} %input_norm.3.refs_1_.refs_2_), channel_id=1, source_target_pairs={{0,16},{8,24},{16,0},{24,8},{1,17},{9,25},{17,1},{25,9},{2,18},{10... | collective-permute-start | bytes 2359304 | tf_op jit(solution)/shard_map/ppermute | solution.py:868
  415.8 43.6 %collective-permute-start.29 = (bf16[256,1536]{1,0:T(8,128)(2,1)}, bf16[256,1536]{1,0:T(8,128)(2,1)}, u32[]{:S(2)}, u32[]{:S(2)}) collective-permute-start(bf16[256,1536]{1,0:T(8,128)(2,1)} %input_norm.3.refs_1_.refs_2_), channel_id=1, source_target_pairs={{0,24},{8,16},{16,8},{24,0},{1,25},{9,17},{17,9},{25,1},{2,26},{10... | collective-permute-start | bytes 2359304 | tf_op jit(solution)/shard_map/ppermute | solution.py:868
  (55 other events, 381.1 us)
Sparse Core Ops, SparseCore 0:
  10.7 99.0 all-gather.13
  211.8 76.8 all-gather.9
  327.5 45.6 all-gather.11
Sparse Core Ops, SparseCore 1:
  214.5 41.9 reduce-scatter.6
  265.9 37.0 reduce-scatter.12
  350.3 37.7 reduce-scatter.8
  390.5 33.6 reduce-scatter.10

commit v3 on v2

--- a/solution.py
+++ b/solution.py
@@ -473,6 +473,14 @@
     out_ref[...] = block_ref[...]
 
 
+def settle_kernel(wide_ref, rest_ref, out_ref):
+    rows, width = wide_ref.shape
+    groups = width // LANES
+    for k in range(groups):
+        out_ref[k * rows : (k + 1) * rows] = wide_ref[:, k * LANES : (k + 1) * LANES]
+    out_ref[groups * rows :] = rest_ref[...]
+
+
 def merged(ref):
     return ref[...].reshape(ref.shape[0] * ref.shape[1], ref.shape[2])
 
@@ -490,8 +498,8 @@
 
 
 def out_grad_kernel(*refs):
-    normed, top, out_ref = refs[:STREAMS], refs[STREAMS : 2 * STREAMS], refs[-1]
-    out_ref[...] = sum(mm_tn(merged(a), merged(b)) for a, b in zip(normed, top)).astype(LOW)
+    top, normed, out_ref = refs[:STREAMS], refs[STREAMS : 2 * STREAMS], refs[-1]
+    out_ref[...] = sum(mm_tn(merged(a), merged(b)) for a, b in zip(top, normed)).astype(LOW)
 
 
 def late_kernel(width, state, *refs):
@@ -835,17 +843,17 @@
             name="gate_grad",
         )(*low, *grads, main_w, *marks)
 
-    def out_grad(normed, top, marks=()):
+    def out_grad(top, normed, marks=()):
         return pl.pallas_call(
             ignoring(out_grad_kernel, 2 * STREAMS, len(marks)),
-            grid=(width // tile,),
-            in_specs=[column] * STREAMS + [whole((seqs, rows, model))] * STREAMS + [anywhere] * len(marks),
-            out_specs=row(model),
-            out_shape=sds((width, model), LOW),
+            grid=(tiles,),
+            in_specs=[column] * STREAMS + [whole((seqs, rows, width))] * STREAMS + [anywhere] * len(marks),
+            out_specs=row(width),
+            out_shape=sds((model, width), LOW),
             compiler_params=params(),
             cost_estimate=cost(2.5e9 * all_seqs),
             name="out_grad",
-        )(*normed, *top, *marks)
+        )(*top, *normed, *marks)
 
     def late_of(low, mixed, step, gain, marks=()):
         return pl.pallas_call(
@@ -935,7 +943,7 @@
         )
         return made, step_low, filter_sum, term_sum
 
-    reduced = lambda a, axis=0: lax.psum_scatter(a, ("seq", "dp"), scatter_dimension=axis, tiled=True)
+    reduced = lambda a: lax.psum_scatter(a, ("seq", "dp"), scatter_dimension=0, tiled=True)
 
     first = [project(0, halo)]
     first.append(project(1, halo, [first[0][-1]]))
@@ -966,27 +974,27 @@
     block_out = lax.all_gather(made_out, "tensor", axis=1, tiled=True)
     out_w = []
     third = [
-        backward_of(0, leaving[0], [made_out, leaving[1][1]], lambda raw: out_w.append(out_grad(normed, top, [raw])))
+        backward_of(0, leaving[0], [made_out, leaving[1][1]], lambda raw: out_w.append(out_grad(top, normed, [raw])))
     ]
-    out_w_sum = reduced(out_w[0], 1)
+    out_w_sum = reduced(out_w[0])
     partial = [lowered_of(grad_gate[0], *third[0][:2], [out_w[0]])]
     sums = [swapped(partial[0])]
     own = []
     third.append(
         backward_of(
-            1, leaving[1], [partial[0][0], block_out], lambda raw: own.append(input_norm(0, sums[0], top[0], [raw]))
+            1, leaving[1], [partial[0][0]], lambda raw: own.append(input_norm(0, sums[0], top[0], [raw, block_out]))
         )
     )
     first_in = lax.all_gather(own[0], "tensor", axis=0, tiled=True)
     grad_mixed, grad_step, filter_sums, term_sums = zip(*third)
-    grad_own, grad_side, gain_sums = late_of(low, grad_mixed, grad_step, gain_sums, [own[0]])
-    partial.append(lowered_of(grad_gate[1], *third[1][:2], [grad_own, gate_w_sum]))
+    partial.append(lowered_of(grad_gate[1], *third[1][:2], [own[0], gate_w_sum]))
+    grad_own, grad_side, gain_sums = late_of(low, grad_mixed, grad_step, gain_sums, [own[0], partial[1][0]])
     sums.append(swapped(partial[1]))
     own_sum = reduced(grad_own)
     grad_own_w = own_sum.astype(F32)
     shared_w = reduced(grad_side)
     grad_gate_w = gate_w_sum.astype(F32)
-    grad_out_w = out_w_sum.astype(F32)
+    grad_out_w = out_w_sum.astype(F32).T
     grad_main_w = jnp.stack([grad_gate_w, grad_own_w[:, :width]], axis=1)
     grad_step_w = grad_own_w[:, width : width + heads]
     filters = jnp.sum(sum(filter_sums).reshape(CONV + 1, 8, mixed_width), axis=1)
@@ -998,26 +1006,31 @@
     packed_sums = jnp.concatenate([a.reshape(-1) for a in everywhere + per_rank])
     packed_sums = jnp.sum(lax.all_gather(packed_sums.reshape(-1, LANES), ("seq", "dp"), axis=0), axis=0)
     split = (everywhere[0].size + everywhere[1].size) // LANES
-    shared_sums = jnp.sum(lax.all_gather(packed_sums[:split], "tensor", axis=0), axis=0).reshape(-1)
     rank_sums = packed_sums[split:].reshape(-1)
-    small_in = shared_sums[:model]
-    small_shared = shared_sums[model:].reshape(CONV + 1, 2 * state)
     small_main = rank_sums[: (CONV + 1) * width].reshape(CONV + 1, width)
     small_terms = rank_sums[(CONV + 1) * width : -width].reshape(3, LANES)[:, :heads]
     small_out = rank_sums[-width:]
-    last_own = input_norm(1, sums[1], top[1], [shared_sums, first_in])
+    last_own = input_norm(1, sums[1], top[1], [packed_sums, first_in])
     pieces = exchanged(last_own)
     stacked = STREAMS * ranks
     block_out = placed(block_out.reshape(stacked, share, model), stacked, [last_own])
     input_grad = placed(first_in.reshape(-1, share, model), stacked, [last_own, block_out])
-    shared_w = pl.pallas_call(
-        ignoring(place_kernel, 1, 2),
-        in_specs=[pl.BlockSpec(memory_space=pltpu.VMEM), anywhere, anywhere],
+    padded_split = -(-split // 8) * 8
+    settled = pl.pallas_call(
+        ignoring(settle_kernel, 2, 2),
+        in_specs=[pl.BlockSpec(memory_space=pltpu.VMEM)] * 2 + [anywhere] * 2,
         out_specs=pl.BlockSpec(memory_space=pltpu.VMEM),
-        out_shape=sds(shared_w.shape, F32),
+        out_shape=sds((shared_w.size // LANES + padded_split, LANES), F32),
         name="settled",
-    )(shared_w, input_grad, own_sum)
-    grad_shared_w = jnp.sum(lax.all_gather(shared_w, "tensor", axis=0), axis=0)
+    )(shared_w, jnp.pad(packed_sums[:split], ((0, padded_split - split), (0, 0))), input_grad, own_sum)
+    settled = jnp.sum(lax.all_gather(settled, "tensor", axis=0), axis=0)
+    share_rows = shared_w.shape[0]
+    grad_shared_w = jnp.concatenate(
+        [settled[k * share_rows : (k + 1) * share_rows] for k in range(2 * state // LANES)], axis=1
+    )
+    shared_sums = settled[shared_w.size // LANES :][:split].reshape(-1)
+    small_in = shared_sums[:model]
+    small_shared = shared_sums[model:].reshape(CONV + 1, 2 * state)
     input_grad = assembled(input_grad, pieces, [block_out])
     return (
         block_out.reshape(residual_in.shape),

time: 480 us -> 481 us (level)
  waiting for transfers between devices: 38.7 us -> 73.3 us
  blocking collectives: 78.4 us -> 50.8 us
  local copies, waits for them, and re-layouts: 35.1 us -> 28.1 us
    all_gather x2 -> x1, blocking collectives: 43.5 us -> 15.7 us  [per_device(): settled = jnp.sum(lax.all_gather(settled, 'tensor', axis=0), axis=0)]
    ppermute x12, waiting for transfers between devices: 8.97 us -> 29.6 us  [swapped(): lax.ppermute(b, 'tensor', [(i, i ^ d) for i in range(ranks)])]
    reduce_scatter x3 -> x4, waiting for transfers between devices: 0.03 us -> 13 us  [per_device(): lax.psum_scatter(a, ('seq', 'dp'), scatter_dimension=0, tiled=True)]
    unnamed x113 -> x115, local copies, waits for them, and re-layouts: 22.8 us -> 15.8 us
  transfers between devices with their start and end apart: 37 -> 37, of which waited for: 6 -> 9; matrix products, arithmetic and copies ran while one was open for 9% -> 8% of each run, Pallas kernels for 49% -> 49%
where the time goes in v3:
time: 481 us; the launch traced here: 473 us
  Pallas kernels  246 us (51%)
  waiting for transfers between devices  73.3 us (15%)
  blocking collectives  50.8 us (11%)
  starting transfers between devices  41.7 us (9%)
  local copies, waits for them, and re-layouts  28.1 us (6%)
  between operations  17 us (4%)
  other arithmetic  15.7 us (3%)
    pallas_call x2, Pallas kernels, backward(): pl.pallas_call(ignoring(functools.partial(back_kernel, *dims), 15 + len(l...  50.7 us
    pallas_call x2, Pallas kernels, project(): pl.pallas_call(ignoring(functools.partial(project_kernel, *dims), 8, len(...  43.7 us
    ppermute x12, waiting for transfers between devices, swapped(): lax.ppermute(b, 'tensor', [(i, i ^ d) for i in range(ranks)])  29.6 us
    pallas_call x2, Pallas kernels, lowered_of(): pl.pallas_call(ignoring(functools.partial(lowered_kernel, width, state),...  25.8 us
    pallas_call x2, Pallas kernels, outward(): pl.pallas_call(ignoring(functools.partial(out_kernel, *dims, inner_total)...  23.6 us
    ppermute x12, waiting for transfers between devices, chained(): lax.ppermute(sent.astype(kind), 'seq', [(sender, sender + direction)])  19.9 us
    all_gather x2, blocking collectives, gated_of_stream(): return (y, entering, stats, lax.all_gather(stats, 'tensor', axis=0))  19.4 us
    pallas_call x2, Pallas kernels, gated_of(): pl.pallas_call(ignoring(functools.partial(gate_kernel, *dims), 9 + len(ar...  19.1 us
  transfers between devices with their start and end apart: 37, of which 9 were waited for; matrix products, arithmetic and copies ran while one was open for 8% of the time, Pallas kernels for 49%

profile of v3, /device:TPU:0, one launch (start us, length us, event | category | flops | bytes accessed | tf_op | source)
XLA Modules:
  0.0 472.6 jit_solution(7969256728657911487)
XLA Ops:
  9.7 4.9 %collective-permute-start = (bf16[4,16,1536]{2,1,0:T(8,128)(2,1)S(1)}, bf16[4,16,1536]{2,1,0:T(8,128)(2,1)S(1)}, u32[]{:S(2)}, u32[]{:S(2)}) collective-permute-start(bf16[4,16,1536]{2,1,0:T(8,128)(2,1)S(1)} %slice.132), channel_id=1, source_target_pairs={{0,2},{2,4},{4,6},{1,3},{3,5},{5,7},{8,10},{10,12},{12,14},{9,11},... | collective-permute-start | bytes 589832 | tf_op jit(solution)/shard_map/ppermute | solution.py:28
  14.8 5.5 %copy.41 = bf16[192,8,2,768]{3,1,2,0:T(8,128)(2,1)} copy(bf16[192,8,2,768]{3,2,1,0:T(2,128)(2,1)} %bitcast.74) | data formatting | bytes 9437184
  25.6 21.7 %project.2 = (bf16[2,512,1536]{2,1,0:T(8,128)(2,1)}, bf16[2,512,1024]{2,1,0:T(8,128)(2,1)}, bf16[2,16,1024]{2,1,0:T(8,128)(2,1)}, f32[2,512,1024]{2,1,0:T(8,128)...) custom-call(bf16[4,512,1536]{2,1,0:T(8,128)(2,1)} %refs_0_.5, ...), custom_call_target="tpu_custom_call" | custom-call | flops 16000000000 | bytes 31457280 | tf_op jit(solution)/shard_map/project/pallas_call | solution.py:618
  52.1 22.0 %project.3 = (bf16[2,512,1536]{2,1,0:T(8,128)(2,1)}, bf16[2,512,1024]{2,1,0:T(8,128)(2,1)}, bf16[2,16,1024]{2,1,0:T(8,128)(2,1)}, f32[2,512,1024]{2,1,0:T(8,128)...) custom-call(bf16[4,512,1536]{2,1,0:T(8,128)(2,1)} %refs_0_.5, ...), custom_call_target="tpu_custom_call" | custom-call | flops 16000000000 | bytes 31457280 | tf_op jit(solution)/shard_map/project/pallas_call | solution.py:618
  80.4 12.2 %collective-permute-done.7.refs_9_ = f32[2,128,768]{2,1,0:T(8,128)S(1)} collective-permute-done((f32[2,128,768]{2,1,0:T(8,128)}, f32[2,128,768]{2,1,0:T(8,128)S(1)}, u32[]{:S(2)}, u32[]{:S(2)}) %collective-permute-start.7) | collective-permute-done | bytes 786464 | tf_op jit(solution)/shard_map/ppermute | solution.py:669
  98.0 6.2 %top.2 = (bf16[2,512,1536]{2,1,0:T(8,128)(2,1)}, f32[2,512,768]{2,1,0:T(8,128)}) custom-call(s32[4]{0:T(128)} %refs_0_.7, s32[1]{0:T(128)} %bitcast.3.refs_1_, bf16[4,512,1536]{2,1,0:T(8,128)(2,1)} %refs_2_.3, bf16[768,1536]{1,0:T(8,128)(2,1)} %refs_3_.3, f32[2,8,768]{2,1,0:T(8,128)} %get-tuple-element.92.refs_4_), custom_call_target="tpu_custom_call" | custom-call | flops 5000000000 | bytes 31457280 | tf_op jit(solution)/shard_map/top/pallas_call | solution.py:673
  104.2 6.2 %top.3 = (bf16[2,512,1536]{2,1,0:T(8,128)(2,1)}, f32[2,512,768]{2,1,0:T(8,128)}) custom-call(s32[4]{0:T(128)} %refs_0_.7, s32[1]{0:T(128)} %bitcast.3.refs_1_, bf16[4,512,1536]{2,1,0:T(8,128)(2,1)} %refs_2_.3, bf16[768,1536]{1,0:T(8,128)(2,1)} %refs_3_.3, bf16[2,512,1536]{2,1,0:T(8,128)(2,1)} %get-tuple-element.95.refs_4_.refs_0_), custom_call_target="tpu_custom_call" | custom-call | flops 5000000000 | bytes 31457280 | tf_op jit(solution)/shard_map/top/pallas_call | solution.py:673
  112.4 9.5 %gated.2 = (f32[2,512,768]{2,1,0:T(8,128)}, f32[2,128,768]{2,1,0:T(8,128)}, f32[2,8,512]{2,1,0:T(8,128)}) custom-call(f32[2,512,768]{2,1,0:T(8,128)} %get-tuple-element.86.refs_0_, f32[2,512,1024]{2,1,0:T(8,128)} %get-tuple-element.87.refs_1_.refs_2_, f32[2,512,768]{2,1,0:T(8,128)} %get-tuple-element.88.refs_2_.refs_3_, ...), custom_call_target="tpu_custom_call" | custom-call | flops 8000000000 | bytes 31457280 | tf_op jit(solution)/shard_map/gated/pallas_call | solution.py:686
  121.8 10.5 %all-gather.1 = f32[8,8,512]{2,1,0:T(8,128)} all-gather(f32[2,8,512]{2,1,0:T(8,128)} %get-tuple-element.98), channel_id=3, replica_groups=mesh['tensor'=4,'seq'=4,'dp'=2] {'tensor'}, dimensions={0}, use_global_device_ids=true | all-gather | bytes 163840 | tf_op jit(solution)/shard_map/all_gather | solution.py:957
  132.4 11.7 %outward.2 = (bf16[2,512,768]{2,1,0:T(8,128)(2,1)}, f32[2,512,768]{2,1,0:T(8,128)}, bf16[2,512,768]{2,1,0:T(8,128)(2,1)}, f32[2,2,128,768]{3,2,1,0:T(8,128)}, f3...) custom-call(s32[1]{0:T(128)} %bitcast.refs_0_, ...), custom_call_target="tpu_custom_call" | custom-call | flops 10000000000 | bytes 31457280 | tf_op jit(solution)/shard_map/outward/pallas_call | solution.py:706
  150.4 9.6 %gated.3 = (f32[2,512,768]{2,1,0:T(8,128)}, f32[2,128,768]{2,1,0:T(8,128)}, f32[2,8,512]{2,1,0:T(8,128)}) custom-call(f32[2,512,768]{2,1,0:T(8,128)} %get-tuple-element.103.refs_0_, f32[2,512,1024]{2,1,0:T(8,128)} %get-tuple-element.104.refs_1_.refs_2_, f32[2,512,768]{2,1,0:T(8,128)} %get-tuple-element.105.refs_2_.refs_3_, ...), custom_call_target="tpu_custom_call" | custom-call | flops 8000000000 | bytes 31457280 | tf_op jit(solution)/shard_map/gated/pallas_call | solution.py:686
  160.0 8.9 %all-gather.2 = f32[8,8,512]{2,1,0:T(8,128)} all-gather(f32[2,8,512]{2,1,0:T(8,128)} %get-tuple-element.112), channel_id=4, replica_groups=mesh['tensor'=4,'seq'=4,'dp'=2] {'tensor'}, dimensions={0}, use_global_device_ids=true | all-gather | bytes 163840 | tf_op jit(solution)/shard_map/all_gather | solution.py:957
  169.8 11.9 %outward.3 = (bf16[2,512,768]{2,1,0:T(8,128)(2,1)}, f32[2,512,768]{2,1,0:T(8,128)}, bf16[2,512,768]{2,1,0:T(8,128)(2,1)}, f32[2,2,128,768]{3,2,1,0:T(8,128)}, f3...) custom-call(s32[1]{0:T(128)} %bitcast.refs_0_, ...), custom_call_target="tpu_custom_call" | custom-call | flops 10000000000 | bytes 31457280 | tf_op jit(solution)/shard_map/outward/pallas_call | solution.py:706
  187.2 10.7 %gate_grad.1 = (bf16[1536,768]{1,0:T(8,128)(2,1)}, f32[1536,128]{1,0:T(8,128)}) custom-call(bf16[2,512,1536]{2,1,0:T(8,128)(2,1)} %get-tuple-element.118.refs_0_, bf16[2,512,1536]{2,1,0:T(8,128)(2,1)} %get-tuple-element.119.refs_1_, bf16[2,512,768]{2,1,0:T(8,128)(2,1)} %get-tuple-element.120.refs_2_.refs_1_, ...), custom_call_target="tpu_custom_call" | custom-call | flops 10000000000 | bytes 31457280 | tf_op jit(solution)/shard_map/gate_grad/pallas_call | solution.py:834
  202.1 10.1 %product.1.refs_18_ = bf16[2,256,1536]{2,1,0:T(8,128)(2,1)} custom-call(s32[1]{0:T(128)} %bitcast.refs_0_, bf16[8,256,1536]{2,1,0:T(8,128)(2,1)} %bitcast.68, bf16[8,256,1536]{2,1,0:T(8,128)(2,1)} %bitcast.69, bf16[4,768,1536]{2,1,0:T(8,128)(2,1)} %bitcast.101, bf16[256,768]{1,0:T(8,128)(2,1)} %get-tuple-element.99.refs_4_, bf16[256,768]{1,0:T(8,128)(2,1)} %copy-done.47, ...), custom_call_target="tpu_custom_call" | custom-call | flops 9600000000 | bytes 31457280 | tf_op jit(solution)/shard_map/product/pallas_call | solution.py:810
  217.1 7.7 %collective-permute-done.18.refs_17_ = bf16[2,128,768]{2,1,0:T(8,128)(2,1)S(1)} collective-permute-done((bf16[2,128,768]{2,1,0:T(8,128)(2,1)S(1)}, bf16[2,128,768]{2,1,0:T(8,128)(2,1)S(1)}, u32[]{:S(2)}, u32[]{:S(2)}) %collective-permute-start.18) | collective-permute-done | bytes 393248 | tf_op jit(solution)/shard_map/ppermute | solution.py:669
  225.7 25.7 %backward.2 = (bf16[2,512,1280]{2,1,0:T(8,128)(2,1)}, bf16[2,512,128]{2,1,0:T(8,128)(2,1)}, f32[2,8,1024]{2,1,0:T(8,128)}, f32[2,16,1024]{2,1,0:T(8,128)}, f32[40,1024]{1,0:T(8,128)}, /*index=5*/f32[16,128]{1,0:T(8,128)}) custom-call(f32[2,512,768]{2,1,0:T(8,128)} %get-tuple-element.97.refs_1_.refs_0_, f32[2,512,1024]{2,1,0:T(8,128)} %get-tuple-element.87.refs_1_.refs_2_, ...), custom_call_target="tpu_custom_call" | custom-call | flops 22000001024 | bytes 31457280 | tf_op jit(solution)/shard_map/backward/pallas_call | solution.py:733
  251.3 10.8 %out_grad.1.refs_6_ = bf16[1536,768]{1,0:T(8,128)(2,1)} custom-call(bf16[2,512,1536]{2,1,0:T(8,128)(2,1)} %get-tuple-element.95.refs_4_.refs_0_, bf16[2,512,1536]{2,1,0:T(8,128)(2,1)} %get-tuple-element.96.refs_12_.refs_1_, bf16[2,512,768]{2,1,0:T(8,128)(2,1)} %get-tuple-element.110.refs_12_.refs_2_, ...), custom_call_target="tpu_custom_call" | custom-call | flops 10000000000 | bytes 31457280 | tf_op jit(solution)/shard_map/out_grad/pallas_call | solution.py:847
  265.9 4.2 collective-permute-done.19
  270.9 12.7 %lowered.2 = (bf16[256,1536]{1,0:T(8,128)(2,1)}, bf16[256,1536]{1,0:T(8,128)(2,1)}, bf16[256,1536]{1,0:T(8,128)(2,1)}, bf16[256,1536]{1,0:T(8,128)(2,1)}) custom-call(s32[1]{0:T(128)} %bitcast.refs_0_, bf16[2,512,768]{2,1,0:T(8,128)(2,1)} %get-tuple-element.120.refs_2_.refs_1_, bf16[2,512,1280]{2,1,0:T(8,128)(2,1)} %maximum_dynamic-update-slice_fusion.refs_2_, ...), custom_call_target="tpu_custom_call" | custom-call | flops 8999999488 | bytes 31457280 | tf_op jit(solution)/shard_map/lowered/pallas_call | solution.py:769
  287.8 25.1 %backward.3 = (bf16[2,512,1280]{2,1,0:T(8,128)(2,1)}, bf16[2,512,128]{2,1,0:T(8,128)(2,1)}, f32[2,8,1024]{2,1,0:T(8,128)}, f32[2,16,1024]{2,1,0:T(8,128)}, f32[40,1024]{1,0:T(8,128)}, /*index=5*/f32[16,128]{1,0:T(8,128)}) custom-call(f32[2,512,768]{2,1,0:T(8,128)} %get-tuple-element.111.refs_1_.refs_0_, f32[2,512,1024]{2,1,0:T(8,128)} %get-tuple-element.104.refs_1_.refs_2_, ...), custom_call_target="tpu_custom_call" | custom-call | flops 22000001024 | bytes 31457280 | tf_op jit(solution)/shard_map/backward/pallas_call | solution.py:733
  312.9 9.3 %collective-permute-done.23.refs_7_ = bf16[256,1536]{1,0:T(8,128)(2,1)S(1)} collective-permute-done((bf16[256,1536]{1,0:T(8,128)(2,1)}, bf16[256,1536]{1,0:T(8,128)(2,1)S(1)}, u32[]{:S(2)}, u32[]{:S(2)}) %collective-permute-start.23) | collective-permute-done | bytes 786464 | tf_op jit(solution)/shard_map/ppermute | solution.py:881
  323.2 4.6 input_norm.2.refs_6_.refs_9_
  329.2 4.5 collective-permute-done.20
  334.5 13.1 %lowered.3 = (bf16[256,1536]{1,0:T(8,128)(2,1)}, bf16[256,1536]{1,0:T(8,128)(2,1)}, bf16[256,1536]{1,0:T(8,128)(2,1)}, bf16[256,1536]{1,0:T(8,128)(2,1)}) custom-call(s32[1]{0:T(128)} %bitcast.refs_0_, bf16[2,512,768]{2,1,0:T(8,128)(2,1)} %get-tuple-element.121.refs_3_.refs_1_, bf16[2,512,1280]{2,1,0:T(8,128)(2,1)} %maximum_dynamic-update-slice_fusion.1.refs_2_.refs_3_, ...), custom_call_target="tpu_custom_call" | custom-call | flops 8999999488 | bytes 31457280 | tf_op jit(solution)/shard_map/lowered/pallas_call | solution.py:769
  347.6 15.7 %late.1 = (bf16[1536,896]{1,0:T(8,128)(2,1)}, f32[1536,256]{1,0:T(8,128)}, f32[1536,128]{1,0:T(8,128)}) custom-call(bf16[2,512,1536]{2,1,0:T(8,128)(2,1)} %get-tuple-element.118.refs_0_, bf16[2,512,1536]{2,1,0:T(8,128)(2,1)} %get-tuple-element.119.refs_1_, bf16[2,512,1280]{2,1,0:T(8,128)(2,1)} %maximum_dynamic-update-slice_fusion.refs_2_, ...), custom_call_target="tpu_custom_call" | custom-call | flops 20000000000 | bytes 31457280 | tf_op jit(solution)/shard_map/late/pallas_call | solution.py:859
  370.4 15.6 %all_gather.40 = f32[8,61,128]{2,1,0:T(8,128)S(1)} all-gather(f32[1,61,128]{2,1,0:T(8,128)S(1)} %bitcast.100), channel_id=1, replica_groups=mesh['tensor'=4,'seq'=4,'dp'=2] {'seq','dp'}, dimensions={0}, use_global_device_ids=true | all-gather | bytes 281088 | tf_op jit(solution)/shard_map/all_gather | solution.py:1007
  388.8 16.6 %collective-permute-done.26.refs_7_ = bf16[256,1536]{1,0:T(8,128)(2,1)S(1)} collective-permute-done((bf16[256,1536]{1,0:T(8,128)(2,1)}, bf16[256,1536]{1,0:T(8,128)(2,1)S(1)}, u32[]{:S(2)}, u32[]{:S(2)}) %collective-permute-start.26) | collective-permute-done | bytes 786464 | tf_op jit(solution)/shard_map/ppermute | solution.py:881
  406.2 4.6 input_norm.3.refs_1_.refs_2_
  414.3 5.9 %placed.2.refs_2_.refs_6_ = bf16[8,256,1536]{2,1,0:T(8,128)(2,1)} custom-call(bf16[8,256,1536]{2,1,0:T(8,128)(2,1)} %bitcast.72, bf16[256,1536]{1,0:T(8,128)(2,1)} %input_norm.3.refs_1_.refs_2_), custom_call_target="tpu_custom_call" | custom-call | tf_op jit(solution)/shard_map/placed/pallas_call | solution.py:890
  424.5 13.0 %reduce-scatter.7.cloned.1.call-done.refs_0_ = f32[192,256]{1,0:T(8,128)} async-done(((f32[1536,256]{1,0:T(8,128)}), f32[192,256]{1,0:T(8,128)}) %reduce-scatter.7.cloned.1.call-update) | async-done | bytes 196624 | tf_op jit(solution)/shard_map/reduce_scatter | solution.py:946
  439.1 15.7 %all-gather.3 = f32[1632,128]{1,0:T(8,128)S(1)} all-gather(f32[408,128]{1,0:T(8,128)} %settled.1), channel_id=5, replica_groups=mesh['tensor'=4,'seq'=4,'dp'=2] {'tensor'}, dimensions={0}, use_global_device_ids=true | all-gather | bytes 1044480 | tf_op jit(solution)/shard_map/all_gather | solution.py:1026
  (266 shorter events, 89.0 us)
Async XLA Ops:
  8.0 193.3 %all-gather.12.cloned.1.call-start = ((), (), s32[]{:S(2)}) async-start(), calls=%async_computation.10 | async-start | bytes 11796480 | tf_op jit(solution)/shard_map/all_gather | solution.py:610
  8.7 313.5 %all-gather.8.cloned.1.call-start = ((), (), s32[]{:S(2)}) async-start(), calls=%async_computation.4 | async-start | bytes 7864320 | tf_op jit(solution)/shard_map/all_gather | solution.py:974
  9.7 15.2 %collective-permute-start = (bf16[4,16,1536]{2,1,0:T(8,128)(2,1)S(1)}, bf16[4,16,1536]{2,1,0:T(8,128)(2,1)S(1)}, u32[]{:S(2)}, u32[]{:S(2)}) collective-permute-start(bf16[4,16,1536]{2,1,0:T(8,128)(2,1)S(1)} %slice.132), channel_id=1, source_target_pairs={{0,2},{2,4},{4,6},{1,3},{3,5},{5,7},{8,10},{10,12},{12,14},{9,11},... | collective-permute-start | bytes 589832 | tf_op jit(solution)/shard_map/ppermute | solution.py:28
  48.1 27.4 %collective-permute-start.1 = (f32[2,128,768]{2,1,0:T(8,128)}, f32[2,128,768]{2,1,0:T(8,128)S(1)}, u32[]{:S(2)}, u32[]{:S(2)}) collective-permute-start(f32[2,128,768]{2,1,0:T(8,128)} %get-tuple-element.94), channel_id=1, source_target_pairs={{0,2},{1,3},{8,10},{9,11},{16,18},{17,19},{24,26},{25,27}} | collective-permute-start | bytes 2359304 | tf_op jit(solution)/shard_map/ppermute | solution.py:669
  74.1 18.5 %collective-permute-start.7 = (f32[2,128,768]{2,1,0:T(8,128)}, f32[2,128,768]{2,1,0:T(8,128)S(1)}, u32[]{:S(2)}, u32[]{:S(2)}) collective-permute-start(f32[2,128,768]{2,1,0:T(8,128)} %get-tuple-element.109), channel_id=1, source_target_pairs={{0,2},{1,3},{8,10},{9,11},{16,18},{17,19},{24,26},{25,27}} | collective-permute-start | bytes 2359304 | tf_op jit(solution)/shard_map/ppermute | solution.py:669
  76.7 18.5 %collective-permute-start.2 = (f32[2,128,768]{2,1,0:T(8,128)}, f32[2,128,768]{2,1,0:T(8,128)}, u32[]{:S(2)}, u32[]{:S(2)}) collective-permute-start(f32[2,128,768]{2,1,0:T(8,128)} %multiply_add_fusion.3), channel_id=1, source_target_pairs={{2,4},{3,5},{10,12},{11,13},{18,20},{19,21},{26,28},{27,29}} | collective-permute-start | bytes 2359304 | tf_op jit(solution)/shard_map/ppermute | solution.py:669
  93.7 16.7 %collective-permute-start.8 = (f32[2,128,768]{2,1,0:T(8,128)}, f32[2,128,768]{2,1,0:T(8,128)}, u32[]{:S(2)}, u32[]{:S(2)}) collective-permute-start(f32[2,128,768]{2,1,0:T(8,128)} %multiply_add_fusion.1), channel_id=1, source_target_pairs={{2,4},{3,5},{10,12},{11,13},{18,20},{19,21},{26,28},{27,29}} | collective-permute-start | bytes 2359304 | tf_op jit(solution)/shard_map/ppermute | solution.py:669
  96.4 15.9 %collective-permute-start.3 = (f32[2,128,768]{2,1,0:T(8,128)S(1)}, f32[2,128,768]{2,1,0:T(8,128)}, u32[]{:S(2)}, u32[]{:S(2)}) collective-permute-start(f32[2,128,768]{2,1,0:T(8,128)S(1)} %multiply_add_fusion.2), channel_id=1, source_target_pairs={{4,6},{5,7},{12,14},{13,15},{20,22},{21,23},{28,30},{29,31}} | collective-permute-start | bytes 2359304 | tf_op jit(solution)/shard_map/ppermute | solution.py:669
  111.6 37.9 %collective-permute-start.9 = (f32[2,128,768]{2,1,0:T(8,128)S(1)}, f32[2,128,768]{2,1,0:T(8,128)S(1)}, u32[]{:S(2)}, u32[]{:S(2)}) collective-permute-start(f32[2,128,768]{2,1,0:T(8,128)S(1)} %multiply_add_fusion), channel_id=1, source_target_pairs={{4,6},{5,7},{12,14},{13,15},{20,22},{21,23},{28,30},{29,31}} | collective-permute-start | bytes 2359304 | tf_op jit(solution)/shard_map/ppermute | solution.py:669
  145.3 23.7 %collective-permute-start.10 = (bf16[2,128,768]{2,1,0:T(8,128)(2,1)S(1)}, bf16[2,128,768]{2,1,0:T(8,128)(2,1)S(1)}, u32[]{:S(2)}, u32[]{:S(2)}) collective-permute-start(bf16[2,128,768]{2,1,0:T(8,128)(2,1)S(1)} %fusion.2), channel_id=1, source_target_pairs={{6,4},{7,5},{14,12},{15,13},{22,20},{23,21},{30,28},{31,29}} | collective-permute-start | bytes 1179656 | tf_op jit(solution)/shard_map/ppermute | solution.py:669
  146.0 37.6 %collective-permute-start.4 = (bf16[256,768]{1,0:T(8,128)(2,1)}, bf16[256,768]{1,0:T(8,128)(2,1)S(1)}, u32[]{:S(2)}, u32[]{:S(2)}) collective-permute-start(bf16[256,768]{1,0:T(8,128)(2,1)} %get-tuple-element.100), channel_id=1, source_target_pairs={{0,8},{8,0},{16,24},{24,16},{1,9},{9,1},{17,25},{25,17},{2,10},{10... | collective-permute-start | bytes 1179656 | tf_op jit(solution)/shard_map/ppermute | solution.py:881
  146.6 37.8 %collective-permute-start.5 = (bf16[256,768]{1,0:T(8,128)(2,1)}, bf16[256,768]{1,0:T(8,128)(2,1)}, u32[]{:S(2)}, u32[]{:S(2)}) collective-permute-start(bf16[256,768]{1,0:T(8,128)(2,1)} %get-tuple-element.101), channel_id=1, source_target_pairs={{0,16},{8,24},{16,0},{24,8},{1,17},{9,25},{17,1},{25,9},{2,18},{10... | collective-permute-start | bytes 1179656 | tf_op jit(solution)/shard_map/ppermute | solution.py:881
  148.1 49.8 %collective-permute-start.6 = (bf16[256,768]{1,0:T(8,128)(2,1)}, bf16[256,768]{1,0:T(8,128)(2,1)}, u32[]{:S(2)}, u32[]{:S(2)}) collective-permute-start(bf16[256,768]{1,0:T(8,128)(2,1)} %get-tuple-element.102), channel_id=1, source_target_pairs={{0,24},{8,16},{16,8},{24,0},{1,25},{9,17},{17,9},{25,1},{2,26},{10... | collective-permute-start | bytes 1179656 | tf_op jit(solution)/shard_map/ppermute | solution.py:881
  169.1 16.6 %collective-permute-start.14 = (bf16[2,128,768]{2,1,0:T(8,128)(2,1)S(1)}, bf16[2,128,768]{2,1,0:T(8,128)(2,1)S(1)}, u32[]{:S(2)}, u32[]{:S(2)}) collective-permute-start(bf16[2,128,768]{2,1,0:T(8,128)(2,1)S(1)} %add_convert_fusion.3), channel_id=1, source_target_pairs={{4,2},{5,3},{12,10},{13,11},{20,18},{21,19},{28,26},{29,27}} | collective-permute-start | bytes 1179656 | tf_op jit(solution)/shard_map/ppermute | solution.py:669
  182.9 15.0 %collective-permute-start.15 = (bf16[2,128,768]{2,1,0:T(8,128)(2,1)S(1)}, bf16[2,128,768]{2,1,0:T(8,128)(2,1)S(1)}, u32[]{:S(2)}, u32[]{:S(2)}) collective-permute-start(bf16[2,128,768]{2,1,0:T(8,128)(2,1)S(1)} %fusion.3), channel_id=1, source_target_pairs={{6,4},{7,5},{14,12},{15,13},{22,20},{23,21},{30,28},{31,29}} | collective-permute-start | bytes 1179656 | tf_op jit(solution)/shard_map/ppermute | solution.py:669
  184.4 16.9 %collective-permute-start.12 = (bf16[256,768]{1,0:T(8,128)(2,1)}, bf16[256,768]{1,0:T(8,128)(2,1)}, u32[]{:S(2)}, u32[]{:S(2)}) collective-permute-start(bf16[256,768]{1,0:T(8,128)(2,1)} %get-tuple-element.116), channel_id=1, source_target_pairs={{0,16},{8,24},{16,0},{24,8},{1,17},{9,25},{17,1},{25,9},{2,18},{10... | collective-permute-start | bytes 1179656 | tf_op jit(solution)/shard_map/ppermute | solution.py:881
  185.7 15.6 %collective-permute-start.13 = (bf16[256,768]{1,0:T(8,128)(2,1)}, bf16[256,768]{1,0:T(8,128)(2,1)S(1)}, u32[]{:S(2)}, u32[]{:S(2)}) collective-permute-start(bf16[256,768]{1,0:T(8,128)(2,1)} %get-tuple-element.117), channel_id=1, source_target_pairs={{0,24},{8,16},{16,8},{24,0},{1,25},{9,17},{17,9},{25,1},{2,26},{10... | collective-permute-start | bytes 1179656 | tf_op jit(solution)/shard_map/ppermute | solution.py:881
  212.2 122.3 %reduce-scatter.5.cloned.1.call-start = ((), (), s32[]{:S(2)}) async-start(), calls=%async_computation.5 | async-start | bytes 2654208 | tf_op jit(solution)/shard_map/reduce_scatter | solution.py:946
  212.8 151.9 %reduce-scatter.11.cloned.1.call-start = ((), (), s32[]{:S(2)}) async-start(), calls=%async_computation.9 | async-start | bytes 2654208 | tf_op jit(solution)/shard_map/reduce_scatter | solution.py:946
  262.2 143.2 %all-gather.10.cloned.1.call-start = ((), (), s32[]{:S(2)}) async-start(), calls=%async_computation.6 | async-start | bytes 3932160 | tf_op jit(solution)/shard_map/all_gather | solution.py:988
  264.6 22.5 %collective-permute-start.17 = (bf16[2,128,768]{2,1,0:T(8,128)(2,1)S(1)}, bf16[2,128,768]{2,1,0:T(8,128)(2,1)S(1)}, u32[]{:S(2)}, u32[]{:S(2)}) collective-permute-start(bf16[2,128,768]{2,1,0:T(8,128)(2,1)S(1)} %add_convert_fusion.1), channel_id=1, source_target_pairs={{2,0},{3,1},{10,8},{11,9},{18,16},{19,17},{26,24},{27,25}} | collective-permute-start | bytes 1179656 | tf_op jit(solution)/shard_map/ppermute | solution.py:669
  283.6 29.3 %collective-permute-start.21 = (bf16[256,1536]{1,0:T(8,128)(2,1)}, bf16[256,1536]{1,0:T(8,128)(2,1)S(1)}, u32[]{:S(2)}, u32[]{:S(2)}) collective-permute-start(bf16[256,1536]{1,0:T(8,128)(2,1)} %get-tuple-element.144), channel_id=1, source_target_pairs={{0,8},{8,0},{16,24},{24,16},{1,9},{9,1},{17,25},{25,17},{2,10},{10... | collective-permute-start | bytes 2359304 | tf_op jit(solution)/shard_map/ppermute | solution.py:881
  285.0 27.9 %collective-permute-start.22 = (bf16[256,1536]{1,0:T(8,128)(2,1)}, bf16[256,1536]{1,0:T(8,128)(2,1)S(1)}, u32[]{:S(2)}, u32[]{:S(2)}) collective-permute-start(bf16[256,1536]{1,0:T(8,128)(2,1)} %get-tuple-element.145), channel_id=1, source_target_pairs={{0,16},{8,24},{16,0},{24,8},{1,17},{9,25},{17,1},{25,9},{2,18},{10... | collective-permute-start | bytes 2359304 | tf_op jit(solution)/shard_map/ppermute | solution.py:881
  285.8 36.5 %collective-permute-start.23 = (bf16[256,1536]{1,0:T(8,128)(2,1)}, bf16[256,1536]{1,0:T(8,128)(2,1)S(1)}, u32[]{:S(2)}, u32[]{:S(2)}) collective-permute-start(bf16[256,1536]{1,0:T(8,128)(2,1)} %get-tuple-element.146), channel_id=1, source_target_pairs={{0,24},{8,16},{16,8},{24,0},{1,25},{9,17},{17,9},{25,1},{2,26},{10... | collective-permute-start | bytes 2359304 | tf_op jit(solution)/shard_map/ppermute | solution.py:881
  327.8 95.6 %reduce-scatter.9.cloned.1.call-start = ((), (), s32[]{:S(2)}) async-start(), calls=%async_computation.8 | async-start | bytes 3096576 | tf_op jit(solution)/shard_map/reduce_scatter | solution.py:946
  363.4 74.1 %reduce-scatter.7.cloned.1.call-start = ((), (), s32[]{:S(2)}) async-start(), calls=%async_computation.7 | async-start | bytes 1769472 | tf_op jit(solution)/shard_map/reduce_scatter | solution.py:946
  366.8 21.9 %collective-permute-start.24 = (bf16[256,1536]{1,0:T(8,128)(2,1)}, bf16[256,1536]{1,0:T(8,128)(2,1)S(1)}, u32[]{:S(2)}, u32[]{:S(2)}) collective-permute-start(bf16[256,1536]{1,0:T(8,128)(2,1)} %get-tuple-element.148), channel_id=1, source_target_pairs={{0,8},{8,0},{16,24},{24,16},{1,9},{9,1},{17,25},{25,17},{2,10},{10... | collective-permute-start | bytes 2359304 | tf_op jit(solution)/shard_map/ppermute | solution.py:881
  367.7 21.0 %collective-permute-start.25 = (bf16[256,1536]{1,0:T(8,128)(2,1)}, bf16[256,1536]{1,0:T(8,128)(2,1)S(1)}, u32[]{:S(2)}, u32[]{:S(2)}) collective-permute-start(bf16[256,1536]{1,0:T(8,128)(2,1)} %get-tuple-element.149), channel_id=1, source_target_pairs={{0,16},{8,24},{16,0},{24,8},{1,17},{9,25},{17,1},{25,9},{2,18},{10... | collective-permute-start | bytes 2359304 | tf_op jit(solution)/shard_map/ppermute | solution.py:881
  368.7 36.6 %collective-permute-start.26 = (bf16[256,1536]{1,0:T(8,128)(2,1)}, bf16[256,1536]{1,0:T(8,128)(2,1)S(1)}, u32[]{:S(2)}, u32[]{:S(2)}) collective-permute-start(bf16[256,1536]{1,0:T(8,128)(2,1)} %get-tuple-element.150), channel_id=1, source_target_pairs={{0,24},{8,16},{16,8},{24,0},{1,25},{9,17},{17,9},{25,1},{2,26},{10... | collective-permute-start | bytes 2359304 | tf_op jit(solution)/shard_map/ppermute | solution.py:881
  410.8 49.5 %collective-permute-start.27 = (bf16[256,1536]{1,0:T(8,128)(2,1)}, bf16[256,1536]{1,0:T(8,128)(2,1)S(1)}, u32[]{:S(2)}, u32[]{:S(2)}) collective-permute-start(bf16[256,1536]{1,0:T(8,128)(2,1)} %input_norm.3.refs_1_.refs_2_), channel_id=1, source_target_pairs={{0,8},{8,0},{16,24},{24,16},{1,9},{9,1},{17,25},{25,17},{2,10},{10... | collective-permute-start | bytes 2359304 | tf_op jit(solution)/shard_map/ppermute | solution.py:876
  411.4 49.0 %collective-permute-start.28 = (bf16[256,1536]{1,0:T(8,128)(2,1)}, bf16[256,1536]{1,0:T(8,128)(2,1)}, u32[]{:S(2)}, u32[]{:S(2)}) collective-permute-start(bf16[256,1536]{1,0:T(8,128)(2,1)} %input_norm.3.refs_1_.refs_2_), channel_id=1, source_target_pairs={{0,16},{8,24},{16,0},{24,8},{1,17},{9,25},{17,1},{25,9},{2,18},{10... | collective-permute-start | bytes 2359304 | tf_op jit(solution)/shard_map/ppermute | solution.py:876
  412.2 48.2 %collective-permute-start.29 = (bf16[256,1536]{1,0:T(8,128)(2,1)}, bf16[256,1536]{1,0:T(8,128)(2,1)}, u32[]{:S(2)}, u32[]{:S(2)}) collective-permute-start(bf16[256,1536]{1,0:T(8,128)(2,1)} %input_norm.3.refs_1_.refs_2_), channel_id=1, source_target_pairs={{0,24},{8,16},{16,8},{24,0},{1,25},{9,17},{17,9},{25,1},{2,26},{10... | collective-permute-start | bytes 2359304 | tf_op jit(solution)/shard_map/ppermute | solution.py:876
  (58 other events, 377.4 us)
Sparse Core Ops, SparseCore 0:
  10.7 99.0 all-gather.11
  212.3 79.9 all-gather.7
  327.9 45.7 all-gather.9
Sparse Core Ops, SparseCore 1:
  215.0 41.8 reduce-scatter.4
  262.3 36.9 reduce-scatter.10
  363.4 38.1 reduce-scatter.8
  404.0 33.5 reduce-scatter.6
